TPU v7x, 256 devices: a whole 4x4x8 slice. The times are simulated.
256 devices in a mesh: sub: 16 (over x, y), dev: 16 (over z, core).
Axes of the slice: x: 4, y: 4, z: 8, core: 2. Of those that a mesh axis runs over, the one named last changes fastest.
Arguments:
- pressure: float32 [1024, 512, 256], P('sub', 'dev'), may hold values from -6 to 6
- storage: float32 [1024, 512, 256], P('sub', 'dev'), may hold values from 0.5 to 4
- source: float32 [1024, 512, 256], P('sub', 'dev'), may hold values from -6 to 6
- left_data: float32 [16, 4, 512, 256], P('sub', None, 'dev'), may hold values from -6 to 6
- right_data: float32 [16, 4, 512, 256], P('sub', None, 'dev'), may hold values from -6 to 6
- widths: int32 [16], P('sub'), may hold values from 32 to 64, as said below
Outputs:
- pressure_end: float32 [1024, 512, 256], P('sub', 'dev')
- new_left: float32 [16, 4, 512, 256], P('sub', None, 'dev')
- new_right: float32 [16, 4, 512, 256], P('sub', None, 'dev')
Inputs may be any that keep to these rules, and one draw needn't show every extreme that they name: `widths`: each subdomain has 32 to 64 live planes; in every draw some subdomain has exactly 64 and another exactly 32.
All inputs are finite; a program needn't handle non-finite values.
Results may differ from a plain program's by a relative error of at most 0.0003.
Values sent between devices are 32-bit elements; how exact they have to be, the bound alone decides.
No kernel may reach another device: no remote copies, remote signals or barrier semaphores. Data moves between devices by JAX's collectives and lax.ppermute only.
A program may use at most 128 MiB of HBM per device.

v0:
```python
import jax
import jax.numpy as jnp
from jax import lax
from jax.sharding import PartitionSpec as P

BETA = 1.5
RHO_ZERO = 0.9
RHO_ONE = 1.0 / (2.0 / 0.9 - 0.9)
COEF_ONE = RHO_ONE * RHO_ZERO
COEF_TWO = 2.0 * RHO_ONE / 0.9


def padded_2(block, sides, width):
    for axis, dim in sides:
        count = lax.axis_size(axis)
        forward = [(i, i + 1) for i in range(count - 1)]
        backward = [(target, source) for source, target in forward]
        low = lax.ppermute(
            lax.slice_in_dim(block, block.shape[dim] - width, None, axis=dim), axis, forward
        )
        high = lax.ppermute(lax.slice_in_dim(block, 0, width, axis=dim), axis, backward)
        block = jnp.concatenate([low, block, high], axis=dim)
    return block


def shifted(block, axis, distance):
    devices = range(lax.axis_size(axis))
    route = [(i - distance, i) for i in devices if i - distance in devices]
    return lax.ppermute(block, axis, route)


def neighbours(padded):
    along_x = padded[2:, 1:-1, 1:-1] + padded[:-2, 1:-1, 1:-1]
    along_y = padded[1:-1, 2:, 1:-1] + padded[1:-1, :-2, 1:-1]
    along_z = padded[1:-1, 1:-1, 2:] + padded[1:-1, 1:-1, :-2]
    return along_x + along_y + along_z


def operate(rimmed, diag, live):
    center = rimmed[:, 1:-1]
    padded = jnp.pad(rimmed, ((1, 1), (0, 0), (1, 1)))
    return (diag * center - neighbours(padded)) * live


def single_rim(field):
    return padded_2(field, (("dev", 1),), 1)


def on_device(pressure, storage, source, left_data, right_data, widths):
    width = widths[0]
    plane_count, rows, depth = pressure.shape
    planes = jnp.arange(plane_count, dtype=jnp.int32)[:, None, None]
    live = (planes < width).astype(jnp.float32)
    first = (planes == 0).astype(jnp.float32)
    last = (planes == width - 1).astype(jnp.float32)
    extra = jnp.where(planes == 0, BETA, 1.0) + jnp.where(planes == width - 1, BETA, 1.0)
    left_in = left_data[0]
    right_in = right_data[0]
    steps = left_in.shape[0]
    field = pressure * live
    diag_own = storage + 4.0 + extra
    lefts = []
    rights = []
    for step in range(steps):
        rhs = (storage * field + source + first * left_in[step] + last * right_in[step]) * live
        resid_zero = rhs - operate(single_rim(field), diag_own, live)
        dir_zero = resid_zero / diag_own
        first_iter = field + dir_zero
        resid_one = rhs - operate(single_rim(first_iter), diag_own, live)
        dir_one = COEF_ONE * dir_zero + COEF_TWO * resid_one / diag_own
        field = first_iter + dir_one
        plane_a = field[0]
        plane_b = field[1]
        plane_c = lax.dynamic_slice_in_dim(field, width - 1, 1, 0)[0]
        plane_d = lax.dynamic_slice_in_dim(field, width - 2, 1, 0)[0]
        trace_low = BETA * plane_a + (plane_a - plane_b)
        trace_high = BETA * plane_c + (plane_c - plane_d)
        lefts.append(trace_high)
        rights.append(trace_low)
    new_left = shifted(jnp.stack(lefts), "sub", 1)
    new_right = shifted(jnp.stack(rights), "sub", -1)
    return (field, new_left[None], new_right[None])


def solution(mesh):
    in_specs = (
        P("sub", "dev", None),
        P("sub", "dev", None),
        P("sub", "dev", None),
        P("sub", None, "dev", None),
        P("sub", None, "dev", None),
        P("sub"),
    )
    out_specs = (P("sub", "dev", None), P("sub", None, "dev", None), P("sub", None, "dev", None))
    return jax.shard_map(
        on_device, mesh=mesh, in_specs=in_specs, out_specs=out_specs, check_vma=False
    )
```

profile of v0, /device:TPU:101, one launch (start us, length us, event | category | flops | bytes accessed | tf_op | source)
XLA Modules:
  0.0 157.3 jit_solution(15027706919854909189)
XLA Ops:
  3.3 5.3 %collective-permute-start = (f32[64,1,256]{2,1,0:T(1,128)S(1)}, f32[64,1,256]{2,1,0:T(1,128)S(1)}, u32[]{:S(2)}, u32[]{:S(2)}) collective-permute-start(f32[64,1,256]{2,1,0:T(1,128)S(1)} %get-tuple-element.33), channel_id=1, source_target_pairs={{0,1},{1,2},{2,3},{3,4},{4,5},{5,6},{6,7},{7,8},{8,9},{9,10},{10,1... | collective-permute-start | bytes 196616 | tf_op jit(solution)/shard_map/ppermute | solution.py:18
  10.6 4.7 %collective-permute-done.1 = f32[64,1,256]{2,1,0:T(1,128)S(1)} collective-permute-done((f32[64,1,256]{2,1,0:T(1,128)S(1)}, f32[64,1,256]{2,1,0:T(1,128)S(1)}, u32[]{:S(2)}, u32[]{:S(2)}) %collective-permute-start.1) | collective-permute-done | bytes 65568 | tf_op jit(solution)/shard_map/ppermute | solution.py:21
  15.4 4.1 %select_maximum_fusion.14 = f32[66,34,258]{2,1,0:T(8,128)S(1)} fusion(f32[64,1,256]{2,1,0:T(1,128)S(1)} %collective-permute-done.1, f32[64,32,256]{2,1,0:T(8,128)} %copy-done.6, f32[64,1,256]{2,1,0:T(1,128)S(1)} %collective-permute-done), kind=kLoop, calls=%fused_computation.18 | loop fusion | flops 8684280 | bytes 4544032 | tf_op jit(solution)/shard_map/concatenate | solution.py:22
  19.5 7.5 %fusion.82 = (f32[64,32,256]{2,1,0:T(8,128)S(1)}, f32[64,32,256]{2,1,0:T(8,128)S(1)}) fusion(f32[64,32,256]{2,1,0:T(8,128)} %copy-done.6, f32[66,34,258]{2,1,0:T(8,128)S(1)} %select_maximum_fusion.14, f32[64,1,256]{2,1,0:T(1,128)S(1)} %collective-permute-done, f32[64,1,256]{2,1,0:T(1,128)S(1)} %collective-permute-done.1, f32[64]{0:T(128)S(1)} %fusion.75, ...), kind=kLoop, calls=%fused_computation.160 | loop fusion | flops 11534336 | bytes 19072000 | tf_op jit(solution)/shard_map/add | solution.py:68
  29.0 2.5 %collective-permute-start.3 = (f32[64,1,256]{2,1,0:T(1,128)S(1)}, f32[64,1,256]{2,1,0:T(1,128)S(1)}, u32[]{:S(2)}, u32[]{:S(2)}) collective-permute-start(f32[64,1,256]{2,1,0:T(1,128)S(1)} %get-tuple-element.32), channel_id=1, source_target_pairs={{1,0},{2,1},{3,2},{4,3},{5,4},{6,5},{7,6},{8,7},{9,8},{10,9},{11,1... | collective-permute-start | bytes 196616 | tf_op jit(solution)/shard_map/ppermute | solution.py:21
  31.6 4.4 %collective-permute-done.3 = f32[64,1,256]{2,1,0:T(1,128)S(1)} collective-permute-done((f32[64,1,256]{2,1,0:T(1,128)S(1)}, f32[64,1,256]{2,1,0:T(1,128)S(1)}, u32[]{:S(2)}, u32[]{:S(2)}) %collective-permute-start.3) | collective-permute-done | bytes 65568 | tf_op jit(solution)/shard_map/ppermute | solution.py:21
  36.0 3.1 %select_maximum_fusion.12 = f32[66,34,258]{2,1,0:T(8,128)S(1)} fusion(f32[64,1,256]{2,1,0:T(1,128)S(1)} %collective-permute-done.3, f32[64,32,256]{2,1,0:T(8,128)S(1)} %get-tuple-element.9, f32[64,1,256]{2,1,0:T(1,128)S(1)} %collective-permute-done.2), kind=kLoop, calls=%fused_computation.16 | loop fusion | flops 8684280 | bytes 4544032 | tf_op jit(solution)/shard_map/concatenate | solution.py:22
  39.1 5.1 %fusion.61 = f32[64,32,256]{2,1,0:T(8,128)S(1)} fusion(f32[64,32,256]{2,1,0:T(8,128)S(1)} %get-tuple-element.9, f32[66,34,258]{2,1,0:T(8,128)S(1)} %select_maximum_fusion.12, f32[64,1,256]{2,1,0:T(1,128)S(1)} %collective-permute-done.2, f32[64,1,256]{2,1,0:T(1,128)S(1)} %collective-permute-done.3, f32[64,32,256]{2,1,0:T(8,128)S(1)} %get-tuple-element.10, ...), kind=kLoop, calls=%fused_computation.106 | loop fusion | flops 13631488 | bytes 21169152 | tf_op jit(solution)/shard_map/add | solution.py:71
  46.2 2.4 %collective-permute-start.5 = (f32[64,1,256]{2,1,0:T(1,128)S(1)}, f32[64,1,256]{2,1,0:T(1,128)S(1)}, u32[]{:S(2)}, u32[]{:S(2)}) collective-permute-start(f32[64,1,256]{2,1,0:T(1,128)S(1)} %get-tuple-element.30), channel_id=1, source_target_pairs={{1,0},{2,1},{3,2},{4,3},{5,4},{6,5},{7,6},{8,7},{9,8},{10,9},{11,1... | collective-permute-start | bytes 196616 | tf_op jit(solution)/shard_map/ppermute | solution.py:21
  48.7 4.4 %collective-permute-done.5 = f32[64,1,256]{2,1,0:T(1,128)S(1)} collective-permute-done((f32[64,1,256]{2,1,0:T(1,128)S(1)}, f32[64,1,256]{2,1,0:T(1,128)S(1)}, u32[]{:S(2)}, u32[]{:S(2)}) %collective-permute-start.5) | collective-permute-done | bytes 65568 | tf_op jit(solution)/shard_map/ppermute | solution.py:21
  53.0 3.1 %select_maximum_fusion.10 = f32[66,34,258]{2,1,0:T(8,128)S(1)} fusion(f32[64,1,256]{2,1,0:T(1,128)S(1)} %collective-permute-done.5, f32[64,32,256]{2,1,0:T(8,128)S(1)} %fusion.61, f32[64,1,256]{2,1,0:T(1,128)S(1)} %collective-permute-done.4), kind=kLoop, calls=%fused_computation.14 | loop fusion | flops 8684280 | bytes 4544032 | tf_op jit(solution)/shard_map/concatenate | solution.py:22
  56.1 4.5 %fusion.80 = (f32[64,32,256]{2,1,0:T(8,128)S(1)}, f32[64,32,256]{2,1,0:T(8,128)S(1)}) fusion(f32[64,32,256]{2,1,0:T(8,128)S(1)} %fusion.61, f32[66,34,258]{2,1,0:T(8,128)S(1)} %select_maximum_fusion.10, f32[64,1,256]{2,1,0:T(1,128)S(1)} %collective-permute-done.4, f32[64,1,256]{2,1,0:T(1,128)S(1)} %collective-permute-done.5, f32[64]{0:T(128)S(1)} %fusion.75, ...), kind=kLoop, calls=%fused_computation.159 | loop fusion | flops 11534336 | bytes 19072000 | tf_op jit(solution)/shard_map/add | solution.py:68
  62.7 2.6 %collective-permute-start.7 = (f32[64,1,256]{2,1,0:T(1,128)S(1)}, f32[64,1,256]{2,1,0:T(1,128)S(1)}, u32[]{:S(2)}, u32[]{:S(2)}) collective-permute-start(f32[64,1,256]{2,1,0:T(1,128)S(1)} %get-tuple-element.28), channel_id=1, source_target_pairs={{1,0},{2,1},{3,2},{4,3},{5,4},{6,5},{7,6},{8,7},{9,8},{10,9},{11,1... | collective-permute-start | bytes 196616 | tf_op jit(solution)/shard_map/ppermute | solution.py:21
  65.3 4.2 %collective-permute-done.7 = f32[64,1,256]{2,1,0:T(1,128)S(1)} collective-permute-done((f32[64,1,256]{2,1,0:T(1,128)S(1)}, f32[64,1,256]{2,1,0:T(1,128)S(1)}, u32[]{:S(2)}, u32[]{:S(2)}) %collective-permute-start.7) | collective-permute-done | bytes 65568 | tf_op jit(solution)/shard_map/ppermute | solution.py:21
  69.5 3.1 %select_maximum_fusion.8 = f32[66,34,258]{2,1,0:T(8,128)S(1)} fusion(f32[64,1,256]{2,1,0:T(1,128)S(1)} %collective-permute-done.7, f32[64,32,256]{2,1,0:T(8,128)S(1)} %get-tuple-element.7, f32[64,1,256]{2,1,0:T(1,128)S(1)} %collective-permute-done.6), kind=kLoop, calls=%fused_computation.12 | loop fusion | flops 8684280 | bytes 4544032 | tf_op jit(solution)/shard_map/concatenate | solution.py:22
  72.6 4.9 %fusion.44 = f32[64,32,256]{2,1,0:T(8,128)S(1)} fusion(f32[64,32,256]{2,1,0:T(8,128)S(1)} %get-tuple-element.7, f32[66,34,258]{2,1,0:T(8,128)S(1)} %select_maximum_fusion.8, f32[64,1,256]{2,1,0:T(1,128)S(1)} %collective-permute-done.6, f32[64,1,256]{2,1,0:T(1,128)S(1)} %collective-permute-done.7, f32[64,32,256]{2,1,0:T(8,128)S(1)} %get-tuple-element.8, ...), kind=kLoop, calls=%fused_computation.81 | loop fusion | flops 13107200 | bytes 21169152 | tf_op jit(solution)/shard_map/add | solution.py:71
  83.4 4.3 %collective-permute-done.9 = f32[64,1,256]{2,1,0:T(1,128)S(1)} collective-permute-done((f32[64,1,256]{2,1,0:T(1,128)S(1)}, f32[64,1,256]{2,1,0:T(1,128)S(1)}, u32[]{:S(2)}, u32[]{:S(2)}) %collective-permute-start.9) | collective-permute-done | bytes 65568 | tf_op jit(solution)/shard_map/ppermute | solution.py:21
  87.7 4.1 %select_maximum_fusion.6 = f32[66,34,258]{2,1,0:T(8,128)S(1)} fusion(f32[64,1,256]{2,1,0:T(1,128)S(1)} %collective-permute-done.9, f32[64,32,256]{2,1,0:T(8,128)} %copy-done.4, f32[64,1,256]{2,1,0:T(1,128)S(1)} %collective-permute-done.8), kind=kLoop, calls=%fused_computation.10 | loop fusion | flops 8684280 | bytes 4544032 | tf_op jit(solution)/shard_map/concatenate | solution.py:22
  91.8 4.5 %fusion.78 = (f32[64,32,256]{2,1,0:T(8,128)S(1)}, f32[64,32,256]{2,1,0:T(8,128)S(1)}) fusion(f32[64,32,256]{2,1,0:T(8,128)S(1)} %copy-done.5, f32[66,34,258]{2,1,0:T(8,128)S(1)} %select_maximum_fusion.6, f32[64,1,256]{2,1,0:T(1,128)S(1)} %collective-permute-done.8, f32[64,1,256]{2,1,0:T(1,128)S(1)} %collective-permute-done.9, f32[64]{0:T(128)S(1)} %fusion.75, ...), kind=kLoop, calls=%fused_computation.158 | loop fusion | flops 11534336 | bytes 19072000 | tf_op jit(solution)/shard_map/add | solution.py:68
  98.4 2.4 %collective-permute-start.11 = (f32[64,1,256]{2,1,0:T(1,128)S(1)}, f32[64,1,256]{2,1,0:T(1,128)S(1)}, u32[]{:S(2)}, u32[]{:S(2)}) collective-permute-start(f32[64,1,256]{2,1,0:T(1,128)S(1)} %get-tuple-element.24), channel_id=1, source_target_pairs={{1,0},{2,1},{3,2},{4,3},{5,4},{6,5},{7,6},{8,7},{9,8},{10,9},{11,1... | collective-permute-start | bytes 196616 | tf_op jit(solution)/shard_map/ppermute | solution.py:21
  101.6 3.5 %collective-permute-done.11 = f32[64,1,256]{2,1,0:T(1,128)S(1)} collective-permute-done((f32[64,1,256]{2,1,0:T(1,128)S(1)}, f32[64,1,256]{2,1,0:T(1,128)S(1)}, u32[]{:S(2)}, u32[]{:S(2)}) %collective-permute-start.11) | collective-permute-done | bytes 65568 | tf_op jit(solution)/shard_map/ppermute | solution.py:21
  105.2 3.1 %select_maximum_fusion.4 = f32[66,34,258]{2,1,0:T(8,128)S(1)} fusion(f32[64,1,256]{2,1,0:T(1,128)S(1)} %collective-permute-done.11, f32[64,32,256]{2,1,0:T(8,128)S(1)} %get-tuple-element.5, f32[64,1,256]{2,1,0:T(1,128)S(1)} %collective-permute-done.10), kind=kLoop, calls=%fused_computation.8 | loop fusion | flops 8684280 | bytes 4544032 | tf_op jit(solution)/shard_map/concatenate | solution.py:22
  108.3 4.9 %fusion.27 = f32[64,32,256]{2,1,0:T(8,128)S(1)} fusion(f32[64,32,256]{2,1,0:T(8,128)S(1)} %get-tuple-element.5, f32[66,34,258]{2,1,0:T(8,128)S(1)} %select_maximum_fusion.4, f32[64,1,256]{2,1,0:T(1,128)S(1)} %collective-permute-done.10, f32[64,1,256]{2,1,0:T(1,128)S(1)} %collective-permute-done.11, f32[64,32,256]{2,1,0:T(8,128)S(1)} %get-tuple-element.6, ...), kind=kLoop, calls=%fused_computation.56 | loop fusion | flops 13107200 | bytes 21169152 | tf_op jit(solution)/shard_map/add | solution.py:71
  115.2 2.6 %collective-permute-start.13 = (f32[64,1,256]{2,1,0:T(1,128)S(1)}, f32[64,1,256]{2,1,0:T(1,128)S(1)}, u32[]{:S(2)}, u32[]{:S(2)}) collective-permute-start(f32[64,1,256]{2,1,0:T(1,128)S(1)} %get-tuple-element.22), channel_id=1, source_target_pairs={{1,0},{2,1},{3,2},{4,3},{5,4},{6,5},{7,6},{8,7},{9,8},{10,9},{11,1... | collective-permute-start | bytes 196616 | tf_op jit(solution)/shard_map/ppermute | solution.py:21
  117.9 4.1 %collective-permute-done.13 = f32[64,1,256]{2,1,0:T(1,128)S(1)} collective-permute-done((f32[64,1,256]{2,1,0:T(1,128)S(1)}, f32[64,1,256]{2,1,0:T(1,128)S(1)}, u32[]{:S(2)}, u32[]{:S(2)}) %collective-permute-start.13) | collective-permute-done | bytes 65568 | tf_op jit(solution)/shard_map/ppermute | solution.py:21
  122.0 3.1 %select_maximum_fusion.2 = f32[66,34,258]{2,1,0:T(8,128)S(1)} fusion(f32[64,1,256]{2,1,0:T(1,128)S(1)} %collective-permute-done.13, f32[64,32,256]{2,1,0:T(8,128)S(1)} %fusion.27, f32[64,1,256]{2,1,0:T(1,128)S(1)} %collective-permute-done.12), kind=kLoop, calls=%fused_computation.6 | loop fusion | flops 8684280 | bytes 4544032 | tf_op jit(solution)/shard_map/concatenate | solution.py:22
  125.1 4.5 %fusion.76 = (f32[64,32,256]{2,1,0:T(8,128)S(1)}, f32[64,32,256]{2,1,0:T(8,128)S(1)}) fusion(f32[64,32,256]{2,1,0:T(8,128)S(1)} %fusion.27, f32[66,34,258]{2,1,0:T(8,128)S(1)} %select_maximum_fusion.2, f32[64,1,256]{2,1,0:T(1,128)S(1)} %collective-permute-done.12, f32[64,1,256]{2,1,0:T(1,128)S(1)} %collective-permute-done.13, f32[64]{0:T(128)S(1)} %fusion.75, ...), kind=kLoop, calls=%fused_computation.157 | loop fusion | flops 11534336 | bytes 19072000 | tf_op jit(solution)/shard_map/add | solution.py:68
  134.1 4.3 %collective-permute-done.15 = f32[64,1,256]{2,1,0:T(1,128)S(1)} collective-permute-done((f32[64,1,256]{2,1,0:T(1,128)S(1)}, f32[64,1,256]{2,1,0:T(1,128)S(1)}, u32[]{:S(2)}, u32[]{:S(2)}) %collective-permute-start.15) | collective-permute-done | bytes 65568 | tf_op jit(solution)/shard_map/ppermute | solution.py:21
  138.5 3.1 %select_maximum_fusion = f32[66,34,258]{2,1,0:T(8,128)S(1)} fusion(f32[64,1,256]{2,1,0:T(1,128)S(1)} %collective-permute-done.15, f32[64,32,256]{2,1,0:T(8,128)S(1)} %get-tuple-element.3, f32[64,1,256]{2,1,0:T(1,128)S(1)} %collective-permute-done.14), kind=kLoop, calls=%fused_computation.4 | loop fusion | flops 8684280 | bytes 4544032 | tf_op jit(solution)/shard_map/concatenate | solution.py:22
  141.6 4.9 %fusion.10 = f32[64,32,256]{2,1,0:T(8,128)S(1)} fusion(f32[64,32,256]{2,1,0:T(8,128)S(1)} %get-tuple-element.3, f32[66,34,258]{2,1,0:T(8,128)S(1)} %select_maximum_fusion, f32[64,1,256]{2,1,0:T(1,128)S(1)} %collective-permute-done.14, f32[64,1,256]{2,1,0:T(1,128)S(1)} %collective-permute-done.15, f32[64,32,256]{2,1,0:T(8,128)S(1)} %get-tuple-element.4, ...), kind=kLoop, calls=%fused_computation.31 | loop fusion | flops 13107200 | bytes 21169152 | tf_op jit(solution)/shard_map/add | solution.py:71
  146.6 3.2 %collective-permute-start.16 = (f32[4,32,256]{2,1,0:T(8,128)S(1)}, f32[4,32,256]{2,1,0:T(8,128)S(1)}, u32[]{:S(2)}, u32[]{:S(2)}) collective-permute-start(f32[4,32,256]{2,1,0:T(8,128)S(1)} %pad_maximum_fusion.16), channel_id=1, source_target_pairs={{0,16},{16,32},{32,48},{48,64},{64,80},{80,96},{96,112},{112,128},... | collective-permute-start | bytes 393224 | tf_op jit(solution)/shard_map/ppermute | solution.py:29
  149.8 4.2 %collective-permute-start.17 = (f32[4,32,256]{2,1,0:T(8,128)S(1)}, f32[4,32,256]{2,1,0:T(8,128)S(1)}, u32[]{:S(2)}, u32[]{:S(2)}) collective-permute-start(f32[4,32,256]{2,1,0:T(8,128)S(1)} %pad_maximum_fusion.17), channel_id=1, source_target_pairs={{16,0},{32,16},{48,32},{64,48},{80,64},{96,80},{112,96},{128,112},... | collective-permute-start | bytes 393224 | tf_op jit(solution)/shard_map/ppermute | solution.py:29
  (63 shorter events, 28.3 us)
Async XLA Ops:
  1.3 9.2 %copy-start.9 = (f32[1,4,32,256]{3,2,1,0:T(8,128)S(1)}, f32[1,4,32,256]{3,2,1,0:T(8,128)}, u32[]{:S(2)}) copy-start(f32[1,4,32,256]{3,2,1,0:T(8,128)} %param.10) | copy-start | bytes 393220
  1.3 9.2 %copy-start.10 = (f32[1,4,32,256]{3,2,1,0:T(8,128)S(1)}, f32[1,4,32,256]{3,2,1,0:T(8,128)}, u32[]{:S(2)}) copy-start(f32[1,4,32,256]{3,2,1,0:T(8,128)} %param.9) | copy-start | bytes 393220
  3.2 7.4 %copy-start.6 = (f32[64,32,256]{2,1,0:T(8,128)}, f32[64,32,256]{2,1,0:T(8,128)S(1)}, u32[]{:S(2)}) copy-start(f32[64,32,256]{2,1,0:T(8,128)S(1)} %broadcast_multiply_fusion) | copy-start | bytes 6291460
  3.3 7.4 %collective-permute-start = (f32[64,1,256]{2,1,0:T(1,128)S(1)}, f32[64,1,256]{2,1,0:T(1,128)S(1)}, u32[]{:S(2)}, u32[]{:S(2)}) collective-permute-start(f32[64,1,256]{2,1,0:T(1,128)S(1)} %get-tuple-element.33), channel_id=1, source_target_pairs={{0,1},{1,2},{2,3},{3,4},{4,5},{5,6},{6,7},{7,8},{8,9},{9,10},{10,1... | collective-permute-start | bytes 196616 | tf_op jit(solution)/shard_map/ppermute | solution.py:18
  8.6 6.8 %collective-permute-start.1 = (f32[64,1,256]{2,1,0:T(1,128)S(1)}, f32[64,1,256]{2,1,0:T(1,128)S(1)}, u32[]{:S(2)}, u32[]{:S(2)}) collective-permute-start(f32[64,1,256]{2,1,0:T(1,128)S(1)} %get-tuple-element.34), channel_id=1, source_target_pairs={{1,0},{2,1},{3,2},{4,3},{5,4},{6,5},{7,6},{8,7},{9,8},{10,9},{11,1... | collective-permute-start | bytes 196616 | tf_op jit(solution)/shard_map/ppermute | solution.py:21
  10.6 8.9 %copy-start = (f32[64,32,256]{2,1,0:T(8,128)S(1)}, f32[64,32,256]{2,1,0:T(8,128)}, u32[]{:S(2)}) copy-start(f32[64,32,256]{2,1,0:T(8,128)} %param.7) | copy-start | bytes 6291460
  10.6 8.9 %copy-start.1 = (f32[64,32,256]{2,1,0:T(8,128)S(1)}, f32[64,32,256]{2,1,0:T(8,128)}, u32[]{:S(2)}) copy-start(f32[64,32,256]{2,1,0:T(8,128)} %param.8) | copy-start | bytes 6291460
  27.1 4.5 %collective-permute-start.2 = (f32[64,1,256]{2,1,0:T(1,128)S(1)}, f32[64,1,256]{2,1,0:T(1,128)S(1)}, u32[]{:S(2)}, u32[]{:S(2)}) collective-permute-start(f32[64,1,256]{2,1,0:T(1,128)S(1)} %get-tuple-element.31), channel_id=1, source_target_pairs={{0,1},{1,2},{2,3},{3,4},{4,5},{5,6},{6,7},{7,8},{8,9},{9,10},{10,1... | collective-permute-start | bytes 196616 | tf_op jit(solution)/shard_map/ppermute | solution.py:18
  29.0 10.1 %copy-start.7 = (f32[64,32,256]{2,1,0:T(8,128)S(1)}, f32[64,32,256]{2,1,0:T(8,128)}, u32[]{:S(2)}) copy-start(f32[64,32,256]{2,1,0:T(8,128)} %param.6) | copy-start | bytes 6291460
  29.0 6.9 %collective-permute-start.3 = (f32[64,1,256]{2,1,0:T(1,128)S(1)}, f32[64,1,256]{2,1,0:T(1,128)S(1)}, u32[]{:S(2)}, u32[]{:S(2)}) collective-permute-start(f32[64,1,256]{2,1,0:T(1,128)S(1)} %get-tuple-element.32), channel_id=1, source_target_pairs={{1,0},{2,1},{3,2},{4,3},{5,4},{6,5},{7,6},{8,7},{9,8},{10,9},{11,1... | collective-permute-start | bytes 196616 | tf_op jit(solution)/shard_map/ppermute | solution.py:21
  44.2 28.4 %copy-start.3 = (f32[64,32,256]{2,1,0:T(8,128)}, f32[64,32,256]{2,1,0:T(8,128)S(1)}, u32[]{:S(2)}) copy-start(f32[64,32,256]{2,1,0:T(8,128)S(1)} %fusion.61) | copy-start | bytes 6291460
  44.3 4.3 %collective-permute-start.4 = (f32[64,1,256]{2,1,0:T(1,128)S(1)}, f32[64,1,256]{2,1,0:T(1,128)S(1)}, u32[]{:S(2)}, u32[]{:S(2)}) collective-permute-start(f32[64,1,256]{2,1,0:T(1,128)S(1)} %get-tuple-element.29), channel_id=1, source_target_pairs={{0,1},{1,2},{2,3},{3,4},{4,5},{5,6},{6,7},{7,8},{8,9},{9,10},{10,1... | collective-permute-start | bytes 196616 | tf_op jit(solution)/shard_map/ppermute | solution.py:18
  46.2 6.8 %collective-permute-start.5 = (f32[64,1,256]{2,1,0:T(1,128)S(1)}, f32[64,1,256]{2,1,0:T(1,128)S(1)}, u32[]{:S(2)}, u32[]{:S(2)}) collective-permute-start(f32[64,1,256]{2,1,0:T(1,128)S(1)} %get-tuple-element.30), channel_id=1, source_target_pairs={{1,0},{2,1},{3,2},{4,3},{5,4},{6,5},{7,6},{8,7},{9,8},{10,9},{11,1... | collective-permute-start | bytes 196616 | tf_op jit(solution)/shard_map/ppermute | solution.py:21
  60.8 4.5 %collective-permute-start.6 = (f32[64,1,256]{2,1,0:T(1,128)S(1)}, f32[64,1,256]{2,1,0:T(1,128)S(1)}, u32[]{:S(2)}, u32[]{:S(2)}) collective-permute-start(f32[64,1,256]{2,1,0:T(1,128)S(1)} %get-tuple-element.27), channel_id=1, source_target_pairs={{0,1},{1,2},{2,3},{3,4},{4,5},{5,6},{6,7},{7,8},{8,9},{9,10},{10,1... | collective-permute-start | bytes 196616 | tf_op jit(solution)/shard_map/ppermute | solution.py:18
  62.7 6.8 %collective-permute-start.7 = (f32[64,1,256]{2,1,0:T(1,128)S(1)}, f32[64,1,256]{2,1,0:T(1,128)S(1)}, u32[]{:S(2)}, u32[]{:S(2)}) collective-permute-start(f32[64,1,256]{2,1,0:T(1,128)S(1)} %get-tuple-element.28), channel_id=1, source_target_pairs={{1,0},{2,1},{3,2},{4,3},{5,4},{6,5},{7,6},{8,7},{9,8},{10,9},{11,1... | collective-permute-start | bytes 196616 | tf_op jit(solution)/shard_map/ppermute | solution.py:21
  77.6 1.3 copy-start.4
  79.0 4.4 %collective-permute-start.8 = (f32[64,1,256]{2,1,0:T(1,128)S(1)}, f32[64,1,256]{2,1,0:T(1,128)S(1)}, u32[]{:S(2)}, u32[]{:S(2)}) collective-permute-start(f32[64,1,256]{2,1,0:T(1,128)S(1)} %get-tuple-element.25), channel_id=1, source_target_pairs={{0,1},{1,2},{2,3},{3,4},{4,5},{5,6},{6,7},{7,8},{8,9},{9,10},{10,1... | collective-permute-start | bytes 196616 | tf_op jit(solution)/shard_map/ppermute | solution.py:18
  80.9 6.8 %collective-permute-start.9 = (f32[64,1,256]{2,1,0:T(1,128)S(1)}, f32[64,1,256]{2,1,0:T(1,128)S(1)}, u32[]{:S(2)}, u32[]{:S(2)}) collective-permute-start(f32[64,1,256]{2,1,0:T(1,128)S(1)} %get-tuple-element.26), channel_id=1, source_target_pairs={{1,0},{2,1},{3,2},{4,3},{5,4},{6,5},{7,6},{8,7},{9,8},{10,9},{11,1... | collective-permute-start | bytes 196616 | tf_op jit(solution)/shard_map/ppermute | solution.py:21
  83.3 8.5 %copy-start.2 = (f32[64,32,256]{2,1,0:T(8,128)S(1)}, f32[64,32,256]{2,1,0:T(8,128)}, u32[]{:S(2)}) copy-start(f32[64,32,256]{2,1,0:T(8,128)} %param.8) | copy-start | bytes 6291460
  83.3 8.5 %copy-start.5 = (f32[64,32,256]{2,1,0:T(8,128)S(1)}, f32[64,32,256]{2,1,0:T(8,128)}, u32[]{:S(2)}) copy-start(f32[64,32,256]{2,1,0:T(8,128)} %copy-done.4) | copy-start | bytes 6291460
  96.4 5.2 %collective-permute-start.10 = (f32[64,1,256]{2,1,0:T(1,128)S(1)}, f32[64,1,256]{2,1,0:T(1,128)S(1)}, u32[]{:S(2)}, u32[]{:S(2)}) collective-permute-start(f32[64,1,256]{2,1,0:T(1,128)S(1)} %get-tuple-element.23), channel_id=1, source_target_pairs={{0,1},{1,2},{2,3},{3,4},{4,5},{5,6},{6,7},{7,8},{8,9},{9,10},{10,1... | collective-permute-start | bytes 196616 | tf_op jit(solution)/shard_map/ppermute | solution.py:18
  98.4 6.8 %collective-permute-start.11 = (f32[64,1,256]{2,1,0:T(1,128)S(1)}, f32[64,1,256]{2,1,0:T(1,128)S(1)}, u32[]{:S(2)}, u32[]{:S(2)}) collective-permute-start(f32[64,1,256]{2,1,0:T(1,128)S(1)} %get-tuple-element.24), channel_id=1, source_target_pairs={{1,0},{2,1},{3,2},{4,3},{5,4},{6,5},{7,6},{8,7},{9,8},{10,9},{11,1... | collective-permute-start | bytes 196616 | tf_op jit(solution)/shard_map/ppermute | solution.py:21
  113.3 4.6 %collective-permute-start.12 = (f32[64,1,256]{2,1,0:T(1,128)S(1)}, f32[64,1,256]{2,1,0:T(1,128)S(1)}, u32[]{:S(2)}, u32[]{:S(2)}) collective-permute-start(f32[64,1,256]{2,1,0:T(1,128)S(1)} %get-tuple-element.21), channel_id=1, source_target_pairs={{0,1},{1,2},{2,3},{3,4},{4,5},{5,6},{6,7},{7,8},{8,9},{9,10},{10,1... | collective-permute-start | bytes 196616 | tf_op jit(solution)/shard_map/ppermute | solution.py:18
  115.2 6.8 %collective-permute-start.13 = (f32[64,1,256]{2,1,0:T(1,128)S(1)}, f32[64,1,256]{2,1,0:T(1,128)S(1)}, u32[]{:S(2)}, u32[]{:S(2)}) collective-permute-start(f32[64,1,256]{2,1,0:T(1,128)S(1)} %get-tuple-element.22), channel_id=1, source_target_pairs={{1,0},{2,1},{3,2},{4,3},{5,4},{6,5},{7,6},{8,7},{9,8},{10,9},{11,1... | collective-permute-start | bytes 196616 | tf_op jit(solution)/shard_map/ppermute | solution.py:21
  129.8 4.4 %collective-permute-start.14 = (f32[64,1,256]{2,1,0:T(1,128)S(1)}, f32[64,1,256]{2,1,0:T(1,128)S(1)}, u32[]{:S(2)}, u32[]{:S(2)}) collective-permute-start(f32[64,1,256]{2,1,0:T(1,128)S(1)} %get-tuple-element.19), channel_id=1, source_target_pairs={{0,1},{1,2},{2,3},{3,4},{4,5},{5,6},{6,7},{7,8},{8,9},{9,10},{10,1... | collective-permute-start | bytes 196616 | tf_op jit(solution)/shard_map/ppermute | solution.py:18
  131.7 6.8 %collective-permute-start.15 = (f32[64,1,256]{2,1,0:T(1,128)S(1)}, f32[64,1,256]{2,1,0:T(1,128)S(1)}, u32[]{:S(2)}, u32[]{:S(2)}) collective-permute-start(f32[64,1,256]{2,1,0:T(1,128)S(1)} %get-tuple-element.20), channel_id=1, source_target_pairs={{1,0},{2,1},{3,2},{4,3},{5,4},{6,5},{7,6},{8,7},{9,8},{10,9},{11,1... | collective-permute-start | bytes 196616 | tf_op jit(solution)/shard_map/ppermute | solution.py:21
  146.5 10.7 %copy-start.8 = (f32[64,32,256]{2,1,0:T(8,128)}, f32[64,32,256]{2,1,0:T(8,128)S(1)}, u32[]{:S(2)}) copy-start(f32[64,32,256]{2,1,0:T(8,128)S(1)} %fusion.10) | copy-start | bytes 6291460
  146.6 7.8 %collective-permute-start.16 = (f32[4,32,256]{2,1,0:T(8,128)S(1)}, f32[4,32,256]{2,1,0:T(8,128)S(1)}, u32[]{:S(2)}, u32[]{:S(2)}) collective-permute-start(f32[4,32,256]{2,1,0:T(8,128)S(1)} %pad_maximum_fusion.16), channel_id=1, source_target_pairs={{0,16},{16,32},{32,48},{48,64},{64,80},{80,96},{96,112},{112,128},... | collective-permute-start | bytes 393224 | tf_op jit(solution)/shard_map/ppermute | solution.py:29
  149.8 6.1 %collective-permute-start.17 = (f32[4,32,256]{2,1,0:T(8,128)S(1)}, f32[4,32,256]{2,1,0:T(8,128)S(1)}, u32[]{:S(2)}, u32[]{:S(2)}) collective-permute-start(f32[4,32,256]{2,1,0:T(8,128)S(1)} %pad_maximum_fusion.17), channel_id=1, source_target_pairs={{16,0},{32,16},{48,32},{64,48},{80,64},{96,80},{112,96},{128,112},... | collective-permute-start | bytes 393224 | tf_op jit(solution)/shard_map/ppermute | solution.py:29
where the time goes:
time: 159 us; the launch traced here: 157 us
  other arithmetic  70.5 us (44%)
  starting transfers between devices  45.5 us (29%)
  waiting for transfers between devices  35.9 us (23%)
  local copies, waits for them, and re-layouts  3.45 us (2%)
  between operations  1.93 us (1%)
    ppermute x8, waiting for transfers between devices, padded_2(): lax.ppermute(lax.slice_in_dim(block, 0, width, axis=dim), axis, backward)  34 us
    concatenate x8, other arithmetic, padded_2(): block = jnp.concatenate([low, block, high], axis=dim)  26.9 us
    add x4, other arithmetic, on_device(): first_iter = field + dir_zero  21.1 us
    add x4, other arithmetic, on_device(): field = first_iter + dir_one  19.8 us
    ppermute x8, starting transfers between devices, padded_2(): lax.ppermute(lax.slice_in_dim(block, 0, width, axis=dim), axis, backward)  19.3 us
    ppermute x8, starting transfers between devices, padded_2(): lax.ppermute(lax.slice_in_dim(block, block.shape[dim] - width, None, axis...  18.8 us
    ppermute x2, starting transfers between devices, shifted(): return lax.ppermute(block, axis, route)  7.39 us
  transfers between devices with their start and end apart: 18, of which 10 were waited for; matrix products, arithmetic and copies ran while one was open for 1% of the time, Pallas kernels for 0%

commit v1 on v0

v1 whole, which is shorter than its diff:
```python
import jax
import jax.numpy as jnp
from jax import lax
from jax.experimental import pallas as pl
from jax.experimental.pallas import tpu as pltpu
from jax.sharding import PartitionSpec as P

BETA = 1.5
RHO_ZERO = 0.9
RHO_ONE = 1.0 / (2.0 / 0.9 - 0.9)
COEF_ONE = RHO_ONE * RHO_ZERO
COEF_TWO = 2.0 * RHO_ONE / 0.9

LANES = 128
SUB = 8
HALO = 8
PLANES = 64
ROWS = 32
STEPS = 4
TALL = ROWS + 2 * HALO
TILES = TALL // SUB
HALVES = 2
CELLS = TILES * HALVES
GROUP = 8


def along_depth(low, high, first_lane, last_lane):
    right_low = pltpu.roll(low, 1, 1)
    right_high = pltpu.roll(high, 1, 1)
    left_low = pltpu.roll(low, LANES - 1, 1)
    left_high = pltpu.roll(high, LANES - 1, 1)
    return (
        jnp.where(first_lane, 0.0, right_low) + jnp.where(last_lane, left_high, left_low),
        jnp.where(first_lane, right_low, right_high) + jnp.where(last_lane, 0.0, left_high),
    )


def sweep(field, group, emit, first_lane, last_lane):
    base = group * GROUP
    for tile in range(TILES):
        before = [field[base, 2 * tile + half] for half in range(HALVES)]
        here = [field[base + 1, 2 * tile + half] for half in range(HALVES)]
        for plane in range(GROUP):
            at = base + plane
            after = [field[at + 2, 2 * tile + half] for half in range(HALVES)]
            depth = along_depth(here[0], here[1], first_lane, last_lane)
            for half in range(HALVES):
                if tile > 0:
                    above = field[at + 1, 2 * (tile - 1) + half]
                else:
                    above = pltpu.roll(field[at + 1, 2 * (TILES - 1) + half], 1, 0)
                if tile < TILES - 1:
                    below = field[at + 1, 2 * (tile + 1) + half]
                else:
                    below = pltpu.roll(field[at + 1, half], SUB - 1, 0)
                around = ((before[half] + after[half]) + (above + below)) + depth[half]
                emit(at, 2 * tile + half, here[half], around)
            before, here = here, after


def strided(tile):
    return pl.ds(tile, SUB, stride=TILES)


def kernel(
    widths, pressure, storage, source, left, right, low, high,
    field_out, trace_high_out, trace_low_out,
    p_nat, s_nat, f_nat, l_nat, r_nat, th_nat, tl_nat,
    u_even, u_odd, x1, b, s, f, dinv, dinv_two, in_sems, out_sems,
):
    width = widths[0]
    copies = []

    def fetch(src, dst):
        copy = pltpu.make_async_copy(src, dst, in_sems.at[len(copies)])
        copy.start()
        copies.append(copy)

    for half in range(HALVES):
        lanes = pl.ds(half * LANES, LANES)
        for index, (own, nat) in enumerate(((pressure, p_nat), (storage, s_nat), (source, f_nat))):
            planes = pl.ds(index * PLANES, PLANES)
            fetch(own.at[:, :, lanes], nat.at[:, half, pl.ds(HALO, ROWS), :])
            fetch(low.at[planes, :, lanes], nat.at[:, half, pl.ds(0, HALO), :])
            fetch(high.at[planes, :, lanes], nat.at[:, half, pl.ds(HALO + ROWS, HALO), :])
        for index, (own, nat) in enumerate(((left, l_nat), (right, r_nat))):
            planes = pl.ds(3 * PLANES + index * STEPS, STEPS)
            fetch(own.at[:, :, lanes], nat.at[:, half, pl.ds(HALO, ROWS), :])
            fetch(low.at[planes, :, lanes], nat.at[:, half, pl.ds(0, HALO), :])
            fetch(high.at[planes, :, lanes], nat.at[:, half, pl.ds(HALO + ROWS, HALO), :])
    for copy in copies:
        copy.wait()

    lane = lax.broadcasted_iota(jnp.int32, (SUB, LANES), 1)
    zero = jnp.zeros((SUB, LANES), jnp.float32)
    for cell in range(CELLS):
        for plane in (0, PLANES + 1):
            u_even[plane, cell] = zero
            u_odd[plane, cell] = zero
            x1[plane, cell] = zero

    def prepare(x, _):
        live = (x < width).astype(jnp.float32)
        extra = 4.0 + jnp.where(x == 0, BETA, 1.0) + jnp.where(x == width - 1, BETA, 1.0)
        for tile in range(TILES):
            for half in range(HALVES):
                cell = 2 * tile + half
                rows = strided(tile)
                coef = s_nat[x, half, rows, :]
                u_even[x + 1, cell] = p_nat[x, half, rows, :] * live
                s[x, cell] = coef
                f[x, cell] = f_nat[x, half, rows, :]
                inverse = jnp.where(coef > 0.0, live / (coef + extra), 0.0)
                dinv[x, cell] = inverse
                dinv_two[x, cell] = COEF_TWO * inverse
        return 0

    lax.fori_loop(0, PLANES, prepare, 0)

    first_lane = lane == 0
    last_lane = lane == LANES - 1
    for step in range(STEPS):
        u, u_next = (u_even, u_odd) if step % 2 == 0 else (u_odd, u_even)
        for cell in range(CELLS):
            rows = strided(cell // 2)
            f[0, cell] = f_nat[0, cell % 2, rows, :] + l_nat[step, cell % 2, rows, :]
            f[width - 1, cell] = f_nat[width - 1, cell % 2, rows, :] + r_nat[step, cell % 2, rows, :]

        def first_half(group, _, u=u):
            def emit(x, cell, here, around):
                rhs = s[x, cell] * here + f[x, cell]
                b[x, cell] = rhs
                x1[x + 1, cell] = (rhs + around) * dinv[x, cell]

            sweep(u, group, emit, first_lane, last_lane)
            return 0

        def second_half(group, _, u=u, u_next=u_next, step=step):
            def emit(x, cell, here, around):
                value = (b[x, cell] + around) * dinv_two[x, cell] - COEF_ONE * u[x + 1, cell]
                u_next[x + 1, cell] = value
                if step == STEPS - 1:
                    p_nat[x, cell % 2, strided(cell // 2), :] = value

            sweep(x1, group, emit, first_lane, last_lane)
            return 0

        lax.fori_loop(0, PLANES // GROUP, first_half, 0)
        lax.fori_loop(0, PLANES // GROUP, second_half, 0)
        for cell in range(CELLS):
            rows = strided(cell // 2)
            at_a, at_b = u_next[1, cell], u_next[2, cell]
            at_c, at_d = u_next[width, cell], u_next[width - 1, cell]
            tl_nat[step, cell % 2, rows, :] = BETA * at_a + (at_a - at_b)
            th_nat[step, cell % 2, rows, :] = BETA * at_c + (at_c - at_d)

    outs = []
    for half in range(HALVES):
        lanes = pl.ds(half * LANES, LANES)
        for nat, out in ((th_nat, trace_high_out), (tl_nat, trace_low_out), (p_nat, field_out)):
            copy = pltpu.make_async_copy(
                nat.at[:, half, pl.ds(HALO, ROWS), :], out.at[:, :, lanes], out_sems.at[len(outs)]
            )
            copy.start()
            outs.append(copy)
    for copy in outs:
        copy.wait()


def on_device(pressure, storage, source, left_data, right_data, widths):
    left_in = left_data[0]
    right_in = right_data[0]
    arrays = (pressure, storage, source, left_in, right_in)
    count = lax.axis_size("dev")
    forward = [(i, i + 1) for i in range(count - 1)]
    backward = [(i + 1, i) for i in range(count - 1)]
    low = lax.ppermute(jnp.concatenate([a[:, ROWS - HALO :] for a in arrays]), "dev", forward)
    high = lax.ppermute(jnp.concatenate([a[:, :HALO] for a in arrays]), "dev", backward)

    anywhere = pl.BlockSpec(memory_space=pl.ANY)
    natural = pltpu.VMEM((PLANES, HALVES, TALL, LANES), jnp.float32)
    narrow = pltpu.VMEM((STEPS, HALVES, TALL, LANES), jnp.float32)
    tiled = pltpu.VMEM((PLANES, CELLS, SUB, LANES), jnp.float32)
    padded = pltpu.VMEM((PLANES + 2, CELLS, SUB, LANES), jnp.float32)
    trace = jax.ShapeDtypeStruct(left_in.shape, jnp.float32)
    field, trace_high, trace_low = pl.pallas_call(
        kernel,
        out_shape=(jax.ShapeDtypeStruct(pressure.shape, jnp.float32), trace, trace),
        in_specs=[pl.BlockSpec(memory_space=pltpu.SMEM)] + [anywhere] * 7,
        out_specs=(anywhere,) * 3,
        scratch_shapes=[
            natural, natural, natural, narrow, narrow, narrow, narrow,
            padded, padded, padded, tiled, tiled, tiled, tiled, tiled,
            pltpu.SemaphoreType.DMA((30,)), pltpu.SemaphoreType.DMA((6,)),
        ],
        compiler_params=pltpu.CompilerParams(vmem_limit_bytes=44 * 2**20),
        name="window",
    )(widths, pressure, storage, source, left_in, right_in, low, high)

    subs = lax.axis_size("sub")
    up = [(i, i + 1) for i in range(subs - 1)]
    down = [(i + 1, i) for i in range(subs - 1)]
    new_left = lax.ppermute(trace_high, "sub", up)
    new_right = lax.ppermute(trace_low, "sub", down)
    return (field, new_left[None], new_right[None])


def solution(mesh):
    in_specs = (
        P("sub", "dev", None),
        P("sub", "dev", None),
        P("sub", "dev", None),
        P("sub", None, "dev", None),
        P("sub", None, "dev", None),
        P("sub"),
    )
    out_specs = (P("sub", "dev", None), P("sub", None, "dev", None), P("sub", None, "dev", None))
    return jax.shard_map(
        on_device, mesh=mesh, in_specs=in_specs, out_specs=out_specs, check_vma=False
    )
```

time: 159 us -> 66.4 us (0.42)
  the two profiles are of different devices: /device:TPU:101 before, /device:TPU:121 now
where the time goes in v1:
time: 66.4 us; the launch traced here: 66.2 us
  waiting for transfers between devices  26.4 us (40%)
  Pallas kernels  21.7 us (33%)
  starting transfers between devices  12.5 us (19%)
  local copies, waits for them, and re-layouts  4.29 us (6%)
  between operations  1.37 us (2%)
    pallas_call x1, Pallas kernels, on_device(): pl.pallas_call(kernel, out_shape=(jax.ShapeDtypeStruct(pressure.shape, jn...  21.7 us
    ppermute x1, waiting for transfers between devices, on_device(): lax.ppermute(jnp.concatenate([a[:, ROWS - HALO:] for a in arrays]), 'dev'...  15.5 us
    ppermute x1, waiting for transfers between devices, on_device(): lax.ppermute(jnp.concatenate([a[:, :HALO] for a in arrays]), 'dev', backw...  5.61 us
    ppermute x1, starting transfers between devices, on_device(): lax.ppermute(jnp.concatenate([a[:, ROWS - HALO:] for a in arrays]), 'dev'...  5.3 us
    ppermute x1, waiting for transfers between devices, on_device(): new_right = lax.ppermute(trace_low, 'sub', down)  4.89 us
    unnamed x16, local copies, waits for them, and re-layouts  4.28 us
    ppermute x1, starting transfers between devices, on_device(): new_left = lax.ppermute(trace_high, 'sub', up)  2.78 us
    ppermute x1, starting transfers between devices, on_device(): new_right = lax.ppermute(trace_low, 'sub', down)  2.5 us
  transfers between devices with their start and end apart: 4, of which 4 were waited for; matrix products, arithmetic and copies ran while one was open for 0% of the time, Pallas kernels for 0%

profile of v1, /device:TPU:121, one launch (start us, length us, event | category | flops | bytes accessed | tf_op | source)
XLA Modules:
  0.0 66.2 jit_solution(18328595784367171770)
XLA Ops:
  0.6 0.0 copy-start.1
  0.6 0.0 copy-start.2
  0.7 1.4 %slice_dynamic-update-slice_fusion.2 = (f32[200,8,256]{2,1,0:T(8,128)S(1)}, f32[200,8,256]{2,1,0:T(8,128)S(1)}) fusion(f32[64,32,256]{2,1,0:T(8,128)} %pressure.1), kind=kLoop, calls=%fused_computation.2 | loop fusion | bytes 2097152
  2.1 0.5 copy-done.1
  2.5 0.0 copy-start.3
  2.5 0.0 copy-start.4
  2.5 0.1 slice_dynamic-update-slice_fusion.1
  2.6 0.0 copy-start
  2.7 0.5 copy-done.2
  3.2 0.1 slice_dynamic-update-slice_fusion
  3.3 0.3 copy-done.3
  3.6 0.0 copy-done.4
  3.7 5.3 %collective-permute-start = (f32[200,8,256]{2,1,0:T(8,128)S(1)}, f32[200,8,256]{2,1,0:T(8,128)S(1)}, u32[]{:S(2)}, u32[]{:S(2)}) collective-permute-start(f32[200,8,256]{2,1,0:T(8,128)S(1)} %get-tuple-element.16), channel_id=1, source_target_pairs={{0,1},{1,2},{2,3},{3,4},{4,5},{5,6},{6,7},{7,8},{8,9},{9,10},{10,1... | collective-permute-start | bytes 4915208 | tf_op jit(solution)/shard_map/ppermute | solution.py:177
  9.0 1.9 %collective-permute-start.1 = (f32[200,8,256]{2,1,0:T(8,128)S(1)}, f32[200,8,256]{2,1,0:T(8,128)S(1)}, u32[]{:S(2)}, u32[]{:S(2)}) collective-permute-start(f32[200,8,256]{2,1,0:T(8,128)S(1)} %get-tuple-element.15), channel_id=1, source_target_pairs={{1,0},{2,1},{3,2},{4,3},{5,4},{6,5},{7,6},{8,7},{9,8},{10,9},{11,1... | collective-permute-start | bytes 4915208 | tf_op jit(solution)/shard_map/ppermute | solution.py:178
  11.5 15.5 %collective-permute-done.low = f32[200,8,256]{2,1,0:T(8,128)S(1)} collective-permute-done((f32[200,8,256]{2,1,0:T(8,128)S(1)}, f32[200,8,256]{2,1,0:T(8,128)S(1)}, u32[]{:S(2)}, u32[]{:S(2)}) %collective-permute-start) | collective-permute-done | bytes 1638432 | tf_op jit(solution)/shard_map/ppermute | solution.py:177
  27.0 5.6 %collective-permute-done.1.high = f32[200,8,256]{2,1,0:T(8,128)S(1)} collective-permute-done((f32[200,8,256]{2,1,0:T(8,128)S(1)}, f32[200,8,256]{2,1,0:T(8,128)S(1)}, u32[]{:S(2)}, u32[]{:S(2)}) %collective-permute-start.1) | collective-permute-done | bytes 1638432 | tf_op jit(solution)/shard_map/ppermute | solution.py:178
  32.6 0.0 copy-done
  32.6 21.7 %window.1 = (f32[64,32,256]{2,1,0:T(8,128)}, f32[4,32,256]{2,1,0:T(8,128)S(1)}, f32[4,32,256]{2,1,0:T(8,128)S(1)}) custom-call(s32[1]{0:T(128)S(6)} %copy.19.widths, f32[64,32,256]{2,1,0:T(8,128)S(1)} %copy-done, f32[64,32,256]{2,1,0:T(8,128)S(1)} %copy-done.1, f32[64,32,256]{2,1,0:T(8,128)S(1)} %copy-done.2, f32[4,32,256]{2,1,0:T(8,128)S(1)} %bitcast.5, ...), custom_call_target="tpu_custom_call" | custom-call | tf_op jit(solution)/shard_map/window/pallas_call | solution.py:186
  54.3 2.8 %collective-permute-start.2 = (f32[4,32,256]{2,1,0:T(8,128)S(1)}, f32[4,32,256]{2,1,0:T(8,128)S(1)}, u32[]{:S(2)}, u32[]{:S(2)}) collective-permute-start(f32[4,32,256]{2,1,0:T(8,128)S(1)} %get-tuple-element.7), channel_id=1, source_target_pairs={{0,16},{16,32},{32,48},{48,64},{64,80},{80,96},{96,112},{112,128},... | collective-permute-start | bytes 393224 | tf_op jit(solution)/shard_map/ppermute | solution.py:203
  57.1 2.5 %collective-permute-start.3 = (f32[4,32,256]{2,1,0:T(8,128)S(1)}, f32[4,32,256]{2,1,0:T(8,128)S(1)}, u32[]{:S(2)}, u32[]{:S(2)}) collective-permute-start(f32[4,32,256]{2,1,0:T(8,128)S(1)} %get-tuple-element.8), channel_id=1, source_target_pairs={{16,0},{32,16},{48,32},{64,48},{80,64},{96,80},{112,96},{128,112},... | collective-permute-start | bytes 393224 | tf_op jit(solution)/shard_map/ppermute | solution.py:204
  59.6 0.4 collective-permute-done.2
  60.0 4.9 %collective-permute-done.3 = f32[4,32,256]{2,1,0:T(8,128)S(1)} collective-permute-done((f32[4,32,256]{2,1,0:T(8,128)S(1)}, f32[4,32,256]{2,1,0:T(8,128)S(1)}, u32[]{:S(2)}, u32[]{:S(2)}) %collective-permute-start.3) | collective-permute-done | bytes 131104 | tf_op jit(solution)/shard_map/ppermute | solution.py:204
  64.9 0.7 copy.20
  65.5 0.7 copy.21
  (2 shorter events, 0.0 us)
Async XLA Ops:
  0.6 1.9 %copy-start.1 = (f32[64,32,256]{2,1,0:T(8,128)S(1)}, f32[64,32,256]{2,1,0:T(8,128)}, u32[]{:S(2)}) copy-start(f32[64,32,256]{2,1,0:T(8,128)} %storage.1) | copy-start | bytes 6291460
  0.6 2.5 %copy-start.2 = (f32[64,32,256]{2,1,0:T(8,128)S(1)}, f32[64,32,256]{2,1,0:T(8,128)}, u32[]{:S(2)}) copy-start(f32[64,32,256]{2,1,0:T(8,128)} %source.1) | copy-start | bytes 6291460
  2.5 1.1 %copy-start.3 = (f32[1,4,32,256]{3,2,1,0:T(8,128)S(1)}, f32[1,4,32,256]{3,2,1,0:T(8,128)}, u32[]{:S(2)}) copy-start(f32[1,4,32,256]{3,2,1,0:T(8,128)} %param.9) | copy-start | bytes 393220
  2.5 1.1 %copy-start.4 = (f32[1,4,32,256]{3,2,1,0:T(8,128)S(1)}, f32[1,4,32,256]{3,2,1,0:T(8,128)}, u32[]{:S(2)}) copy-start(f32[1,4,32,256]{3,2,1,0:T(8,128)} %param.10) | copy-start | bytes 393220
  2.6 30.0 %copy-start = (f32[64,32,256]{2,1,0:T(8,128)S(1)}, f32[64,32,256]{2,1,0:T(8,128)}, u32[]{:S(2)}) copy-start(f32[64,32,256]{2,1,0:T(8,128)} %pressure.1) | copy-start | bytes 6291460
  3.7 23.4 %collective-permute-start = (f32[200,8,256]{2,1,0:T(8,128)S(1)}, f32[200,8,256]{2,1,0:T(8,128)S(1)}, u32[]{:S(2)}, u32[]{:S(2)}) collective-permute-start(f32[200,8,256]{2,1,0:T(8,128)S(1)} %get-tuple-element.16), channel_id=1, source_target_pairs={{0,1},{1,2},{2,3},{3,4},{4,5},{5,6},{6,7},{7,8},{8,9},{9,10},{10,1... | collective-permute-start | bytes 4915208 | tf_op jit(solution)/shard_map/ppermute | solution.py:177
  9.0 23.6 %collective-permute-start.1 = (f32[200,8,256]{2,1,0:T(8,128)S(1)}, f32[200,8,256]{2,1,0:T(8,128)S(1)}, u32[]{:S(2)}, u32[]{:S(2)}) collective-permute-start(f32[200,8,256]{2,1,0:T(8,128)S(1)} %get-tuple-element.15), channel_id=1, source_target_pairs={{1,0},{2,1},{3,2},{4,3},{5,4},{6,5},{7,6},{8,7},{9,8},{10,9},{11,1... | collective-permute-start | bytes 4915208 | tf_op jit(solution)/shard_map/ppermute | solution.py:178
  54.3 5.7 %collective-permute-start.2 = (f32[4,32,256]{2,1,0:T(8,128)S(1)}, f32[4,32,256]{2,1,0:T(8,128)S(1)}, u32[]{:S(2)}, u32[]{:S(2)}) collective-permute-start(f32[4,32,256]{2,1,0:T(8,128)S(1)} %get-tuple-element.7), channel_id=1, source_target_pairs={{0,16},{16,32},{32,48},{48,64},{64,80},{80,96},{96,112},{112,128},... | collective-permute-start | bytes 393224 | tf_op jit(solution)/shard_map/ppermute | solution.py:203
  57.1 7.8 %collective-permute-start.3 = (f32[4,32,256]{2,1,0:T(8,128)S(1)}, f32[4,32,256]{2,1,0:T(8,128)S(1)}, u32[]{:S(2)}, u32[]{:S(2)}) collective-permute-start(f32[4,32,256]{2,1,0:T(8,128)S(1)} %get-tuple-element.8), channel_id=1, source_target_pairs={{16,0},{32,16},{48,32},{64,48},{80,64},{96,80},{112,96},{128,112},... | collective-permute-start | bytes 393224 | tf_op jit(solution)/shard_map/ppermute | solution.py:204

commit v2 on v1

v2 whole, which is shorter than its diff:
```python
import functools

import jax
import jax.numpy as jnp
from jax import lax
from jax.experimental import pallas as pl
from jax.experimental.pallas import tpu as pltpu
from jax.sharding import PartitionSpec as P

BETA = 1.5
RHO_ZERO = 0.9
RHO_ONE = 1.0 / (2.0 / 0.9 - 0.9)
COEF_ONE = RHO_ONE * RHO_ZERO
COEF_TWO = 2.0 * RHO_ONE / 0.9

LANES = 128
SUB = 8
HALVES = 2
HALO = 8
PLANES = 64
ROWS = 32
STEPS = 4
GROUP = 8
CHUNKS = 4
PACK_BYTES = 57 * 2**20
WINDOW_BYTES = 50 * 2**20


def along_depth(low, high, first_lane, last_lane):
    right_low = pltpu.roll(low, 1, 1)
    right_high = pltpu.roll(high, 1, 1)
    left_low = pltpu.roll(low, LANES - 1, 1)
    left_high = pltpu.roll(high, LANES - 1, 1)
    return (
        jnp.where(first_lane, 0.0, right_low) + jnp.where(last_lane, left_high, left_low),
        jnp.where(first_lane, right_low, right_high) + jnp.where(last_lane, 0.0, left_high),
    )


def sweep(tiles, field, group, emit, first_lane, last_lane):
    cells = tiles * HALVES
    base = group * GROUP
    before = [field[base, cell] for cell in range(cells)]
    here = [field[base + 1, cell] for cell in range(cells)]
    for plane in range(GROUP):
        at = base + plane
        after = [field[at + 2, cell] for cell in range(cells)]
        for tile in range(tiles):
            depth = along_depth(here[2 * tile], here[2 * tile + 1], first_lane, last_lane)
            for half in range(HALVES):
                cell = 2 * tile + half
                if tile > 0:
                    above = here[cell - 2]
                else:
                    above = pltpu.roll(here[cells - 2 + half], 1, 0)
                if tile < tiles - 1:
                    below = here[cell + 2]
                else:
                    below = pltpu.roll(here[half], SUB - 1, 0)
                around = ((before[cell] + after[cell]) + (above + below)) + depth[half]
                emit(at, cell, here[cell], around)
        before, here = here, after


def pack_kernel(pressure, storage, source, left, right, off_chip, on_chip, sems):
    odd = lax.rem(lax.axis_index("dev"), 2)
    copies = []
    for out, row in ((off_chip, odd * (ROWS - HALO)), (on_chip, (1 - odd) * (ROWS - HALO))):
        rows = pl.ds(pl.multiple_of(row, SUB), HALO)
        at = 0
        for own in (pressure, storage, source, left, right):
            planes = own.shape[0]
            copy = pltpu.make_async_copy(
                own.at[:, rows, :], out.at[pl.ds(at, planes)], sems.at[len(copies)]
            )
            copy.start()
            copies.append(copy)
            at += planes
    for copy in copies:
        copy.wait()


def window_kernel(
    tiles, own_rows, halo_at_end, kept_rows, aliased,
    widths, pressure, storage, source, left, right, halo, *rest,
):
    if aliased:
        rest = rest[3:]
    (
        field_out, trace_high_out, trace_low_out,
        p_nat, s_nat, f_nat, l_nat, r_nat, th_nat, tl_nat,
        u_even, u_odd, x1, b, s, f, dinv, dinv_two, in_sems, out_sems,
    ) = rest
    cells = tiles * HALVES
    width = widths[0]
    odd = lax.rem(lax.axis_index("dev"), 2)
    at_end = odd if halo_at_end == 1 else 1 - odd
    own_src = pl.ds(pl.multiple_of(at_end * (ROWS - own_rows), SUB), own_rows)
    own_dst = pl.ds(pl.multiple_of((1 - at_end) * HALO, SUB), own_rows)
    halo_dst = pl.ds(pl.multiple_of(at_end * own_rows, SUB), HALO)
    kept_src = pl.ds(HALO, kept_rows)
    kept_dst = pl.ds(pl.multiple_of(at_end * (ROWS - kept_rows), SUB), kept_rows)

    count = 0

    def fetch(own, nat, size, start, offset):
        nonlocal count
        copies = []
        for half in range(HALVES):
            lanes = pl.ds(half * LANES, LANES)
            planes = pl.ds(start, size)
            for src, dst in (
                (own.at[planes, own_src, lanes], nat.at[planes, half, own_dst, :]),
                (halo.at[pl.ds(offset + start, size), :, lanes], nat.at[planes, half, halo_dst, :]),
            ):
                copy = pltpu.make_async_copy(src, dst, in_sems.at[count])
                copy.start()
                copies.append(copy)
                count += 1
        return copies

    size = PLANES // CHUNKS
    waits = []
    for chunk in range(CHUNKS):
        waits.append([])
        for index, (own, nat) in enumerate(((pressure, p_nat), (storage, s_nat), (source, f_nat))):
            waits[chunk] += fetch(own, nat, size, chunk * size, index * PLANES)
    last_waits = fetch(left, l_nat, STEPS, 0, 3 * PLANES)
    last_waits += fetch(right, r_nat, STEPS, 0, 3 * PLANES + STEPS)

    lane = lax.broadcasted_iota(jnp.int32, (SUB, LANES), 1)
    first_lane = lane == 0
    last_lane = lane == LANES - 1
    zero = jnp.zeros((SUB, LANES), jnp.float32)
    for cell in range(cells):
        for plane in (0, PLANES + 1):
            u_even[plane, cell] = zero
            u_odd[plane, cell] = zero
            x1[plane, cell] = zero

    def strided(tile):
        return pl.ds(tile, SUB, stride=tiles)

    def prepare(x, _):
        live = (x < width).astype(jnp.float32)
        extra = 4.0 + jnp.where(x == 0, BETA, 1.0) + jnp.where(x == width - 1, BETA, 1.0)
        for cell in range(cells):
            half, rows = cell % 2, strided(cell // 2)
            coef = s_nat[x, half, rows, :]
            u_even[x + 1, cell] = p_nat[x, half, rows, :] * live
            s[x, cell] = coef
            f[x, cell] = f_nat[x, half, rows, :]
            inverse = jnp.where(coef > 0.0, live / (coef + extra), 0.0)
            dinv[x, cell] = inverse
            dinv_two[x, cell] = COEF_TWO * inverse
        return 0

    for chunk in range(CHUNKS):
        for copy in waits[chunk]:
            copy.wait()
        lax.fori_loop(chunk * size, (chunk + 1) * size, prepare, 0)
    for copy in last_waits:
        copy.wait()

    for step in range(STEPS):
        u, u_next = (u_even, u_odd) if step % 2 == 0 else (u_odd, u_even)
        for cell in range(cells):
            half, rows = cell % 2, strided(cell // 2)
            f[0, cell] = f_nat[0, half, rows, :] + l_nat[step, half, rows, :]
            f[width - 1, cell] = f_nat[width - 1, half, rows, :] + r_nat[step, half, rows, :]

        def first_half(group, _, u=u):
            def emit(x, cell, here, around):
                rhs = s[x, cell] * here + f[x, cell]
                b[x, cell] = rhs
                x1[x + 1, cell] = (rhs + around) * dinv[x, cell]

            sweep(tiles, u, group, emit, first_lane, last_lane)
            return 0

        def second_half(group, _, u=u, u_next=u_next, step=step):
            def emit(x, cell, here, around):
                value = (b[x, cell] + around) * dinv_two[x, cell] - COEF_ONE * u[x + 1, cell]
                u_next[x + 1, cell] = value
                if step == STEPS - 1:
                    p_nat[x, cell % 2, strided(cell // 2), :] = value

            sweep(tiles, x1, group, emit, first_lane, last_lane)
            return 0

        lax.fori_loop(0, PLANES // GROUP, first_half, 0)
        lax.fori_loop(0, PLANES // GROUP, second_half, 0)
        for cell in range(cells):
            half, rows = cell % 2, strided(cell // 2)
            at_a, at_b = u_next[1, cell], u_next[2, cell]
            at_c, at_d = u_next[width, cell], u_next[width - 1, cell]
            tl_nat[step, half, rows, :] = BETA * at_a + (at_a - at_b)
            th_nat[step, half, rows, :] = BETA * at_c + (at_c - at_d)

    outs = []
    for half in range(HALVES):
        lanes = pl.ds(half * LANES, LANES)
        for nat, out in ((th_nat, trace_high_out), (tl_nat, trace_low_out), (p_nat, field_out)):
            copy = pltpu.make_async_copy(
                nat.at[:, half, kept_src, :], out.at[:, kept_dst, lanes], out_sems.at[len(outs)]
            )
            copy.start()
            outs.append(copy)
    for copy in outs:
        copy.wait()


ANYWHERE = pl.BlockSpec(memory_space=pl.ANY)
IN_HBM = pl.BlockSpec(memory_space=pltpu.HBM)


def run_window(tiles, own_rows, halo_at_end, kept_rows, name, args, previous=()):
    rows = tiles * SUB
    cells = tiles * HALVES
    natural = pltpu.VMEM((PLANES, HALVES, rows, LANES), jnp.float32)
    narrow = pltpu.VMEM((STEPS, HALVES, rows, LANES), jnp.float32)
    tiled = pltpu.VMEM((PLANES, cells, SUB, LANES), jnp.float32)
    padded = pltpu.VMEM((PLANES + 2, cells, SUB, LANES), jnp.float32)
    pressure, left = args[1], args[4]
    field = jax.ShapeDtypeStruct(pressure.shape, jnp.float32)
    trace = jax.ShapeDtypeStruct(left.shape, jnp.float32)
    return pl.pallas_call(
        functools.partial(
            window_kernel, tiles, own_rows, halo_at_end, kept_rows, bool(previous)
        ),
        out_shape=(field, trace, trace),
        in_specs=[pl.BlockSpec(memory_space=pltpu.SMEM)] + [IN_HBM] * 5 + [ANYWHERE] * (1 + len(previous)),
        out_specs=(ANYWHERE,) * 3,
        input_output_aliases={7 + i: i for i in range(len(previous))},
        scratch_shapes=[
            natural, natural, natural, narrow, narrow, narrow, narrow,
            padded, padded, padded, tiled, tiled, tiled, tiled, tiled,
            pltpu.SemaphoreType.DMA((12 * CHUNKS + 8,)), pltpu.SemaphoreType.DMA((6,)),
        ],
        compiler_params=pltpu.CompilerParams(vmem_limit_bytes=WINDOW_BYTES),
        cost_estimate=pl.CostEstimate(
            flops=PLANES * rows * HALVES * LANES * 22 * STEPS,
            bytes_accessed=4 * PLANES * rows * HALVES * LANES * 4,
            transcendentals=0,
        ),
        name=name,
    )(*args, *previous)


def on_device(pressure, storage, source, left_data, right_data, widths):
    left_in = left_data[0]
    right_in = right_data[0]
    arrays = (pressure, storage, source, left_in, right_in)
    edge = jax.ShapeDtypeStruct((3 * PLANES + 2 * STEPS, HALO, pressure.shape[2]), jnp.float32)
    off_chip, on_chip = pl.pallas_call(
        pack_kernel,
        out_shape=(edge, edge),
        in_specs=[IN_HBM] * 5,
        out_specs=(ANYWHERE,) * 2,
        scratch_shapes=[pltpu.SemaphoreType.DMA((10,))],
        compiler_params=pltpu.CompilerParams(vmem_limit_bytes=PACK_BYTES),
        name="pack",
    )(*arrays)
    count = lax.axis_size("dev")
    chips = [(i, i + 1) for i in range(1, count - 1, 2)]
    cores = [(i, i + 1) for i in range(0, count, 2)]
    off_chip = lax.ppermute(off_chip, "dev", chips + [(j, i) for i, j in chips])
    on_chip = lax.ppermute(on_chip, "dev", cores + [(j, i) for i, j in cores])

    inner = run_window(5, ROWS, 0, ROWS - HALO, "inner", (widths, *arrays, on_chip))
    field, trace_high, trace_low = run_window(
        3, 2 * HALO, 1, HALO, "outer", (widths, *arrays, off_chip), inner
    )

    subs = lax.axis_size("sub")
    up = [(i, i + 1) for i in range(subs - 1)]
    down = [(i + 1, i) for i in range(subs - 1)]
    new_left = lax.ppermute(trace_high, "sub", up)
    new_right = lax.ppermute(trace_low, "sub", down)
    return (field, new_left[None], new_right[None])


def solution(mesh):
    in_specs = (
        P("sub", "dev", None),
        P("sub", "dev", None),
        P("sub", "dev", None),
        P("sub", None, "dev", None),
        P("sub", None, "dev", None),
        P("sub"),
    )
    out_specs = (P("sub", "dev", None), P("sub", None, "dev", None), P("sub", None, "dev", None))
    return jax.shard_map(
        on_device, mesh=mesh, in_specs=in_specs, out_specs=out_specs, check_vma=False
    )
```

time: 66.4 us -> 155 us (2.33)
  the two profiles are of different devices: /device:TPU:121 before, /device:TPU:101 now
where the time goes in v2:
time: 155 us; the launch traced here: 154 us
  Pallas kernels  136 us (88%)
  starting transfers between devices  12.8 us (8%)
  waiting for transfers between devices  2.4 us (2%)
    pallas_call x1, Pallas kernels, on_device(): pl.pallas_call(pack_kernel, out_shape=(edge, edge), in_specs=[IN_HBM] * 5...  100 us
    pallas_call x2, Pallas kernels, run_window(): pl.pallas_call(functools.partial(window_kernel, tiles, own_rows, halo_at_...  35.3 us
    ppermute x1, starting transfers between devices, on_device(): off_chip = lax.ppermute(off_chip, 'dev', chips + [(j, i) for i, j in chips])  4.65 us
    ppermute x1, starting transfers between devices, on_device(): new_right = lax.ppermute(trace_low, 'sub', down)  4.2 us
    ppermute x1, starting transfers between devices, on_device(): new_left = lax.ppermute(trace_high, 'sub', up)  3.19 us
  transfers between devices with their start and end apart: 4, of which 2 were waited for; matrix products, arithmetic and copies ran while one was open for 0% of the time, Pallas kernels for 13%

profile of v2, /device:TPU:101, one launch (start us, length us, event | category | flops | bytes accessed | tf_op | source)
XLA Modules:
  0.0 153.7 jit_solution(18044962510850841306)
XLA Ops:
  0.6 0.0 copy-start
  0.6 0.0 copy-start.1
  0.7 100.5 %pack.1 = (f32[200,8,256]{2,1,0:T(8,128)}, f32[200,8,256]{2,1,0:T(8,128)}) custom-call(f32[64,32,256]{2,1,0:T(8,128)} %pressure.5, f32[64,32,256]{2,1,0:T(8,128)} %storage.5, f32[64,32,256]{2,1,0:T(8,128)} %source.5, f32[4,32,256]{2,1,0:T(8,128)} %bitcast.4, f32[4,32,256]{2,1,0:T(8,128)} %bitcast.7), custom_call_target="tpu_custom_call" | custom-call | tf_op jit(solution)/shard_map/pack/pallas_call | solution.py:255
  101.1 0.8 collective-permute-start.1
  101.9 4.7 %collective-permute-start = (f32[200,8,256]{2,1,0:T(8,128)}, f32[200,8,256]{2,1,0:T(8,128)S(1)}, u32[]{:S(2)}, u32[]{:S(2)}) collective-permute-start(f32[200,8,256]{2,1,0:T(8,128)} %get-tuple-element.11), channel_id=1, source_target_pairs={{1,2},{3,4},{5,6},{7,8},{9,10},{11,12},{13,14},{2,1},{4,3},{6,5},{... | collective-permute-start | bytes 4915208 | tf_op jit(solution)/shard_map/ppermute | solution.py:267
  107.2 0.0 collective-permute-done.1.halo
  107.2 0.0 copy-done
  107.2 0.0 copy-done.1
  107.2 20.4 %inner.1 = (f32[64,32,256]{2,1,0:T(8,128)}, f32[4,32,256]{2,1,0:T(8,128)S(1)}, f32[4,32,256]{2,1,0:T(8,128)S(1)}) custom-call(s32[1]{0:T(128)S(6)} %copy.17.widths, f32[64,32,256]{2,1,0:T(8,128)} %pressure.5, f32[64,32,256]{2,1,0:T(8,128)} %storage.5, f32[64,32,256]{2,1,0:T(8,128)} %source.5, f32[4,32,256]{2,1,0:T(8,128)S(1)} %bitcast.5, ...), custom_call_target="tpu_custom_call" | custom-call | flops 57671680 | bytes 10485760 | tf_op jit(solution)/shard_map/inner/pallas_call | solution.py:227
  127.7 0.0 collective-permute-done.halo
  127.7 14.9 %outer.1 = (f32[64,32,256]{2,1,0:T(8,128)}, f32[4,32,256]{2,1,0:T(8,128)S(1)}, f32[4,32,256]{2,1,0:T(8,128)S(1)}) custom-call(s32[1]{0:T(128)S(6)} %copy.17.widths, f32[64,32,256]{2,1,0:T(8,128)} %pressure.5, f32[64,32,256]{2,1,0:T(8,128)} %storage.5, f32[64,32,256]{2,1,0:T(8,128)} %source.5, ...), custom_call_target="tpu_custom_call", output_to_operand_aliasing={{0}: (7, {}), {1}: (8, {}), {2}: (9, {})} | custom-call | flops 34603008 | bytes 6291456 | tf_op jit(solution)/shard_map/outer/pallas_call | solution.py:227
  142.6 3.2 %collective-permute-start.2 = (f32[4,32,256]{2,1,0:T(8,128)S(1)}, f32[4,32,256]{2,1,0:T(8,128)S(1)}, u32[]{:S(2)}, u32[]{:S(2)}) collective-permute-start(f32[4,32,256]{2,1,0:T(8,128)S(1)} %get-tuple-element.17), channel_id=1, source_target_pairs={{0,16},{16,32},{32,48},{48,64},{64,80},{80,96},{96,112},{112,128},... | collective-permute-start | bytes 393224 | tf_op jit(solution)/shard_map/ppermute | solution.py:278
  145.8 4.2 %collective-permute-start.3 = (f32[4,32,256]{2,1,0:T(8,128)S(1)}, f32[4,32,256]{2,1,0:T(8,128)S(1)}, u32[]{:S(2)}, u32[]{:S(2)}) collective-permute-start(f32[4,32,256]{2,1,0:T(8,128)S(1)} %get-tuple-element.18), channel_id=1, source_target_pairs={{16,0},{32,16},{48,32},{64,48},{80,64},{96,80},{112,96},{128,112},... | collective-permute-start | bytes 393224 | tf_op jit(solution)/shard_map/ppermute | solution.py:279
  150.0 0.6 collective-permute-done.2
  150.6 1.8 %collective-permute-done.3 = f32[4,32,256]{2,1,0:T(8,128)S(1)} collective-permute-done((f32[4,32,256]{2,1,0:T(8,128)S(1)}, f32[4,32,256]{2,1,0:T(8,128)S(1)}, u32[]{:S(2)}, u32[]{:S(2)}) %collective-permute-start.3) | collective-permute-done | bytes 131104 | tf_op jit(solution)/shard_map/ppermute | solution.py:279
  152.4 0.7 copy.18
  153.0 0.7 copy.19
Async XLA Ops:
  0.6 106.6 %copy-start = (f32[1,4,32,256]{3,2,1,0:T(8,128)S(1)}, f32[1,4,32,256]{3,2,1,0:T(8,128)}, u32[]{:S(2)}) copy-start(f32[1,4,32,256]{3,2,1,0:T(8,128)} %param.9) | copy-start | bytes 393220
  0.6 106.6 %copy-start.1 = (f32[1,4,32,256]{3,2,1,0:T(8,128)S(1)}, f32[1,4,32,256]{3,2,1,0:T(8,128)}, u32[]{:S(2)}) copy-start(f32[1,4,32,256]{3,2,1,0:T(8,128)} %param.10) | copy-start | bytes 393220
  101.1 6.1 %collective-permute-start.1 = (f32[200,8,256]{2,1,0:T(8,128)}, f32[200,8,256]{2,1,0:T(8,128)S(1)}, u32[]{:S(2)}, u32[]{:S(2)}) collective-permute-start(f32[200,8,256]{2,1,0:T(8,128)} %get-tuple-element.12), channel_id=1, source_target_pairs={{0,1},{2,3},{4,5},{6,7},{8,9},{10,11},{12,13},{14,15},{1,0},{3,2},... | collective-permute-start | bytes 4915208 | tf_op jit(solution)/shard_map/ppermute | solution.py:268
  101.9 25.8 %collective-permute-start = (f32[200,8,256]{2,1,0:T(8,128)}, f32[200,8,256]{2,1,0:T(8,128)S(1)}, u32[]{:S(2)}, u32[]{:S(2)}) collective-permute-start(f32[200,8,256]{2,1,0:T(8,128)} %get-tuple-element.11), channel_id=1, source_target_pairs={{1,2},{3,4},{5,6},{7,8},{9,10},{11,12},{13,14},{2,1},{4,3},{6,5},{... | collective-permute-start | bytes 4915208 | tf_op jit(solution)/shard_map/ppermute | solution.py:267
  142.6 8.0 %collective-permute-start.2 = (f32[4,32,256]{2,1,0:T(8,128)S(1)}, f32[4,32,256]{2,1,0:T(8,128)S(1)}, u32[]{:S(2)}, u32[]{:S(2)}) collective-permute-start(f32[4,32,256]{2,1,0:T(8,128)S(1)} %get-tuple-element.17), channel_id=1, source_target_pairs={{0,16},{16,32},{32,48},{48,64},{64,80},{80,96},{96,112},{112,128},... | collective-permute-start | bytes 393224 | tf_op jit(solution)/shard_map/ppermute | solution.py:278
  145.8 6.6 %collective-permute-start.3 = (f32[4,32,256]{2,1,0:T(8,128)S(1)}, f32[4,32,256]{2,1,0:T(8,128)S(1)}, u32[]{:S(2)}, u32[]{:S(2)}) collective-permute-start(f32[4,32,256]{2,1,0:T(8,128)S(1)} %get-tuple-element.18), channel_id=1, source_target_pairs={{16,0},{32,16},{48,32},{64,48},{80,64},{96,80},{112,96},{128,112},... | collective-permute-start | bytes 393224 | tf_op jit(solution)/shard_map/ppermute | solution.py:279

commit v3 on v0

v3 whole, which is shorter than its diff:
```python
import functools

import jax
import jax.numpy as jnp
from jax import lax
from jax.experimental import pallas as pl
from jax.experimental.pallas import tpu as pltpu
from jax.sharding import PartitionSpec as P

BETA = 1.5
RHO_ZERO = 0.9
RHO_ONE = 1.0 / (2.0 / 0.9 - 0.9)
COEF_TWO = 2.0 * RHO_ONE / 0.9
ROOT = COEF_TWO**0.5

LANES = 128
SUB = 8
HALVES = 2
DEPTH = HALVES * LANES
HALO = 8
PLANES = 64
ROWS = 32
STEPS = 4
REACH = 10
PART = 16
MIDDLE = PLANES - 2 * PART
PREPARED = 4
PACK_BYTES = 60 * 2**20
WINDOW_BYTES = 50 * 2**20


def rotated_sum(low, high, first_lane, last_lane):
    right_low = pltpu.roll(low, 1, 1)
    right_high = pltpu.roll(high, 1, 1)
    left_low = pltpu.roll(low, LANES - 1, 1)
    left_high = pltpu.roll(high, LANES - 1, 1)
    return (
        jnp.where(first_lane, 0.0, right_low) + jnp.where(last_lane, left_high, left_low),
        jnp.where(first_lane, right_low, right_high) + jnp.where(last_lane, 0.0, left_high),
    )


def place(cell):
    return pl.ds(SUB * (cell // 2), SUB), pl.ds(LANES * (cell % 2), LANES)


def sweep(tiles, rotated, planes, group_planes, field, band, depth, emit, finish=None):
    cells = tiles * HALVES
    others = tiles - rotated
    size = group_planes * others * SUB

    def load(plane, cell):
        return field[(plane, *place(cell % cells))]

    def body(group, _):
        base = group * group_planes
        lane = lax.broadcasted_iota(jnp.int32, (SUB, LANES), 1)
        first_lane = lane == 0
        last_lane = lane == LANES - 1
        block = field[pl.ds(base + 1, group_planes), pl.ds(rotated * SUB, others * SUB), :]
        block = block.reshape(size, DEPTH)
        coarse = block.astype(jnp.bfloat16)
        fine = (block - coarse.astype(jnp.float32)).astype(jnp.bfloat16)
        parts = jnp.concatenate([coarse, fine], axis=0)
        sums = jnp.dot(parts, band[...], preferred_element_type=jnp.float32)
        depth[...] = sums[:size] + sums[size:]
        for tile in range(tiles):
            pair = [2 * tile + half for half in range(HALVES)]
            before = [load(base, cell) for cell in pair]
            here = [load(base + 1, cell) for cell in pair]
            for plane in range(group_planes):
                at = base + plane
                after = [load(at + 2, cell) for cell in pair]
                if tile < rotated:
                    along = rotated_sum(here[0], here[1], first_lane, last_lane)
                else:
                    rows = pl.ds((plane * others + tile - rotated) * SUB, SUB)
                    along = [depth[rows, pl.ds(half * LANES, LANES)] for half in range(HALVES)]
                for half, cell in enumerate(pair):
                    above = load(at + 1, cell - 2)
                    if tile == 0:
                        above = pltpu.roll(above, 1, 0)
                    below = load(at + 1, cell + 2)
                    if tile == tiles - 1:
                        below = pltpu.roll(below, SUB - 1, 0)
                    around = ((before[half] + after[half]) + (above + below)) + along[half]
                    emit(at, cell, here[half], around)
                before, here = here, after
        if finish is not None:
            finish(group)
        return 0

    lax.fori_loop(0, planes // group_planes, body, 0)


def pack_kernel(
    widths, pressure, storage, source, left, right, edge, middle, on_chip,
    edge_hold, middle_hold, on_hold, in_sems, out_sems,
):
    odd = lax.rem(lax.axis_index("dev"), 2)
    off_rows = pl.ds(pl.multiple_of(odd * (ROWS - HALO), SUB), HALO)
    on_rows = pl.ds(pl.multiple_of((1 - odd) * (ROWS - HALO), SUB), HALO)
    fields = (pressure, storage, source)
    everything = [(own, 0, own.shape[0]) for own in (*fields, left, right)]
    ends = [(own, at, PART) for own in fields for at in (0, widths[0] - PART)]
    ends += [(own, 0, STEPS) for own in (left, right)]
    moves = []
    for out, hold, rows, parts in (
        (edge, edge_hold, off_rows, ends),
        (on_chip, on_hold, on_rows, everything),
        (middle, middle_hold, off_rows, [(own, PART, MIDDLE) for own in fields]),
    ):
        at = 0
        for own, start, count in parts:
            index = len(moves)
            into = pl.ds(at, count)
            fetch = pltpu.make_async_copy(
                own.at[pl.ds(start, count), rows, :], hold.at[into], in_sems.at[index]
            )
            fetch.start()
            moves.append((fetch, pltpu.make_async_copy(hold.at[into], out.at[into], out_sems.at[index])))
            at += count
    for fetch, put in moves:
        fetch.wait()
        put.start()
    for fetch, put in moves:
        put.wait()


def window_kernel(kind, tiles, rotated, group_planes, own_rows, widths, *refs):
    refs = iter(refs)

    def take(count):
        return [next(refs) for _ in range(count)]

    fields = take(3)
    sides = take(2)
    halos = take(2 if kind == "outer" else 1)
    with_field, with_traces = kind != "corner", kind != "outer"
    take({"inner": 0, "corner": 2, "outer": 2}[kind])
    field_out = take(1)[0] if with_field else None
    trace_outs = take(2) if with_traces else []
    naturals = take(3)
    side_naturals = take(2)
    out_nat = take(1)[0] if with_field else None
    trace_nats = take(2) if with_traces else []
    u_even, u_odd, change, f, inverse, band, depth, in_sems, out_sems = take(9)

    cells = tiles * HALVES
    planes = 2 * REACH if kind == "corner" else PLANES
    kept_rows = ROWS - HALO if kind == "inner" else HALO
    true_width = widths[0]
    width = planes if kind == "corner" else true_width
    odd = lax.rem(lax.axis_index("dev"), 2)
    at_end = 1 - odd if kind == "inner" else odd
    own_src = pl.ds(pl.multiple_of(at_end * (ROWS - own_rows), SUB), own_rows)
    own_dst = pl.ds(pl.multiple_of((1 - at_end) * HALO, SUB), own_rows)
    halo_dst = pl.ds(pl.multiple_of(at_end * own_rows, SUB), HALO)
    kept_src = pl.ds(HALO, kept_rows)
    kept_dst = pl.ds(pl.multiple_of(at_end * (ROWS - kept_rows), SUB), kept_rows)

    used = 0

    def fetch(src, src_start, src_rows, dst, dst_start, dst_rows, count):
        nonlocal used
        copies = []
        for half in range(HALVES):
            copy = pltpu.make_async_copy(
                src.at[pl.ds(src_start, count), src_rows, pl.ds(half * LANES, LANES)],
                dst.at[pl.ds(dst_start, count), half, dst_rows, :],
                in_sems.at[used],
            )
            copy.start()
            copies.append(copy)
            used += 1
        return copies

    whole = pl.ds(0, HALO)
    chunks = 1 if kind == "corner" else 4
    size = planes // chunks
    waits = [[] for _ in range(chunks)]
    late = []
    for chunk in range(chunks):
        for index, (own, nat) in enumerate(zip(fields, naturals)):
            if kind == "corner":
                waits[0] += fetch(own, 0, own_src, nat, 0, own_dst, REACH)
                waits[0] += fetch(own, true_width - REACH, own_src, nat, REACH, own_dst, REACH)
                at = 2 * index * PART
                waits[0] += fetch(halos[0], at, whole, nat, 0, halo_dst, REACH)
                waits[0] += fetch(halos[0], at + 2 * PART - REACH, whole, nat, REACH, halo_dst, REACH)
            else:
                at = chunk * size
                waits[chunk] += fetch(own, at, own_src, nat, at, own_dst, size)
                if kind == "inner":
                    waits[chunk] += fetch(halos[0], index * planes + at, whole, nat, at, halo_dst, size)
                elif chunk == 0:
                    waits[0] += fetch(halos[0], 2 * index * PART, whole, nat, 0, halo_dst, PART)
                    waits[0] += fetch(halos[1], index * MIDDLE, whole, nat, PART, halo_dst, MIDDLE)
    side_waits = []
    side_at = 3 * (PLANES if kind == "inner" else 2 * PART)
    for index, (own, nat) in enumerate(zip(sides, side_naturals)):
        side_waits += fetch(own, 0, own_src, nat, 0, own_dst, STEPS)
        side_waits += fetch(halos[0], side_at + index * STEPS, whole, nat, 0, halo_dst, STEPS)

    row_at = lax.broadcasted_iota(jnp.int32, (DEPTH, DEPTH), 0)
    column_at = lax.broadcasted_iota(jnp.int32, (DEPTH, DEPTH), 1)
    band[...] = jnp.where(jnp.abs(row_at - column_at) == 1, 1.0, 0.0).astype(jnp.bfloat16)
    for plane in (0, planes + 1):
        for field in (u_even, u_odd, change):
            field[plane] = jnp.zeros((tiles * SUB, DEPTH), jnp.float32)

    def strided(tile):
        return pl.ds(tile, SUB, stride=tiles)

    def own_part(x):
        return 4.0 + jnp.where(x == 0, BETA, 1.0) + jnp.where(x == width - 1, BETA, 1.0)

    def prepare(index, _):
        for plane in range(PREPARED):
            x = index * PREPARED + plane
            for cell in range(cells):
                half, rows = cell % 2, strided(cell // 2)
                first, coef, rate = (nat[x, half, rows, :] for nat in naturals)
                live = jnp.full((SUB, LANES), x, jnp.int32) < width
                u_even[(x + 1, *place(cell))] = jnp.where(live, first, 0.0)
                f[x, cell] = jnp.where(live, rate, 0.0)
                inside = jnp.logical_and(live, coef > 0.0)
                inverse[x, cell] = jnp.where(inside, ROOT / (coef + own_part(x)), 0.0)
        return 0

    for chunk in range(chunks):
        for copy in waits[chunk] + late:
            copy.wait()
        late = []
        if kind == "outer" and chunk == 0:
            for index, nat in enumerate(naturals):
                late += fetch(
                    halos[0], (2 * index + 1) * PART, whole, nat, true_width - PART, halo_dst, PART
                )
        lax.fori_loop(chunk * size // PREPARED, (chunk + 1) * size // PREPARED, prepare, 0)
    for copy in side_waits:
        copy.wait()

    def field_copies(index):
        part = pl.ds(index * group_planes, group_planes)
        return [
            pltpu.make_async_copy(
                out_nat.at[part, half, kept_src, :],
                field_out.at[part, kept_dst, pl.ds(half * LANES, LANES)],
                out_sems.at[4 + 2 * index + half],
            )
            for half in range(HALVES)
        ]

    def put_field(index):
        for copy in field_copies(index):
            copy.start()

    def advance(step, u, u_next):
        for cell in range(cells):
            half, rows = cell % 2, strided(cell // 2)
            for x, side in ((0, side_naturals[0]), (width - 1, side_naturals[1])):
                f[x, cell] = naturals[2][x, half, rows, :] + side[step, half, rows, :]

        def first_half(x, cell, here, around):
            rest = (f[x, cell] - own_part(x) * here) + around
            change[(x + 1, *place(cell))] = rest * inverse[x, cell]

        def second_half(x, cell, here, around):
            value = (u[(x + 1, *place(cell))] + ROOT * here) + around * inverse[x, cell]
            u_next[(x + 1, *place(cell))] = value
            if with_field and u is u_odd:
                out_nat[x, cell % 2, strided(cell // 2), :] = value

        def finish(index):
            if with_field and u is u_odd:
                pl.when(step == STEPS - 1)(lambda: put_field(index))

        sweep(tiles, rotated, planes, group_planes, u, band, depth, first_half)
        sweep(tiles, rotated, planes, group_planes, change, band, depth, second_half, finish)
        if not with_traces:
            return
        for cell in range(cells):
            half, rows = cell % 2, strided(cell // 2)
            for nat, end, inward in ((trace_nats[0], width, width - 1), (trace_nats[1], 1, 2)):
                at_end_plane = u_next[(end, *place(cell))]
                nat[step, half, rows, :] = BETA * at_end_plane + (
                    at_end_plane - u_next[(inward, *place(cell))]
                )

    def two_steps(index, _):
        advance(2 * index, u_even, u_odd)
        advance(2 * index + 1, u_odd, u_even)
        return 0

    lax.fori_loop(0, STEPS // 2, two_steps, 0)

    copies = []
    for nat, out in zip(trace_nats, trace_outs):
        for half in range(HALVES):
            copy = pltpu.make_async_copy(
                nat.at[:, half, kept_src, :],
                out.at[:, kept_dst, pl.ds(half * LANES, LANES)],
                out_sems.at[len(copies)],
            )
            copy.start()
            copies.append(copy)
    if with_field:
        for index in range(planes // group_planes):
            copies += field_copies(index)
    for copy in copies:
        copy.wait()


ANYWHERE = pl.BlockSpec(memory_space=pl.ANY)
IN_HBM = pl.BlockSpec(memory_space=pltpu.HBM)
IN_SMEM = pl.BlockSpec(memory_space=pltpu.SMEM)


def run_window(kind, tiles, rotated, group_planes, args, halos, previous=(), after=()):
    planes = 2 * REACH if kind == "corner" else PLANES
    rows = tiles * SUB
    cells = tiles * HALVES
    natural = pltpu.VMEM((planes, HALVES, rows, LANES), jnp.float32)
    narrow = pltpu.VMEM((STEPS, HALVES, rows, LANES), jnp.float32)
    tiled = pltpu.VMEM((planes, cells, SUB, LANES), jnp.float32)
    padded = pltpu.VMEM((planes + 2, rows, DEPTH), jnp.float32)
    field = jax.ShapeDtypeStruct(args[1].shape, jnp.float32)
    trace = jax.ShapeDtypeStruct(args[4].shape, jnp.float32)
    outs = {"inner": (field, trace, trace), "corner": (trace, trace), "outer": (field,)}[kind]
    return pl.pallas_call(
        functools.partial(window_kernel, kind, tiles, rotated, group_planes, rows - HALO),
        out_shape=outs,
        in_specs=[IN_SMEM] + [IN_HBM] * 5 + [ANYWHERE] * len((*halos, *previous, *after)),
        out_specs=(ANYWHERE,) * len(outs),
        input_output_aliases={6 + len(halos) + i: i for i in range(len(previous))},
        scratch_shapes=[
            *[natural] * 3, *[narrow] * 2,
            *([] if kind == "corner" else [natural]), *([] if kind == "outer" else [narrow] * 2),
            padded, padded, padded, tiled, tiled,
            pltpu.VMEM((DEPTH, DEPTH), jnp.bfloat16),
            pltpu.VMEM((group_planes * (tiles - rotated) * SUB, DEPTH), jnp.float32),
            pltpu.SemaphoreType.DMA((64,)),
            pltpu.SemaphoreType.DMA((4 + HALVES * planes // group_planes,)),
        ],
        compiler_params=pltpu.CompilerParams(vmem_limit_bytes=WINDOW_BYTES),
        cost_estimate=pl.CostEstimate(
            flops=planes * rows * DEPTH * 22 * STEPS,
            bytes_accessed=4 * planes * rows * DEPTH * 4,
            transcendentals=0,
        ),
        name=kind,
    )(*args, *halos, *previous, *after)


def on_device(pressure, storage, source, left_data, right_data, widths):
    args = (widths, pressure, storage, source, left_data[0], right_data[0])
    rims = [
        jax.ShapeDtypeStruct((planes, HALO, DEPTH), jnp.float32)
        for planes in (6 * PART + 2 * STEPS, 3 * MIDDLE, 3 * PLANES + 2 * STEPS)
    ]
    edge, middle, on_chip = pl.pallas_call(
        pack_kernel,
        out_shape=tuple(rims),
        in_specs=[IN_SMEM] + [IN_HBM] * 5,
        out_specs=(ANYWHERE,) * 3,
        scratch_shapes=[
            *[pltpu.VMEM(rim.shape, rim.dtype) for rim in rims],
            pltpu.SemaphoreType.DMA((16,)), pltpu.SemaphoreType.DMA((16,)),
        ],
        compiler_params=pltpu.CompilerParams(vmem_limit_bytes=PACK_BYTES),
        name="pack",
    )(*args)
    count = lax.axis_size("dev")
    chips = [(i, i + 1) for i in range(1, count - 1, 2)]
    chips += [(j, i) for i, j in chips]
    cores = [(i, i + 1) for i in range(0, count, 2)]
    cores += [(j, i) for i, j in cores]
    edge = lax.ppermute(edge, "dev", chips)
    on_chip = lax.ppermute(on_chip, "dev", cores)
    middle = lax.ppermute(middle, "dev", chips)

    field, trace_high, trace_low = run_window("inner", 5, 2, 16, args, (on_chip,))
    trace_high, trace_low = run_window("corner", 3, 1, 10, args, (edge,), (trace_high, trace_low))

    subs = lax.axis_size("sub")
    up = [(i, i + 1) for i in range(subs - 1)]
    down = [(i + 1, i) for i in range(subs - 1)]
    new_left = lax.ppermute(trace_high, "sub", up)
    new_right = lax.ppermute(trace_low, "sub", down)
    (field,) = run_window("outer", 3, 1, 16, args, (edge, middle), (field,), (trace_low,))
    return (field, new_left[None], new_right[None])


def solution(mesh):
    in_specs = (
        P("sub", "dev", None),
        P("sub", "dev", None),
        P("sub", "dev", None),
        P("sub", None, "dev", None),
        P("sub", None, "dev", None),
        P("sub"),
    )
    out_specs = (P("sub", "dev", None), P("sub", None, "dev", None), P("sub", None, "dev", None))
    return jax.shard_map(
        on_device, mesh=mesh, in_specs=in_specs, out_specs=out_specs, check_vma=False
    )
```

time: 159 us -> 53.6 us (0.34)
  other arithmetic: 70.5 us -> 0 us
  waiting for transfers between devices: 35.9 us -> 0.01 us
  Pallas kernels: 0 us -> 35.5 us
  starting transfers between devices: 45.5 us -> 15 us
  local copies, waits for them, and re-layouts: 3.45 us -> 1.33 us
    add x13 -> x0, other arithmetic: 41.7 us -> none  [the longest x4 21.1 us: on_device(): first_iter = field + dir_zero]
    ppermute x18 -> x5, waiting for transfers between devices: 35.9 us -> 0.01 us  [the longest x1 0.01 us: on_device(): edge = lax.ppermute(edge, 'dev', chips)]
    pallas_call x0 -> x4, Pallas kernels: none -> 35.5 us  [the longest x3 32.2 us: run_window(): pl.pallas_call(functools.partial(window_kernel, kind, tiles, rotated, gro...]
    ppermute x18 -> x5, starting transfers between devices: 45.5 us -> 15 us  [the longest x1 4.65 us: on_device(): edge = lax.ppermute(edge, 'dev', chips)]
    concatenate x8 -> x0, other arithmetic: 26.9 us -> none  [padded_2(): block = jnp.concatenate([low, block, high], axis=dim)]
    mul x1 -> x0, other arithmetic: 1.83 us -> none  [on_device(): field = pressure * live]
  transfers between devices with their start and end apart: 18 -> 5, of which waited for: 10 -> 0; matrix products, arithmetic and copies ran while one was open for 1% -> 0% of each run, Pallas kernels for 0% -> 60%
where the time goes in v3:
time: 53.6 us; the launch traced here: 53.3 us
  Pallas kernels  35.5 us (66%)
  starting transfers between devices  15 us (28%)
  between operations  1.43 us (3%)
  local copies, waits for them, and re-layouts  1.33 us (2%)
    pallas_call x3, Pallas kernels, run_window(): pl.pallas_call(functools.partial(window_kernel, kind, tiles, rotated, gro...  32.2 us
    ppermute x1, starting transfers between devices, on_device(): edge = lax.ppermute(edge, 'dev', chips)  4.65 us
    ppermute x1, starting transfers between devices, on_device(): new_right = lax.ppermute(trace_low, 'sub', down)  4.19 us
    pallas_call x1, Pallas kernels, on_device(): pl.pallas_call(pack_kernel, out_shape=tuple(rims), in_specs=[IN_SMEM] + [...  3.33 us
    ppermute x1, starting transfers between devices, on_device(): new_left = lax.ppermute(trace_high, 'sub', up)  3.21 us
    ppermute x1, starting transfers between devices, on_device(): middle = lax.ppermute(middle, 'dev', chips)  2.24 us
    unnamed x8, local copies, waits for them, and re-layouts  1.33 us
  transfers between devices with their start and end apart: 5, of which 0 were waited for; matrix products, arithmetic and copies ran while one was open for 0% of the time, Pallas kernels for 60%

profile of v3, /device:TPU:101, one launch (start us, length us, event | category | flops | bytes accessed | tf_op | source)
XLA Modules:
  0.0 53.3 jit_solution(13139908432118209767)
XLA Ops:
  1.3 0.0 copy-start.1
  1.3 0.0 copy-start.2
  1.3 3.3 %pack.1 = (f32[104,8,256]{2,1,0:T(8,128)}, f32[96,8,256]{2,1,0:T(8,128)}, f32[200,8,256]{2,1,0:T(8,128)}) custom-call(s32[1]{0:T(128)S(6)} %copy.17.widths, f32[64,32,256]{2,1,0:T(8,128)} %refs_0_.5, f32[64,32,256]{2,1,0:T(8,128)} %refs_1_.5, f32[64,32,256]{2,1,0:T(8,128)} %refs_2_.5, f32[4,32,256]{2,1,0:T(8,128)} %bitcast.4, f32[4,32,256]{2,1,0:T(8,128)} %bitcast.8), custom_call_target="tpu_custom_call" | custom-call | tf_op jit(solution)/shard_map/pack/pallas_call | solution.py:362
  4.6 0.8 %collective-permute-start.2 = (f32[200,8,256]{2,1,0:T(8,128)}, f32[200,8,256]{2,1,0:T(8,128)S(1)}, u32[]{:S(2)}, u32[]{:S(2)}) collective-permute-start(f32[200,8,256]{2,1,0:T(8,128)} %get-tuple-element.13), channel_id=1, source_target_pairs={{0,1},{2,3},{4,5},{6,7},{8,9},{10,11},{12,13},{14,15},{1,0},{3,2},... | collective-permute-start | bytes 4915208 | tf_op jit(solution)/shard_map/ppermute | solution.py:380
  5.4 4.7 %collective-permute-start = (f32[104,8,256]{2,1,0:T(8,128)}, f32[104,8,256]{2,1,0:T(8,128)S(1)}, u32[]{:S(2)}, u32[]{:S(2)}) collective-permute-start(f32[104,8,256]{2,1,0:T(8,128)} %get-tuple-element.11), channel_id=1, source_target_pairs={{1,2},{3,4},{5,6},{7,8},{9,10},{11,12},{13,14},{2,1},{4,3},{6,5},{... | collective-permute-start | bytes 2555912 | tf_op jit(solution)/shard_map/ppermute | solution.py:379
  10.1 0.0 copy-start
  10.1 2.2 %collective-permute-start.1 = (f32[96,8,256]{2,1,0:T(8,128)}, f32[96,8,256]{2,1,0:T(8,128)S(1)}, u32[]{:S(2)}, u32[]{:S(2)}) collective-permute-start(f32[96,8,256]{2,1,0:T(8,128)} %get-tuple-element.12), channel_id=1, source_target_pairs={{1,2},{3,4},{5,6},{7,8},{9,10},{11,12},{13,14},{2,1},{4,3},{6,5},{... | collective-permute-start | bytes 2359304 | tf_op jit(solution)/shard_map/ppermute | solution.py:381
  12.3 0.0 collective-permute-done.2.refs_5_
  12.3 0.0 copy-done.1
  12.3 0.0 copy-done.2
  12.3 15.4 %inner.1 = (f32[64,32,256]{2,1,0:T(8,128)}, f32[4,32,256]{2,1,0:T(8,128)S(1)}, f32[4,32,256]{2,1,0:T(8,128)S(1)}) custom-call(s32[1]{0:T(128)S(6)} %copy.17.widths, f32[64,32,256]{2,1,0:T(8,128)} %refs_0_.5, f32[64,32,256]{2,1,0:T(8,128)} %refs_1_.5, f32[64,32,256]{2,1,0:T(8,128)} %refs_2_.5, f32[4,32,256]{2,1,0:T(8,128)S(1)} %bitcast.5, ...), custom_call_target="tpu_custom_call" | custom-call | flops 57671680 | bytes 10485760 | tf_op jit(solution)/shard_map/inner/pallas_call | solution.py:331
  27.8 0.0 collective-permute-done.refs_5_
  27.8 0.0 copy-done
  27.8 5.6 %corner.1 = (f32[4,32,256]{2,1,0:T(8,128)S(1)}, f32[4,32,256]{2,1,0:T(8,128)S(1)}) custom-call(s32[1]{0:T(128)S(6)} %copy.17.widths, f32[64,32,256]{2,1,0:T(8,128)S(1)} %copy-done, f32[64,32,256]{2,1,0:T(8,128)} %refs_1_.5, f32[64,32,256]{2,1,0:T(8,128)} %refs_2_.5, f32[4,32,256]{2,1,0:T(8,128)S(1)} %bitcast.6, ...), custom_call_target="tpu_custom_call", output_to_operand_aliasing={{0}: (7, {}), {1}: (8, {})} | custom-call | flops 10813440 | bytes 1966080 | tf_op jit(solution)/shard_map/corner/pallas_call | solution.py:331
  33.3 3.2 %collective-permute-start.3 = (f32[4,32,256]{2,1,0:T(8,128)S(1)}, f32[4,32,256]{2,1,0:T(8,128)S(1)}, u32[]{:S(2)}, u32[]{:S(2)}) collective-permute-start(f32[4,32,256]{2,1,0:T(8,128)S(1)} %get-tuple-element.18), channel_id=1, source_target_pairs={{0,16},{16,32},{32,48},{48,64},{64,80},{80,96},{96,112},{112,128},... | collective-permute-start | bytes 393224 | tf_op jit(solution)/shard_map/ppermute | solution.py:389
  36.6 4.2 %collective-permute-start.4 = (f32[4,32,256]{2,1,0:T(8,128)S(1)}, f32[4,32,256]{2,1,0:T(8,128)S(1)}, u32[]{:S(2)}, u32[]{:S(2)}) collective-permute-start(f32[4,32,256]{2,1,0:T(8,128)S(1)} %get-tuple-element.17.refs_8_), channel_id=1, source_target_pairs={{16,0},{32,16},{48,32},{64,48},{80,64},{96,80},{112,96},{128,112},... | collective-permute-start | bytes 393224 | tf_op jit(solution)/shard_map/ppermute | solution.py:390
  40.8 0.0 collective-permute-done.1.refs_6_
  40.8 11.2 %outer.1 = f32[64,32,256]{2,1,0:T(8,128)} custom-call(s32[1]{0:T(128)S(6)} %copy.17.widths, f32[64,32,256]{2,1,0:T(8,128)S(1)} %copy-done, f32[64,32,256]{2,1,0:T(8,128)} %refs_1_.5, f32[64,32,256]{2,1,0:T(8,128)} %refs_2_.5, f32[4,32,256]{2,1,0:T(8,128)S(1)} %bitcast.7, f32[4,32,256]{2,1,0:T(8,128)S(1)} %bitcast.11, ...), custom_call_target="tpu_custom_call", output_to_operand_aliasing={{}: (8, {})} | custom-call | flops 34603008 | bytes 6291456 | tf_op jit(solution)/shard_map/outer/pallas_call | solution.py:331
  52.0 0.0 collective-permute-done.3
  52.0 0.0 collective-permute-done.4
  52.0 0.7 %copy.18 = f32[1,4,32,256]{3,2,1,0:T(8,128)} copy(f32[1,4,32,256]{3,2,1,0:T(8,128)S(1)} %bitcast.12) | data formatting | bytes 262144
  52.7 0.7 %copy.19 = f32[1,4,32,256]{3,2,1,0:T(8,128)} copy(f32[1,4,32,256]{3,2,1,0:T(8,128)S(1)} %bitcast.13) | data formatting | bytes 262144
Async XLA Ops:
  1.3 11.1 %copy-start.1 = (f32[1,4,32,256]{3,2,1,0:T(8,128)S(1)}, f32[1,4,32,256]{3,2,1,0:T(8,128)}, u32[]{:S(2)}) copy-start(f32[1,4,32,256]{3,2,1,0:T(8,128)} %param.9) | copy-start | bytes 393220
  1.3 11.1 %copy-start.2 = (f32[1,4,32,256]{3,2,1,0:T(8,128)S(1)}, f32[1,4,32,256]{3,2,1,0:T(8,128)}, u32[]{:S(2)}) copy-start(f32[1,4,32,256]{3,2,1,0:T(8,128)} %param.10) | copy-start | bytes 393220
  4.6 7.7 %collective-permute-start.2 = (f32[200,8,256]{2,1,0:T(8,128)}, f32[200,8,256]{2,1,0:T(8,128)S(1)}, u32[]{:S(2)}, u32[]{:S(2)}) collective-permute-start(f32[200,8,256]{2,1,0:T(8,128)} %get-tuple-element.13), channel_id=1, source_target_pairs={{0,1},{2,3},{4,5},{6,7},{8,9},{10,11},{12,13},{14,15},{1,0},{3,2},... | collective-permute-start | bytes 4915208 | tf_op jit(solution)/shard_map/ppermute | solution.py:380
  5.4 22.4 %collective-permute-start = (f32[104,8,256]{2,1,0:T(8,128)}, f32[104,8,256]{2,1,0:T(8,128)S(1)}, u32[]{:S(2)}, u32[]{:S(2)}) collective-permute-start(f32[104,8,256]{2,1,0:T(8,128)} %get-tuple-element.11), channel_id=1, source_target_pairs={{1,2},{3,4},{5,6},{7,8},{9,10},{11,12},{13,14},{2,1},{4,3},{6,5},{... | collective-permute-start | bytes 2555912 | tf_op jit(solution)/shard_map/ppermute | solution.py:379
  10.1 17.7 %copy-start = (f32[64,32,256]{2,1,0:T(8,128)S(1)}, f32[64,32,256]{2,1,0:T(8,128)}, u32[]{:S(2)}) copy-start(f32[64,32,256]{2,1,0:T(8,128)} %refs_0_.5) | copy-start | bytes 6291460
  10.1 30.7 %collective-permute-start.1 = (f32[96,8,256]{2,1,0:T(8,128)}, f32[96,8,256]{2,1,0:T(8,128)S(1)}, u32[]{:S(2)}, u32[]{:S(2)}) collective-permute-start(f32[96,8,256]{2,1,0:T(8,128)} %get-tuple-element.12), channel_id=1, source_target_pairs={{1,2},{3,4},{5,6},{7,8},{9,10},{11,12},{13,14},{2,1},{4,3},{6,5},{... | collective-permute-start | bytes 2359304 | tf_op jit(solution)/shard_map/ppermute | solution.py:381
  33.3 18.6 %collective-permute-start.3 = (f32[4,32,256]{2,1,0:T(8,128)S(1)}, f32[4,32,256]{2,1,0:T(8,128)S(1)}, u32[]{:S(2)}, u32[]{:S(2)}) collective-permute-start(f32[4,32,256]{2,1,0:T(8,128)S(1)} %get-tuple-element.18), channel_id=1, source_target_pairs={{0,16},{16,32},{32,48},{48,64},{64,80},{80,96},{96,112},{112,128},... | collective-permute-start | bytes 393224 | tf_op jit(solution)/shard_map/ppermute | solution.py:389
  36.6 15.4 %collective-permute-start.4 = (f32[4,32,256]{2,1,0:T(8,128)S(1)}, f32[4,32,256]{2,1,0:T(8,128)S(1)}, u32[]{:S(2)}, u32[]{:S(2)}) collective-permute-start(f32[4,32,256]{2,1,0:T(8,128)S(1)} %get-tuple-element.17.refs_8_), channel_id=1, source_target_pairs={{16,0},{32,16},{48,32},{64,48},{80,64},{96,80},{112,96},{128,112},... | collective-permute-start | bytes 393224 | tf_op jit(solution)/shard_map/ppermute | solution.py:390

commit v4 on v3

--- a/solution.py
+++ b/solution.py
@@ -25,8 +25,9 @@
 PART = 16
 MIDDLE = PLANES - 2 * PART
 PREPARED = 4
-PACK_BYTES = 60 * 2**20
+PACK_BYTES = 50 * 2**20
 WINDOW_BYTES = 50 * 2**20
+OUTER_BYTES = 50 * 2**20
 
 
 def rotated_sum(low, high, first_lane, last_lane):
@@ -44,7 +45,7 @@
     return pl.ds(SUB * (cell // 2), SUB), pl.ds(LANES * (cell % 2), LANES)
 
 
-def sweep(tiles, rotated, planes, group_planes, field, band, depth, emit, finish=None):
+def sweep(tiles, rotated, planes, group_planes, field, band, depths, emit, finish=None):
     cells = tiles * HALVES
     others = tiles - rotated
     size = group_planes * others * SUB
@@ -52,18 +53,20 @@
     def load(plane, cell):
         return field[(plane, *place(cell % cells))]
 
-    def body(group, _):
-        base = group * group_planes
-        lane = lax.broadcasted_iota(jnp.int32, (SUB, LANES), 1)
-        first_lane = lane == 0
-        last_lane = lane == LANES - 1
-        block = field[pl.ds(base + 1, group_planes), pl.ds(rotated * SUB, others * SUB), :]
+    def multiply(group, out):
+        block = field[pl.ds(group * group_planes + 1, group_planes), pl.ds(rotated * SUB, others * SUB), :]
         block = block.reshape(size, DEPTH)
         coarse = block.astype(jnp.bfloat16)
         fine = (block - coarse.astype(jnp.float32)).astype(jnp.bfloat16)
         parts = jnp.concatenate([coarse, fine], axis=0)
         sums = jnp.dot(parts, band[...], preferred_element_type=jnp.float32)
-        depth[...] = sums[:size] + sums[size:]
+        out[...] = sums[:size] + sums[size:]
+
+    def work(group, depth):
+        base = group * group_planes
+        lane = lax.broadcasted_iota(jnp.int32, (SUB, LANES), 1)
+        first_lane = lane == 0
+        last_lane = lane == LANES - 1
         for tile in range(tiles):
             pair = [2 * tile + half for half in range(HALVES)]
             before = [load(base, cell) for cell in pair]
@@ -86,45 +89,48 @@
                     around = ((before[half] + after[half]) + (above + below)) + along[half]
                     emit(at, cell, here[half], around)
                 before, here = here, after
+
+    groups = planes // group_planes
+    multiply(0, depths[0])
+
+    def body(index, _):
+        for side in range(2):
+            group = 2 * index + side
+            multiply(jnp.minimum(group + 1, groups - 1), depths[1 - side])
+            work(group, depths[side])
         if finish is not None:
-            finish(group)
+            finish(index)
         return 0
 
-    lax.fori_loop(0, planes // group_planes, body, 0)
+    lax.fori_loop(0, groups // 2, body, 0)
 
 
 def pack_kernel(
-    widths, pressure, storage, source, left, right, edge, middle, on_chip,
-    edge_hold, middle_hold, on_hold, in_sems, out_sems,
+    widths, pressure, storage, source, sides, edge, middle, on_chip, sems,
 ):
     odd = lax.rem(lax.axis_index("dev"), 2)
     off_rows = pl.ds(pl.multiple_of(odd * (ROWS - HALO), SUB), HALO)
     on_rows = pl.ds(pl.multiple_of((1 - odd) * (ROWS - HALO), SUB), HALO)
     fields = (pressure, storage, source)
-    everything = [(own, 0, own.shape[0]) for own in (*fields, left, right)]
+    everything = [(own, 0, own.shape[0]) for own in (*fields, sides)]
     ends = [(own, at, PART) for own in fields for at in (0, widths[0] - PART)]
-    ends += [(own, 0, STEPS) for own in (left, right)]
+    ends.append((sides, 0, 2 * STEPS))
     moves = []
-    for out, hold, rows, parts in (
-        (edge, edge_hold, off_rows, ends),
-        (on_chip, on_hold, on_rows, everything),
-        (middle, middle_hold, off_rows, [(own, PART, MIDDLE) for own in fields]),
+    for out, rows, parts in (
+        (edge, off_rows, ends),
+        (on_chip, on_rows, everything),
+        (middle, off_rows, [(own, PART, MIDDLE) for own in fields]),
     ):
         at = 0
         for own, start, count in parts:
-            index = len(moves)
-            into = pl.ds(at, count)
-            fetch = pltpu.make_async_copy(
-                own.at[pl.ds(start, count), rows, :], hold.at[into], in_sems.at[index]
+            move = pltpu.make_async_copy(
+                own.at[pl.ds(start, count), rows, :], out.at[pl.ds(at, count)], sems.at[len(moves)]
             )
-            fetch.start()
-            moves.append((fetch, pltpu.make_async_copy(hold.at[into], out.at[into], out_sems.at[index])))
+            move.start()
+            moves.append(move)
             at += count
-    for fetch, put in moves:
-        fetch.wait()
-        put.start()
-    for fetch, put in moves:
-        put.wait()
+    for move in moves:
+        move.wait()
 
 
 def window_kernel(kind, tiles, rotated, group_planes, own_rows, widths, *refs):
@@ -134,7 +140,7 @@
         return [next(refs) for _ in range(count)]
 
     fields = take(3)
-    sides = take(2)
+    sides = take(1)[0]
     halos = take(2 if kind == "outer" else 1)
     with_field, with_traces = kind != "corner", kind != "outer"
     take({"inner": 0, "corner": 2, "outer": 2}[kind])
@@ -144,7 +150,8 @@
     side_naturals = take(2)
     out_nat = take(1)[0] if with_field else None
     trace_nats = take(2) if with_traces else []
-    u_even, u_odd, change, f, inverse, band, depth, in_sems, out_sems = take(9)
+    u_even, u_odd, change, f, inverse, band, depth_a, depth_b, in_sems, out_sems = take(10)
+    depths = (depth_a, depth_b)
 
     cells = tiles * HALVES
     planes = 2 * REACH if kind == "corner" else PLANES
@@ -176,7 +183,7 @@
         return copies
 
     whole = pl.ds(0, HALO)
-    chunks = 1 if kind == "corner" else 4
+    chunks = 1 if kind == "corner" else 2
     size = planes // chunks
     waits = [[] for _ in range(chunks)]
     late = []
@@ -198,8 +205,8 @@
                     waits[0] += fetch(halos[1], index * MIDDLE, whole, nat, PART, halo_dst, MIDDLE)
     side_waits = []
     side_at = 3 * (PLANES if kind == "inner" else 2 * PART)
-    for index, (own, nat) in enumerate(zip(sides, side_naturals)):
-        side_waits += fetch(own, 0, own_src, nat, 0, own_dst, STEPS)
+    for index, nat in enumerate(side_naturals):
+        side_waits += fetch(sides, index * STEPS, own_src, nat, 0, own_dst, STEPS)
         side_waits += fetch(halos[0], side_at + index * STEPS, whole, nat, 0, halo_dst, STEPS)
 
     row_at = lax.broadcasted_iota(jnp.int32, (DEPTH, DEPTH), 0)
@@ -242,7 +249,7 @@
         copy.wait()
 
     def field_copies(index):
-        part = pl.ds(index * group_planes, group_planes)
+        part = pl.ds(2 * index * group_planes, 2 * group_planes)
         return [
             pltpu.make_async_copy(
                 out_nat.at[part, half, kept_src, :],
@@ -276,8 +283,8 @@
             if with_field and u is u_odd:
                 pl.when(step == STEPS - 1)(lambda: put_field(index))
 
-        sweep(tiles, rotated, planes, group_planes, u, band, depth, first_half)
-        sweep(tiles, rotated, planes, group_planes, change, band, depth, second_half, finish)
+        sweep(tiles, rotated, planes, group_planes, u, band, depths, first_half)
+        sweep(tiles, rotated, planes, group_planes, change, band, depths, second_half, finish)
         if not with_traces:
             return
         for cell in range(cells):
@@ -306,7 +313,7 @@
             copy.start()
             copies.append(copy)
     if with_field:
-        for index in range(planes // group_planes):
+        for index in range(planes // group_planes // 2):
             copies += field_copies(index)
     for copy in copies:
         copy.wait()
@@ -317,7 +324,7 @@
 IN_SMEM = pl.BlockSpec(memory_space=pltpu.SMEM)
 
 
-def run_window(kind, tiles, rotated, group_planes, args, halos, previous=(), after=()):
+def run_window(kind, tiles, rotated, group_planes, limit, args, halos, previous=(), after=()):
     planes = 2 * REACH if kind == "corner" else PLANES
     rows = tiles * SUB
     cells = tiles * HALVES
@@ -326,24 +333,24 @@
     tiled = pltpu.VMEM((planes, cells, SUB, LANES), jnp.float32)
     padded = pltpu.VMEM((planes + 2, rows, DEPTH), jnp.float32)
     field = jax.ShapeDtypeStruct(args[1].shape, jnp.float32)
-    trace = jax.ShapeDtypeStruct(args[4].shape, jnp.float32)
+    trace = jax.ShapeDtypeStruct((STEPS, ROWS, DEPTH), jnp.float32)
     outs = {"inner": (field, trace, trace), "corner": (trace, trace), "outer": (field,)}[kind]
     return pl.pallas_call(
         functools.partial(window_kernel, kind, tiles, rotated, group_planes, rows - HALO),
         out_shape=outs,
-        in_specs=[IN_SMEM] + [IN_HBM] * 5 + [ANYWHERE] * len((*halos, *previous, *after)),
+        in_specs=[IN_SMEM] + [IN_HBM] * 3 + [ANYWHERE] * len((args[4], *halos, *previous, *after)),
         out_specs=(ANYWHERE,) * len(outs),
-        input_output_aliases={6 + len(halos) + i: i for i in range(len(previous))},
+        input_output_aliases={5 + len(halos) + i: i for i in range(len(previous))},
         scratch_shapes=[
             *[natural] * 3, *[narrow] * 2,
             *([] if kind == "corner" else [natural]), *([] if kind == "outer" else [narrow] * 2),
             padded, padded, padded, tiled, tiled,
             pltpu.VMEM((DEPTH, DEPTH), jnp.bfloat16),
-            pltpu.VMEM((group_planes * (tiles - rotated) * SUB, DEPTH), jnp.float32),
+            *[pltpu.VMEM((group_planes * (tiles - rotated) * SUB, DEPTH), jnp.float32)] * 2,
             pltpu.SemaphoreType.DMA((64,)),
-            pltpu.SemaphoreType.DMA((4 + HALVES * planes // group_planes,)),
+            pltpu.SemaphoreType.DMA((4 + planes // group_planes,)),
         ],
-        compiler_params=pltpu.CompilerParams(vmem_limit_bytes=WINDOW_BYTES),
+        compiler_params=pltpu.CompilerParams(vmem_limit_bytes=limit),
         cost_estimate=pl.CostEstimate(
             flops=planes * rows * DEPTH * 22 * STEPS,
             bytes_accessed=4 * planes * rows * DEPTH * 4,
@@ -354,7 +361,8 @@
 
 
 def on_device(pressure, storage, source, left_data, right_data, widths):
-    args = (widths, pressure, storage, source, left_data[0], right_data[0])
+    sides = jnp.concatenate([left_data[0], right_data[0]])
+    args = (widths, pressure, storage, source, sides)
     rims = [
         jax.ShapeDtypeStruct((planes, HALO, DEPTH), jnp.float32)
         for planes in (6 * PART + 2 * STEPS, 3 * MIDDLE, 3 * PLANES + 2 * STEPS)
@@ -362,12 +370,9 @@
     edge, middle, on_chip = pl.pallas_call(
         pack_kernel,
         out_shape=tuple(rims),
-        in_specs=[IN_SMEM] + [IN_HBM] * 5,
+        in_specs=[IN_SMEM] + [IN_HBM] * 3 + [ANYWHERE],
         out_specs=(ANYWHERE,) * 3,
-        scratch_shapes=[
-            *[pltpu.VMEM(rim.shape, rim.dtype) for rim in rims],
-            pltpu.SemaphoreType.DMA((16,)), pltpu.SemaphoreType.DMA((16,)),
-        ],
+        scratch_shapes=[pltpu.SemaphoreType.DMA((16,))],
         compiler_params=pltpu.CompilerParams(vmem_limit_bytes=PACK_BYTES),
         name="pack",
     )(*args)
@@ -380,15 +385,15 @@
     on_chip = lax.ppermute(on_chip, "dev", cores)
     middle = lax.ppermute(middle, "dev", chips)
 
-    field, trace_high, trace_low = run_window("inner", 5, 2, 16, args, (on_chip,))
-    trace_high, trace_low = run_window("corner", 3, 1, 10, args, (edge,), (trace_high, trace_low))
+    field, trace_high, trace_low = run_window("inner", 5, 2, 8, WINDOW_BYTES, args, (on_chip,))
+    trace_high, trace_low = run_window("corner", 3, 1, 5, WINDOW_BYTES, args, (edge,), (trace_high, trace_low))
 
     subs = lax.axis_size("sub")
     up = [(i, i + 1) for i in range(subs - 1)]
     down = [(i + 1, i) for i in range(subs - 1)]
     new_left = lax.ppermute(trace_high, "sub", up)
     new_right = lax.ppermute(trace_low, "sub", down)
-    (field,) = run_window("outer", 3, 1, 16, args, (edge, middle), (field,), (trace_low,))
+    (field,) = run_window("outer", 3, 1, 8, OUTER_BYTES, args, (edge, middle), (field,), (trace_low,))
     return (field, new_left[None], new_right[None])
 
 

time: 53.6 us -> 58.3 us (1.088)
  Pallas kernels: 35.5 us -> 39.2 us
  other arithmetic: 0 us -> 0.99 us
    pallas_call x3, Pallas kernels: 32.2 us -> 37.1 us  [run_window(): pl.pallas_call(functools.partial(window_kernel, kind, tiles, rotated, gro...]
    pallas_call x1, Pallas kernels: 3.33 us -> 2.11 us  [on_device(): pl.pallas_call(pack_kernel, out_shape=tuple(rims), in_specs=[IN_SMEM] + [...]
    concatenate x0 -> x1, other arithmetic: none -> 0.99 us  [on_device(): sides = jnp.concatenate([left_data[0], right_data[0]])]
    unnamed x8 -> x4, local copies, waits for them, and re-layouts: 1.33 us -> 1.32 us
  transfers between devices with their start and end apart: 5 -> 5, of which waited for: 0 -> 0; matrix products, arithmetic and copies ran while one was open for 0% -> 0% of each run, Pallas kernels for 60% -> 64%
where the time goes in v4:
time: 58.3 us; the launch traced here: 58 us
  Pallas kernels  39.2 us (67%)
  starting transfers between devices  15 us (26%)
  between operations  1.4 us (2%)
  local copies, waits for them, and re-layouts  1.32 us (2%)
  other arithmetic  0.99 us (2%)
    pallas_call x3, Pallas kernels, run_window(): pl.pallas_call(functools.partial(window_kernel, kind, tiles, rotated, gro...  37.1 us
    ppermute x1, starting transfers between devices, on_device(): edge = lax.ppermute(edge, 'dev', chips)  4.66 us
    ppermute x1, starting transfers between devices, on_device(): new_right = lax.ppermute(trace_low, 'sub', down)  4.17 us
    ppermute x1, starting transfers between devices, on_device(): new_left = lax.ppermute(trace_high, 'sub', up)  3.23 us
    ppermute x1, starting transfers between devices, on_device(): middle = lax.ppermute(middle, 'dev', chips)  2.24 us
    pallas_call x1, Pallas kernels, on_device(): pl.pallas_call(pack_kernel, out_shape=tuple(rims), in_specs=[IN_SMEM] + [...  2.11 us
    unnamed x4, local copies, waits for them, and re-layouts  1.32 us
  transfers between devices with their start and end apart: 5, of which 0 were waited for; matrix products, arithmetic and copies ran while one was open for 0% of the time, Pallas kernels for 64%

profile of v4, /device:TPU:101, one launch (start us, length us, event | category | flops | bytes accessed | tf_op | source)
XLA Modules:
  0.0 58.0 jit_solution(16390096337029156750)
XLA Ops:
  1.3 1.0 %pad_maximum_fusion.sides.refs_3_ = f32[8,32,256]{2,1,0:T(8,128)S(1)} fusion(f32[4,32,256]{2,1,0:T(8,128)} %bitcast.6, f32[4,32,256]{2,1,0:T(8,128)} %bitcast.7), kind=kLoop, calls=%fused_computation | loop fusion | flops 65536 | bytes 524288 | tf_op jit(solution)/shard_map/concatenate | solution.py:364
  2.3 2.1 %pack.1 = (f32[104,8,256]{2,1,0:T(8,128)S(1)}, f32[96,8,256]{2,1,0:T(8,128)S(1)}, f32[200,8,256]{2,1,0:T(8,128)S(1)}) custom-call(s32[1]{0:T(128)S(6)} %copy.17.widths, f32[64,32,256]{2,1,0:T(8,128)} %refs_0_.5, f32[64,32,256]{2,1,0:T(8,128)} %refs_1_.5, f32[64,32,256]{2,1,0:T(8,128)} %refs_2_.5, f32[8,32,256]{2,1,0:T(8,128)S(1)} %pad_maximum_fusion.sides.refs_3_), custom_call_target="tpu_custom_call" | custom-call | tf_op jit(solution)/shard_map/pack/pallas_call | solution.py:370
  4.4 0.8 %collective-permute-start.2 = (f32[200,8,256]{2,1,0:T(8,128)S(1)}, f32[200,8,256]{2,1,0:T(8,128)S(1)}, u32[]{:S(2)}, u32[]{:S(2)}) collective-permute-start(f32[200,8,256]{2,1,0:T(8,128)S(1)} %get-tuple-element.13), channel_id=1, source_target_pairs={{0,1},{2,3},{4,5},{6,7},{8,9},{10,11},{12,13},{14,15},{1,0},{3,2},... | collective-permute-start | bytes 4915208 | tf_op jit(solution)/shard_map/ppermute | solution.py:385
  5.1 4.7 %collective-permute-start = (f32[104,8,256]{2,1,0:T(8,128)S(1)}, f32[104,8,256]{2,1,0:T(8,128)S(1)}, u32[]{:S(2)}, u32[]{:S(2)}) collective-permute-start(f32[104,8,256]{2,1,0:T(8,128)S(1)} %get-tuple-element.11), channel_id=1, source_target_pairs={{1,2},{3,4},{5,6},{7,8},{9,10},{11,12},{13,14},{2,1},{4,3},{6,5},{... | collective-permute-start | bytes 2555912 | tf_op jit(solution)/shard_map/ppermute | solution.py:384
  9.8 0.0 copy-start
  9.8 2.2 %collective-permute-start.1 = (f32[96,8,256]{2,1,0:T(8,128)S(1)}, f32[96,8,256]{2,1,0:T(8,128)S(1)}, u32[]{:S(2)}, u32[]{:S(2)}) collective-permute-start(f32[96,8,256]{2,1,0:T(8,128)S(1)} %get-tuple-element.12), channel_id=1, source_target_pairs={{1,2},{3,4},{5,6},{7,8},{9,10},{11,12},{13,14},{2,1},{4,3},{6,5},{... | collective-permute-start | bytes 2359304 | tf_op jit(solution)/shard_map/ppermute | solution.py:386
  12.1 0.0 collective-permute-done.2.refs_4_
  12.1 17.5 %inner.1 = (f32[64,32,256]{2,1,0:T(8,128)}, f32[4,32,256]{2,1,0:T(8,128)S(1)}, f32[4,32,256]{2,1,0:T(8,128)S(1)}) custom-call(s32[1]{0:T(128)S(6)} %copy.17.widths, f32[64,32,256]{2,1,0:T(8,128)} %refs_0_.5, f32[64,32,256]{2,1,0:T(8,128)} %refs_1_.5, f32[64,32,256]{2,1,0:T(8,128)} %refs_2_.5, f32[8,32,256]{2,1,0:T(8,128)S(1)} %pad_maximum_fusion.sides.refs_3_, ...), custom_call_target="tpu_custom_call" | custom-call | flops 57671680 | bytes 10485760 | tf_op jit(solution)/shard_map/inner/pallas_call | solution.py:338
  29.6 0.0 collective-permute-done.refs_4_
  29.6 0.0 copy-done
  29.6 6.9 %corner.1 = (f32[4,32,256]{2,1,0:T(8,128)S(1)}, f32[4,32,256]{2,1,0:T(8,128)S(1)}) custom-call(s32[1]{0:T(128)S(6)} %copy.17.widths, f32[64,32,256]{2,1,0:T(8,128)S(1)} %copy-done, f32[64,32,256]{2,1,0:T(8,128)} %refs_1_.5, f32[64,32,256]{2,1,0:T(8,128)} %refs_2_.5, ...), custom_call_target="tpu_custom_call", output_to_operand_aliasing={{0}: (6, {}), {1}: (7, {})} | custom-call | flops 10813440 | bytes 1966080 | tf_op jit(solution)/shard_map/corner/pallas_call | solution.py:338
  36.5 3.2 %collective-permute-start.3 = (f32[4,32,256]{2,1,0:T(8,128)S(1)}, f32[4,32,256]{2,1,0:T(8,128)S(1)}, u32[]{:S(2)}, u32[]{:S(2)}) collective-permute-start(f32[4,32,256]{2,1,0:T(8,128)S(1)} %get-tuple-element.18), channel_id=1, source_target_pairs={{0,16},{16,32},{32,48},{48,64},{64,80},{80,96},{96,112},{112,128},... | collective-permute-start | bytes 393224 | tf_op jit(solution)/shard_map/ppermute | solution.py:394
  39.8 4.2 %collective-permute-start.4 = (f32[4,32,256]{2,1,0:T(8,128)S(1)}, f32[4,32,256]{2,1,0:T(8,128)S(1)}, u32[]{:S(2)}, u32[]{:S(2)}) collective-permute-start(f32[4,32,256]{2,1,0:T(8,128)S(1)} %get-tuple-element.17.refs_7_), channel_id=1, source_target_pairs={{16,0},{32,16},{48,32},{64,48},{80,64},{96,80},{112,96},{128,112},... | collective-permute-start | bytes 393224 | tf_op jit(solution)/shard_map/ppermute | solution.py:395
  43.9 0.0 collective-permute-done.1.refs_5_
  44.0 12.7 %outer.1 = f32[64,32,256]{2,1,0:T(8,128)} custom-call(s32[1]{0:T(128)S(6)} %copy.17.widths, f32[64,32,256]{2,1,0:T(8,128)S(1)} %copy-done, f32[64,32,256]{2,1,0:T(8,128)} %refs_1_.5, f32[64,32,256]{2,1,0:T(8,128)} %refs_2_.5, f32[8,32,256]{2,1,0:T(8,128)S(1)} %pad_maximum_fusion.sides.refs_3_, ...), custom_call_target="tpu_custom_call", output_to_operand_aliasing={{}: (7, {})} | custom-call | flops 34603008 | bytes 6291456 | tf_op jit(solution)/shard_map/outer/pallas_call | solution.py:338
  56.7 0.0 collective-permute-done.3
  56.7 0.0 collective-permute-done.4
  56.7 0.7 %copy.18 = f32[1,4,32,256]{3,2,1,0:T(8,128)} copy(f32[1,4,32,256]{3,2,1,0:T(8,128)S(1)} %bitcast.4) | data formatting | bytes 262144
  57.3 0.7 %copy.19 = f32[1,4,32,256]{3,2,1,0:T(8,128)} copy(f32[1,4,32,256]{3,2,1,0:T(8,128)S(1)} %bitcast.5) | data formatting | bytes 262144
Async XLA Ops:
  4.4 7.7 %collective-permute-start.2 = (f32[200,8,256]{2,1,0:T(8,128)S(1)}, f32[200,8,256]{2,1,0:T(8,128)S(1)}, u32[]{:S(2)}, u32[]{:S(2)}) collective-permute-start(f32[200,8,256]{2,1,0:T(8,128)S(1)} %get-tuple-element.13), channel_id=1, source_target_pairs={{0,1},{2,3},{4,5},{6,7},{8,9},{10,11},{12,13},{14,15},{1,0},{3,2},... | collective-permute-start | bytes 4915208 | tf_op jit(solution)/shard_map/ppermute | solution.py:385
  5.1 24.5 %collective-permute-start = (f32[104,8,256]{2,1,0:T(8,128)S(1)}, f32[104,8,256]{2,1,0:T(8,128)S(1)}, u32[]{:S(2)}, u32[]{:S(2)}) collective-permute-start(f32[104,8,256]{2,1,0:T(8,128)S(1)} %get-tuple-element.11), channel_id=1, source_target_pairs={{1,2},{3,4},{5,6},{7,8},{9,10},{11,12},{13,14},{2,1},{4,3},{6,5},{... | collective-permute-start | bytes 2555912 | tf_op jit(solution)/shard_map/ppermute | solution.py:384
  9.8 19.8 %copy-start = (f32[64,32,256]{2,1,0:T(8,128)S(1)}, f32[64,32,256]{2,1,0:T(8,128)}, u32[]{:S(2)}) copy-start(f32[64,32,256]{2,1,0:T(8,128)} %refs_0_.5) | copy-start | bytes 6291460
  9.8 34.1 %collective-permute-start.1 = (f32[96,8,256]{2,1,0:T(8,128)S(1)}, f32[96,8,256]{2,1,0:T(8,128)S(1)}, u32[]{:S(2)}, u32[]{:S(2)}) collective-permute-start(f32[96,8,256]{2,1,0:T(8,128)S(1)} %get-tuple-element.12), channel_id=1, source_target_pairs={{1,2},{3,4},{5,6},{7,8},{9,10},{11,12},{13,14},{2,1},{4,3},{6,5},{... | collective-permute-start | bytes 2359304 | tf_op jit(solution)/shard_map/ppermute | solution.py:386
  36.5 20.1 %collective-permute-start.3 = (f32[4,32,256]{2,1,0:T(8,128)S(1)}, f32[4,32,256]{2,1,0:T(8,128)S(1)}, u32[]{:S(2)}, u32[]{:S(2)}) collective-permute-start(f32[4,32,256]{2,1,0:T(8,128)S(1)} %get-tuple-element.18), channel_id=1, source_target_pairs={{0,16},{16,32},{32,48},{48,64},{64,80},{80,96},{96,112},{112,128},... | collective-permute-start | bytes 393224 | tf_op jit(solution)/shard_map/ppermute | solution.py:394
  39.8 16.9 %collective-permute-start.4 = (f32[4,32,256]{2,1,0:T(8,128)S(1)}, f32[4,32,256]{2,1,0:T(8,128)S(1)}, u32[]{:S(2)}, u32[]{:S(2)}) collective-permute-start(f32[4,32,256]{2,1,0:T(8,128)S(1)} %get-tuple-element.17.refs_7_), channel_id=1, source_target_pairs={{16,0},{32,16},{48,32},{64,48},{80,64},{96,80},{112,96},{128,112},... | collective-permute-start | bytes 393224 | tf_op jit(solution)/shard_map/ppermute | solution.py:395

commit v5 on v4

--- a/solution.py
+++ b/solution.py
@@ -26,8 +26,7 @@
 MIDDLE = PLANES - 2 * PART
 PREPARED = 4
 PACK_BYTES = 50 * 2**20
-WINDOW_BYTES = 50 * 2**20
-OUTER_BYTES = 50 * 2**20
+WINDOW_BYTES = 40 * 2**20
 
 
 def rotated_sum(low, high, first_lane, last_lane):
@@ -41,32 +40,32 @@
     )
 
 
-def place(cell):
-    return pl.ds(SUB * (cell // 2), SUB), pl.ds(LANES * (cell % 2), LANES)
-
-
-def sweep(tiles, rotated, planes, group_planes, field, band, depths, emit, finish=None):
-    cells = tiles * HALVES
+def place(tiles, cell, shift=0):
+    return cell % HALVES, pl.ds(SUB + cell // HALVES + shift, SUB, stride=tiles), slice(None)
+
+
+def sweep(tiles, rotated, planes, group_planes, field, band, depth, emit, finish=None):
     others = tiles - rotated
     size = group_planes * others * SUB
 
-    def load(plane, cell):
-        return field[(plane, *place(cell % cells))]
-
-    def multiply(group, out):
-        block = field[pl.ds(group * group_planes + 1, group_planes), pl.ds(rotated * SUB, others * SUB), :]
-        block = block.reshape(size, DEPTH)
+    def load(plane, cell, shift=0):
+        return field[(plane, *place(tiles, cell, shift))]
+
+    def body(group, _):
+        base = group * group_planes
+        lane = lax.broadcasted_iota(jnp.int32, (SUB, LANES), 1)
+        first_lane = lane == 0
+        last_lane = lane == LANES - 1
+        block = jnp.concatenate([
+            jnp.concatenate([load(base + 1 + plane, 2 * tile), load(base + 1 + plane, 2 * tile + 1)], axis=1)
+            for plane in range(group_planes)
+            for tile in range(rotated, tiles)
+        ])
         coarse = block.astype(jnp.bfloat16)
         fine = (block - coarse.astype(jnp.float32)).astype(jnp.bfloat16)
         parts = jnp.concatenate([coarse, fine], axis=0)
         sums = jnp.dot(parts, band[...], preferred_element_type=jnp.float32)
-        out[...] = sums[:size] + sums[size:]
-
-    def work(group, depth):
-        base = group * group_planes
-        lane = lax.broadcasted_iota(jnp.int32, (SUB, LANES), 1)
-        first_lane = lane == 0
-        last_lane = lane == LANES - 1
+        depth[...] = sums[:size] + sums[size:]
         for tile in range(tiles):
             pair = [2 * tile + half for half in range(HALVES)]
             before = [load(base, cell) for cell in pair]
@@ -80,29 +79,15 @@
                     rows = pl.ds((plane * others + tile - rotated) * SUB, SUB)
                     along = [depth[rows, pl.ds(half * LANES, LANES)] for half in range(HALVES)]
                 for half, cell in enumerate(pair):
-                    above = load(at + 1, cell - 2)
-                    if tile == 0:
-                        above = pltpu.roll(above, 1, 0)
-                    below = load(at + 1, cell + 2)
-                    if tile == tiles - 1:
-                        below = pltpu.roll(below, SUB - 1, 0)
-                    around = ((before[half] + after[half]) + (above + below)) + along[half]
+                    beside = load(at + 1, cell, -1) + load(at + 1, cell, 1)
+                    around = ((before[half] + after[half]) + beside) + along[half]
                     emit(at, cell, here[half], around)
                 before, here = here, after
-
-    groups = planes // group_planes
-    multiply(0, depths[0])
-
-    def body(index, _):
-        for side in range(2):
-            group = 2 * index + side
-            multiply(jnp.minimum(group + 1, groups - 1), depths[1 - side])
-            work(group, depths[side])
         if finish is not None:
-            finish(index)
+            finish(group)
         return 0
 
-    lax.fori_loop(0, groups // 2, body, 0)
+    lax.fori_loop(0, planes // group_planes, body, 0)
 
 
 def pack_kernel(
@@ -146,12 +131,10 @@
     take({"inner": 0, "corner": 2, "outer": 2}[kind])
     field_out = take(1)[0] if with_field else None
     trace_outs = take(2) if with_traces else []
-    naturals = take(3)
+    naturals = take(2)
     side_naturals = take(2)
-    out_nat = take(1)[0] if with_field else None
     trace_nats = take(2) if with_traces else []
-    u_even, u_odd, change, f, inverse, band, depth_a, depth_b, in_sems, out_sems = take(10)
-    depths = (depth_a, depth_b)
+    u_even, u_odd, change, f, inverse, band, depth, in_sems, out_sems = take(9)
 
     cells = tiles * HALVES
     planes = 2 * REACH if kind == "corner" else PLANES
@@ -171,6 +154,9 @@
     def fetch(src, src_start, src_rows, dst, dst_start, dst_rows, count):
         nonlocal used
         copies = []
+        if dst is u_even:
+            dst_start = 1 + dst_start
+            dst_rows = pl.ds(SUB + dst_rows.start, dst_rows.size)
         for half in range(HALVES):
             copy = pltpu.make_async_copy(
                 src.at[pl.ds(src_start, count), src_rows, pl.ds(half * LANES, LANES)],
@@ -183,20 +169,21 @@
         return copies
 
     whole = pl.ds(0, HALO)
-    chunks = 1 if kind == "corner" else 2
-    size = planes // chunks
+    loaded = (u_even, *naturals)
+    bounds = (0, planes) if kind == "corner" else (0, PART, planes)
+    chunks = len(bounds) - 1
     waits = [[] for _ in range(chunks)]
     late = []
     for chunk in range(chunks):
-        for index, (own, nat) in enumerate(zip(fields, naturals)):
+        at, size = bounds[chunk], bounds[chunk + 1] - bounds[chunk]
+        for index, (own, nat) in enumerate(zip(fields, loaded)):
             if kind == "corner":
                 waits[0] += fetch(own, 0, own_src, nat, 0, own_dst, REACH)
                 waits[0] += fetch(own, true_width - REACH, own_src, nat, REACH, own_dst, REACH)
-                at = 2 * index * PART
-                waits[0] += fetch(halos[0], at, whole, nat, 0, halo_dst, REACH)
-                waits[0] += fetch(halos[0], at + 2 * PART - REACH, whole, nat, REACH, halo_dst, REACH)
+                low, high = 2 * index * PART, 2 * (index + 1) * PART - REACH
+                waits[0] += fetch(halos[0], low, whole, nat, 0, halo_dst, REACH)
+                waits[0] += fetch(halos[0], high, whole, nat, REACH, halo_dst, REACH)
             else:
-                at = chunk * size
                 waits[chunk] += fetch(own, at, own_src, nat, at, own_dst, size)
                 if kind == "inner":
                     waits[chunk] += fetch(halos[0], index * planes + at, whole, nat, at, halo_dst, size)
@@ -214,7 +201,7 @@
     band[...] = jnp.where(jnp.abs(row_at - column_at) == 1, 1.0, 0.0).astype(jnp.bfloat16)
     for plane in (0, planes + 1):
         for field in (u_even, u_odd, change):
-            field[plane] = jnp.zeros((tiles * SUB, DEPTH), jnp.float32)
+            field[plane] = jnp.zeros(field.shape[1:], jnp.float32)
 
     def strided(tile):
         return pl.ds(tile, SUB, stride=tiles)
@@ -227,9 +214,8 @@
             x = index * PREPARED + plane
             for cell in range(cells):
                 half, rows = cell % 2, strided(cell // 2)
-                first, coef, rate = (nat[x, half, rows, :] for nat in naturals)
+                coef, rate = (nat[x, half, rows, :] for nat in naturals)
                 live = jnp.full((SUB, LANES), x, jnp.int32) < width
-                u_even[(x + 1, *place(cell))] = jnp.where(live, first, 0.0)
                 f[x, cell] = jnp.where(live, rate, 0.0)
                 inside = jnp.logical_and(live, coef > 0.0)
                 inverse[x, cell] = jnp.where(inside, ROOT / (coef + own_part(x)), 0.0)
@@ -240,19 +226,27 @@
             copy.wait()
         late = []
         if kind == "outer" and chunk == 0:
-            for index, nat in enumerate(naturals):
+            for index, nat in enumerate(loaded):
                 late += fetch(
                     halos[0], (2 * index + 1) * PART, whole, nat, true_width - PART, halo_dst, PART
                 )
-        lax.fori_loop(chunk * size // PREPARED, (chunk + 1) * size // PREPARED, prepare, 0)
+        lax.fori_loop(bounds[chunk] // PREPARED, bounds[chunk + 1] // PREPARED, prepare, 0)
     for copy in side_waits:
         copy.wait()
 
+    def clear(x, _):
+        u_even[x + 1] = jnp.zeros(u_even.shape[1:], jnp.float32)
+        return 0
+
+    if kind != "corner":
+        lax.fori_loop(width, planes, clear, 0)
+
     def field_copies(index):
-        part = pl.ds(2 * index * group_planes, 2 * group_planes)
+        part = pl.ds(index * group_planes, group_planes)
+        held = pl.ds(1 + index * group_planes, group_planes)
         return [
             pltpu.make_async_copy(
-                out_nat.at[part, half, kept_src, :],
+                u_even.at[held, half, pl.ds(SUB + HALO, kept_rows), :],
                 field_out.at[part, kept_dst, pl.ds(half * LANES, LANES)],
                 out_sems.at[4 + 2 * index + half],
             )
@@ -267,32 +261,30 @@
         for cell in range(cells):
             half, rows = cell % 2, strided(cell // 2)
             for x, side in ((0, side_naturals[0]), (width - 1, side_naturals[1])):
-                f[x, cell] = naturals[2][x, half, rows, :] + side[step, half, rows, :]
+                f[x, cell] = naturals[1][x, half, rows, :] + side[step, half, rows, :]
 
         def first_half(x, cell, here, around):
             rest = (f[x, cell] - own_part(x) * here) + around
-            change[(x + 1, *place(cell))] = rest * inverse[x, cell]
+            change[(x + 1, *place(tiles, cell))] = rest * inverse[x, cell]
 
         def second_half(x, cell, here, around):
-            value = (u[(x + 1, *place(cell))] + ROOT * here) + around * inverse[x, cell]
-            u_next[(x + 1, *place(cell))] = value
-            if with_field and u is u_odd:
-                out_nat[x, cell % 2, strided(cell // 2), :] = value
+            value = (u[(x + 1, *place(tiles, cell))] + ROOT * here) + around * inverse[x, cell]
+            u_next[(x + 1, *place(tiles, cell))] = value
 
         def finish(index):
             if with_field and u is u_odd:
                 pl.when(step == STEPS - 1)(lambda: put_field(index))
 
-        sweep(tiles, rotated, planes, group_planes, u, band, depths, first_half)
-        sweep(tiles, rotated, planes, group_planes, change, band, depths, second_half, finish)
+        sweep(tiles, rotated, planes, group_planes, u, band, depth, first_half)
+        sweep(tiles, rotated, planes, group_planes, change, band, depth, second_half, finish)
         if not with_traces:
             return
         for cell in range(cells):
             half, rows = cell % 2, strided(cell // 2)
             for nat, end, inward in ((trace_nats[0], width, width - 1), (trace_nats[1], 1, 2)):
-                at_end_plane = u_next[(end, *place(cell))]
+                at_end_plane = u_next[(end, *place(tiles, cell))]
                 nat[step, half, rows, :] = BETA * at_end_plane + (
-                    at_end_plane - u_next[(inward, *place(cell))]
+                    at_end_plane - u_next[(inward, *place(tiles, cell))]
                 )
 
     def two_steps(index, _):
@@ -313,7 +305,7 @@
             copy.start()
             copies.append(copy)
     if with_field:
-        for index in range(planes // group_planes // 2):
+        for index in range(planes // group_planes):
             copies += field_copies(index)
     for copy in copies:
         copy.wait()
@@ -331,7 +323,7 @@
     natural = pltpu.VMEM((planes, HALVES, rows, LANES), jnp.float32)
     narrow = pltpu.VMEM((STEPS, HALVES, rows, LANES), jnp.float32)
     tiled = pltpu.VMEM((planes, cells, SUB, LANES), jnp.float32)
-    padded = pltpu.VMEM((planes + 2, rows, DEPTH), jnp.float32)
+    padded = pltpu.VMEM((planes + 2, HALVES, rows + 2 * SUB, LANES), jnp.float32)
     field = jax.ShapeDtypeStruct(args[1].shape, jnp.float32)
     trace = jax.ShapeDtypeStruct((STEPS, ROWS, DEPTH), jnp.float32)
     outs = {"inner": (field, trace, trace), "corner": (trace, trace), "outer": (field,)}[kind]
@@ -342,13 +334,13 @@
         out_specs=(ANYWHERE,) * len(outs),
         input_output_aliases={5 + len(halos) + i: i for i in range(len(previous))},
         scratch_shapes=[
-            *[natural] * 3, *[narrow] * 2,
-            *([] if kind == "corner" else [natural]), *([] if kind == "outer" else [narrow] * 2),
+            *[natural] * 2, *[narrow] * 2,
+            *([] if kind == "outer" else [narrow] * 2),
             padded, padded, padded, tiled, tiled,
             pltpu.VMEM((DEPTH, DEPTH), jnp.bfloat16),
-            *[pltpu.VMEM((group_planes * (tiles - rotated) * SUB, DEPTH), jnp.float32)] * 2,
+            pltpu.VMEM((group_planes * (tiles - rotated) * SUB, DEPTH), jnp.float32),
             pltpu.SemaphoreType.DMA((64,)),
-            pltpu.SemaphoreType.DMA((4 + planes // group_planes,)),
+            pltpu.SemaphoreType.DMA((4 + HALVES * planes // group_planes,)),
         ],
         compiler_params=pltpu.CompilerParams(vmem_limit_bytes=limit),
         cost_estimate=pl.CostEstimate(
@@ -385,15 +377,15 @@
     on_chip = lax.ppermute(on_chip, "dev", cores)
     middle = lax.ppermute(middle, "dev", chips)
 
-    field, trace_high, trace_low = run_window("inner", 5, 2, 8, WINDOW_BYTES, args, (on_chip,))
-    trace_high, trace_low = run_window("corner", 3, 1, 5, WINDOW_BYTES, args, (edge,), (trace_high, trace_low))
+    field, trace_high, trace_low = run_window("inner", 5, 3, 16, WINDOW_BYTES, args, (on_chip,))
+    trace_high, trace_low = run_window("corner", 3, 2, 10, WINDOW_BYTES, args, (edge,), (trace_high, trace_low))
 
     subs = lax.axis_size("sub")
     up = [(i, i + 1) for i in range(subs - 1)]
     down = [(i + 1, i) for i in range(subs - 1)]
     new_left = lax.ppermute(trace_high, "sub", up)
     new_right = lax.ppermute(trace_low, "sub", down)
-    (field,) = run_window("outer", 3, 1, 8, OUTER_BYTES, args, (edge, middle), (field,), (trace_low,))
+    (field,) = run_window("outer", 3, 2, 16, WINDOW_BYTES, args, (edge, middle), (field,), (trace_low,))
     return (field, new_left[None], new_right[None])
 
 

time: 58.3 us -> 49.8 us (0.85)
  Pallas kernels: 39.2 us -> 30.8 us
    pallas_call x3, Pallas kernels: 37.1 us -> 28.5 us  [run_window(): pl.pallas_call(functools.partial(window_kernel, kind, tiles, rotated, gro...]
    unnamed x4 -> x8, local copies, waits for them, and re-layouts: 1.32 us -> 1.33 us
  transfers between devices with their start and end apart: 5 -> 5, of which waited for: 0 -> 0; matrix products, arithmetic and copies ran while one was open for 0% -> 0% of each run, Pallas kernels for 64% -> 58%
where the time goes in v5:
time: 49.8 us; the launch traced here: 49.4 us
  Pallas kernels  30.8 us (62%)
  starting transfers between devices  14.9 us (30%)
  between operations  1.43 us (3%)
  local copies, waits for them, and re-layouts  1.33 us (3%)
  other arithmetic  0.99 us (2%)
    pallas_call x3, Pallas kernels, run_window(): pl.pallas_call(functools.partial(window_kernel, kind, tiles, rotated, gro...  28.5 us
    ppermute x1, starting transfers between devices, on_device(): edge = lax.ppermute(edge, 'dev', chips)  4.79 us
    ppermute x1, starting transfers between devices, on_device(): new_right = lax.ppermute(trace_low, 'sub', down)  4.06 us
    ppermute x1, starting transfers between devices, on_device(): new_left = lax.ppermute(trace_high, 'sub', up)  3.33 us
    pallas_call x1, Pallas kernels, on_device(): pl.pallas_call(pack_kernel, out_shape=tuple(rims), in_specs=[IN_SMEM] + [...  2.24 us
    ppermute x1, starting transfers between devices, on_device(): middle = lax.ppermute(middle, 'dev', chips)  1.97 us
    unnamed x8, local copies, waits for them, and re-layouts  1.33 us
  transfers between devices with their start and end apart: 5, of which 0 were waited for; matrix products, arithmetic and copies ran while one was open for 0% of the time, Pallas kernels for 58%

profile of v5, /device:TPU:101, one launch (start us, length us, event | category | flops | bytes accessed | tf_op | source)
XLA Modules:
  0.0 49.4 jit_solution(11561036936269986082)
XLA Ops:
  1.3 1.0 %pad_maximum_fusion.sides.refs_3_ = f32[8,32,256]{2,1,0:T(8,128)S(1)} fusion(f32[4,32,256]{2,1,0:T(8,128)} %bitcast.6, f32[4,32,256]{2,1,0:T(8,128)} %bitcast.7), kind=kLoop, calls=%fused_computation | loop fusion | flops 65536 | bytes 524288 | tf_op jit(solution)/shard_map/concatenate | solution.py:356
  2.3 0.0 copy-start
  2.3 0.0 copy-start.1
  2.3 0.0 copy-start.2
  2.3 2.2 %pack.1 = (f32[104,8,256]{2,1,0:T(8,128)S(1)}, f32[96,8,256]{2,1,0:T(8,128)S(1)}, f32[200,8,256]{2,1,0:T(8,128)S(1)}) custom-call(s32[1]{0:T(128)S(6)} %copy.17.widths, f32[64,32,256]{2,1,0:T(8,128)} %refs_0_.5, f32[64,32,256]{2,1,0:T(8,128)} %refs_1_.5, f32[64,32,256]{2,1,0:T(8,128)} %refs_2_.5, f32[8,32,256]{2,1,0:T(8,128)S(1)} %pad_maximum_fusion.sides.refs_3_), custom_call_target="tpu_custom_call" | custom-call | tf_op jit(solution)/shard_map/pack/pallas_call | solution.py:362
  4.6 0.8 %collective-permute-start.2 = (f32[200,8,256]{2,1,0:T(8,128)S(1)}, f32[200,8,256]{2,1,0:T(8,128)S(1)}, u32[]{:S(2)}, u32[]{:S(2)}) collective-permute-start(f32[200,8,256]{2,1,0:T(8,128)S(1)} %get-tuple-element.13), channel_id=1, source_target_pairs={{0,1},{2,3},{4,5},{6,7},{8,9},{10,11},{12,13},{14,15},{1,0},{3,2},... | collective-permute-start | bytes 4915208 | tf_op jit(solution)/shard_map/ppermute | solution.py:377
  5.3 4.8 %collective-permute-start = (f32[104,8,256]{2,1,0:T(8,128)S(1)}, f32[104,8,256]{2,1,0:T(8,128)S(1)}, u32[]{:S(2)}, u32[]{:S(2)}) collective-permute-start(f32[104,8,256]{2,1,0:T(8,128)S(1)} %get-tuple-element.11), channel_id=1, source_target_pairs={{1,2},{3,4},{5,6},{7,8},{9,10},{11,12},{13,14},{2,1},{4,3},{6,5},{... | collective-permute-start | bytes 2555912 | tf_op jit(solution)/shard_map/ppermute | solution.py:376
  10.1 2.0 %collective-permute-start.1 = (f32[96,8,256]{2,1,0:T(8,128)S(1)}, f32[96,8,256]{2,1,0:T(8,128)S(1)}, u32[]{:S(2)}, u32[]{:S(2)}) collective-permute-start(f32[96,8,256]{2,1,0:T(8,128)S(1)} %get-tuple-element.12), channel_id=1, source_target_pairs={{1,2},{3,4},{5,6},{7,8},{9,10},{11,12},{13,14},{2,1},{4,3},{6,5},{... | collective-permute-start | bytes 2359304 | tf_op jit(solution)/shard_map/ppermute | solution.py:378
  12.1 0.0 collective-permute-done.2.refs_4_
  12.1 0.0 copy-done
  12.1 0.0 copy-done.1
  12.1 0.0 copy-done.2
  12.1 14.3 %inner.1 = (f32[64,32,256]{2,1,0:T(8,128)}, f32[4,32,256]{2,1,0:T(8,128)S(1)}, f32[4,32,256]{2,1,0:T(8,128)S(1)}) custom-call(s32[1]{0:T(128)S(6)} %copy.17.widths, f32[64,32,256]{2,1,0:T(8,128)S(1)} %copy-done, f32[64,32,256]{2,1,0:T(8,128)S(1)} %copy-done.1, f32[64,32,256]{2,1,0:T(8,128)S(1)} %copy-done.2, ...), custom_call_target="tpu_custom_call" | custom-call | flops 57671680 | bytes 10485760 | tf_op jit(solution)/shard_map/inner/pallas_call | solution.py:330
  26.4 0.0 collective-permute-done.refs_4_
  26.4 4.1 %corner.1 = (f32[4,32,256]{2,1,0:T(8,128)S(1)}, f32[4,32,256]{2,1,0:T(8,128)S(1)}) custom-call(s32[1]{0:T(128)S(6)} %copy.17.widths, f32[64,32,256]{2,1,0:T(8,128)S(1)} %copy-done, f32[64,32,256]{2,1,0:T(8,128)S(1)} %copy-done.1, f32[64,32,256]{2,1,0:T(8,128)S(1)} %copy-done.2, ...), custom_call_target="tpu_custom_call", output_to_operand_aliasing={{0}: (6, {}), {1}: (7, {})} | custom-call | flops 10813440 | bytes 1966080 | tf_op jit(solution)/shard_map/corner/pallas_call | solution.py:330
  30.6 3.3 %collective-permute-start.3 = (f32[4,32,256]{2,1,0:T(8,128)S(1)}, f32[4,32,256]{2,1,0:T(8,128)S(1)}, u32[]{:S(2)}, u32[]{:S(2)}) collective-permute-start(f32[4,32,256]{2,1,0:T(8,128)S(1)} %get-tuple-element.18), channel_id=1, source_target_pairs={{0,16},{16,32},{32,48},{48,64},{64,80},{80,96},{96,112},{112,128},... | collective-permute-start | bytes 393224 | tf_op jit(solution)/shard_map/ppermute | solution.py:386
  33.9 4.1 %collective-permute-start.4 = (f32[4,32,256]{2,1,0:T(8,128)S(1)}, f32[4,32,256]{2,1,0:T(8,128)S(1)}, u32[]{:S(2)}, u32[]{:S(2)}) collective-permute-start(f32[4,32,256]{2,1,0:T(8,128)S(1)} %get-tuple-element.17.refs_7_), channel_id=1, source_target_pairs={{16,0},{32,16},{48,32},{64,48},{80,64},{96,80},{112,96},{128,112},... | collective-permute-start | bytes 393224 | tf_op jit(solution)/shard_map/ppermute | solution.py:387
  38.0 0.0 collective-permute-done.1.refs_5_
  38.0 10.1 %outer.1 = f32[64,32,256]{2,1,0:T(8,128)} custom-call(s32[1]{0:T(128)S(6)} %copy.17.widths, f32[64,32,256]{2,1,0:T(8,128)S(1)} %copy-done, f32[64,32,256]{2,1,0:T(8,128)S(1)} %copy-done.1, f32[64,32,256]{2,1,0:T(8,128)S(1)} %copy-done.2, f32[8,32,256]{2,1,0:T(8,128)S(1)} %pad_maximum_fusion.sides.refs_3_, ...), custom_call_target="tpu_custom_call", output_to_operand_aliasing={{}: (7, {})} | custom-call | flops 34603008 | bytes 6291456 | tf_op jit(solution)/shard_map/outer/pallas_call | solution.py:330
  48.1 0.0 collective-permute-done.3
  48.1 0.0 collective-permute-done.4
  48.1 0.7 %copy.18 = f32[1,4,32,256]{3,2,1,0:T(8,128)} copy(f32[1,4,32,256]{3,2,1,0:T(8,128)S(1)} %bitcast.4) | data formatting | bytes 262144
  48.8 0.7 %copy.19 = f32[1,4,32,256]{3,2,1,0:T(8,128)} copy(f32[1,4,32,256]{3,2,1,0:T(8,128)S(1)} %bitcast.5) | data formatting | bytes 262144
Async XLA Ops:
  2.3 9.8 %copy-start = (f32[64,32,256]{2,1,0:T(8,128)S(1)}, f32[64,32,256]{2,1,0:T(8,128)}, u32[]{:S(2)}) copy-start(f32[64,32,256]{2,1,0:T(8,128)} %refs_0_.5) | copy-start | bytes 6291460
  2.3 9.8 %copy-start.1 = (f32[64,32,256]{2,1,0:T(8,128)S(1)}, f32[64,32,256]{2,1,0:T(8,128)}, u32[]{:S(2)}) copy-start(f32[64,32,256]{2,1,0:T(8,128)} %refs_1_.5) | copy-start | bytes 6291460
  2.3 9.8 %copy-start.2 = (f32[64,32,256]{2,1,0:T(8,128)S(1)}, f32[64,32,256]{2,1,0:T(8,128)}, u32[]{:S(2)}) copy-start(f32[64,32,256]{2,1,0:T(8,128)} %refs_2_.5) | copy-start | bytes 6291460
  4.6 7.5 %collective-permute-start.2 = (f32[200,8,256]{2,1,0:T(8,128)S(1)}, f32[200,8,256]{2,1,0:T(8,128)S(1)}, u32[]{:S(2)}, u32[]{:S(2)}) collective-permute-start(f32[200,8,256]{2,1,0:T(8,128)S(1)} %get-tuple-element.13), channel_id=1, source_target_pairs={{0,1},{2,3},{4,5},{6,7},{8,9},{10,11},{12,13},{14,15},{1,0},{3,2},... | collective-permute-start | bytes 4915208 | tf_op jit(solution)/shard_map/ppermute | solution.py:377
  5.3 21.1 %collective-permute-start = (f32[104,8,256]{2,1,0:T(8,128)S(1)}, f32[104,8,256]{2,1,0:T(8,128)S(1)}, u32[]{:S(2)}, u32[]{:S(2)}) collective-permute-start(f32[104,8,256]{2,1,0:T(8,128)S(1)} %get-tuple-element.11), channel_id=1, source_target_pairs={{1,2},{3,4},{5,6},{7,8},{9,10},{11,12},{13,14},{2,1},{4,3},{6,5},{... | collective-permute-start | bytes 2555912 | tf_op jit(solution)/shard_map/ppermute | solution.py:376
  10.1 27.9 %collective-permute-start.1 = (f32[96,8,256]{2,1,0:T(8,128)S(1)}, f32[96,8,256]{2,1,0:T(8,128)S(1)}, u32[]{:S(2)}, u32[]{:S(2)}) collective-permute-start(f32[96,8,256]{2,1,0:T(8,128)S(1)} %get-tuple-element.12), channel_id=1, source_target_pairs={{1,2},{3,4},{5,6},{7,8},{9,10},{11,12},{13,14},{2,1},{4,3},{6,5},{... | collective-permute-start | bytes 2359304 | tf_op jit(solution)/shard_map/ppermute | solution.py:378
  30.6 17.5 %collective-permute-start.3 = (f32[4,32,256]{2,1,0:T(8,128)S(1)}, f32[4,32,256]{2,1,0:T(8,128)S(1)}, u32[]{:S(2)}, u32[]{:S(2)}) collective-permute-start(f32[4,32,256]{2,1,0:T(8,128)S(1)} %get-tuple-element.18), channel_id=1, source_target_pairs={{0,16},{16,32},{32,48},{48,64},{64,80},{80,96},{96,112},{112,128},... | collective-permute-start | bytes 393224 | tf_op jit(solution)/shard_map/ppermute | solution.py:386
  33.9 14.2 %collective-permute-start.4 = (f32[4,32,256]{2,1,0:T(8,128)S(1)}, f32[4,32,256]{2,1,0:T(8,128)S(1)}, u32[]{:S(2)}, u32[]{:S(2)}) collective-permute-start(f32[4,32,256]{2,1,0:T(8,128)S(1)} %get-tuple-element.17.refs_7_), channel_id=1, source_target_pairs={{16,0},{32,16},{48,32},{64,48},{80,64},{96,80},{112,96},{128,112},... | collective-permute-start | bytes 393224 | tf_op jit(solution)/shard_map/ppermute | solution.py:387

commit v6 on v4

--- a/solution.py
+++ b/solution.py
@@ -26,8 +26,7 @@
 MIDDLE = PLANES - 2 * PART
 PREPARED = 4
 PACK_BYTES = 50 * 2**20
-WINDOW_BYTES = 50 * 2**20
-OUTER_BYTES = 50 * 2**20
+WINDOW_BYTES = 40 * 2**20
 
 
 def rotated_sum(low, high, first_lane, last_lane):
@@ -45,7 +44,7 @@
     return pl.ds(SUB * (cell // 2), SUB), pl.ds(LANES * (cell % 2), LANES)
 
 
-def sweep(tiles, rotated, planes, group_planes, field, band, depths, emit, finish=None):
+def sweep(tiles, rotated, planes, group_planes, field, band, depth, emit, finish=None):
     cells = tiles * HALVES
     others = tiles - rotated
     size = group_planes * others * SUB
@@ -53,20 +52,18 @@
     def load(plane, cell):
         return field[(plane, *place(cell % cells))]
 
-    def multiply(group, out):
-        block = field[pl.ds(group * group_planes + 1, group_planes), pl.ds(rotated * SUB, others * SUB), :]
+    def body(group, _):
+        base = group * group_planes
+        lane = lax.broadcasted_iota(jnp.int32, (SUB, LANES), 1)
+        first_lane = lane == 0
+        last_lane = lane == LANES - 1
+        block = field[pl.ds(base + 1, group_planes), pl.ds(rotated * SUB, others * SUB), :]
         block = block.reshape(size, DEPTH)
         coarse = block.astype(jnp.bfloat16)
         fine = (block - coarse.astype(jnp.float32)).astype(jnp.bfloat16)
         parts = jnp.concatenate([coarse, fine], axis=0)
         sums = jnp.dot(parts, band[...], preferred_element_type=jnp.float32)
-        out[...] = sums[:size] + sums[size:]
-
-    def work(group, depth):
-        base = group * group_planes
-        lane = lax.broadcasted_iota(jnp.int32, (SUB, LANES), 1)
-        first_lane = lane == 0
-        last_lane = lane == LANES - 1
+        depth[...] = sums[:size] + sums[size:]
         for tile in range(tiles):
             pair = [2 * tile + half for half in range(HALVES)]
             before = [load(base, cell) for cell in pair]
@@ -89,20 +86,11 @@
                     around = ((before[half] + after[half]) + (above + below)) + along[half]
                     emit(at, cell, here[half], around)
                 before, here = here, after
-
-    groups = planes // group_planes
-    multiply(0, depths[0])
-
-    def body(index, _):
-        for side in range(2):
-            group = 2 * index + side
-            multiply(jnp.minimum(group + 1, groups - 1), depths[1 - side])
-            work(group, depths[side])
         if finish is not None:
-            finish(index)
+            finish(group)
         return 0
 
-    lax.fori_loop(0, groups // 2, body, 0)
+    lax.fori_loop(0, planes // group_planes, body, 0)
 
 
 def pack_kernel(
@@ -150,8 +138,7 @@
     side_naturals = take(2)
     out_nat = take(1)[0] if with_field else None
     trace_nats = take(2) if with_traces else []
-    u_even, u_odd, change, f, inverse, band, depth_a, depth_b, in_sems, out_sems = take(10)
-    depths = (depth_a, depth_b)
+    u_even, u_odd, change, f, inverse, band, depth, in_sems, out_sems = take(9)
 
     cells = tiles * HALVES
     planes = 2 * REACH if kind == "corner" else PLANES
@@ -183,20 +170,20 @@
         return copies
 
     whole = pl.ds(0, HALO)
-    chunks = 1 if kind == "corner" else 2
-    size = planes // chunks
+    bounds = (0, planes) if kind == "corner" else (0, PART, planes)
+    chunks = len(bounds) - 1
     waits = [[] for _ in range(chunks)]
     late = []
     for chunk in range(chunks):
+        at, size = bounds[chunk], bounds[chunk + 1] - bounds[chunk]
         for index, (own, nat) in enumerate(zip(fields, naturals)):
             if kind == "corner":
                 waits[0] += fetch(own, 0, own_src, nat, 0, own_dst, REACH)
                 waits[0] += fetch(own, true_width - REACH, own_src, nat, REACH, own_dst, REACH)
-                at = 2 * index * PART
-                waits[0] += fetch(halos[0], at, whole, nat, 0, halo_dst, REACH)
-                waits[0] += fetch(halos[0], at + 2 * PART - REACH, whole, nat, REACH, halo_dst, REACH)
+                low, high = 2 * index * PART, 2 * (index + 1) * PART - REACH
+                waits[0] += fetch(halos[0], low, whole, nat, 0, halo_dst, REACH)
+                waits[0] += fetch(halos[0], high, whole, nat, REACH, halo_dst, REACH)
             else:
-                at = chunk * size
                 waits[chunk] += fetch(own, at, own_src, nat, at, own_dst, size)
                 if kind == "inner":
                     waits[chunk] += fetch(halos[0], index * planes + at, whole, nat, at, halo_dst, size)
@@ -244,12 +231,12 @@
                 late += fetch(
                     halos[0], (2 * index + 1) * PART, whole, nat, true_width - PART, halo_dst, PART
                 )
-        lax.fori_loop(chunk * size // PREPARED, (chunk + 1) * size // PREPARED, prepare, 0)
+        lax.fori_loop(bounds[chunk] // PREPARED, bounds[chunk + 1] // PREPARED, prepare, 0)
     for copy in side_waits:
         copy.wait()
 
     def field_copies(index):
-        part = pl.ds(2 * index * group_planes, 2 * group_planes)
+        part = pl.ds(index * group_planes, group_planes)
         return [
             pltpu.make_async_copy(
                 out_nat.at[part, half, kept_src, :],
@@ -283,8 +270,8 @@
             if with_field and u is u_odd:
                 pl.when(step == STEPS - 1)(lambda: put_field(index))
 
-        sweep(tiles, rotated, planes, group_planes, u, band, depths, first_half)
-        sweep(tiles, rotated, planes, group_planes, change, band, depths, second_half, finish)
+        sweep(tiles, rotated, planes, group_planes, u, band, depth, first_half)
+        sweep(tiles, rotated, planes, group_planes, change, band, depth, second_half, finish)
         if not with_traces:
             return
         for cell in range(cells):
@@ -313,7 +300,7 @@
             copy.start()
             copies.append(copy)
     if with_field:
-        for index in range(planes // group_planes // 2):
+        for index in range(planes // group_planes):
             copies += field_copies(index)
     for copy in copies:
         copy.wait()
@@ -346,9 +333,9 @@
             *([] if kind == "corner" else [natural]), *([] if kind == "outer" else [narrow] * 2),
             padded, padded, padded, tiled, tiled,
             pltpu.VMEM((DEPTH, DEPTH), jnp.bfloat16),
-            *[pltpu.VMEM((group_planes * (tiles - rotated) * SUB, DEPTH), jnp.float32)] * 2,
+            pltpu.VMEM((group_planes * (tiles - rotated) * SUB, DEPTH), jnp.float32),
             pltpu.SemaphoreType.DMA((64,)),
-            pltpu.SemaphoreType.DMA((4 + planes // group_planes,)),
+            pltpu.SemaphoreType.DMA((4 + HALVES * planes // group_planes,)),
         ],
         compiler_params=pltpu.CompilerParams(vmem_limit_bytes=limit),
         cost_estimate=pl.CostEstimate(
@@ -385,15 +372,15 @@
     on_chip = lax.ppermute(on_chip, "dev", cores)
     middle = lax.ppermute(middle, "dev", chips)
 
-    field, trace_high, trace_low = run_window("inner", 5, 2, 8, WINDOW_BYTES, args, (on_chip,))
-    trace_high, trace_low = run_window("corner", 3, 1, 5, WINDOW_BYTES, args, (edge,), (trace_high, trace_low))
+    field, trace_high, trace_low = run_window("inner", 5, 4, 32, WINDOW_BYTES, args, (on_chip,))
+    trace_high, trace_low = run_window("corner", 3, 2, 20, WINDOW_BYTES, args, (edge,), (trace_high, trace_low))
 
     subs = lax.axis_size("sub")
     up = [(i, i + 1) for i in range(subs - 1)]
     down = [(i + 1, i) for i in range(subs - 1)]
     new_left = lax.ppermute(trace_high, "sub", up)
     new_right = lax.ppermute(trace_low, "sub", down)
-    (field,) = run_window("outer", 3, 1, 8, OUTER_BYTES, args, (edge, middle), (field,), (trace_low,))
+    (field,) = run_window("outer", 3, 2, 32, WINDOW_BYTES, args, (edge, middle), (field,), (trace_low,))
     return (field, new_left[None], new_right[None])
 
 

time: 58.3 us -> 47.3 us (0.81)
  Pallas kernels: 39.2 us -> 28.4 us
    pallas_call x3, Pallas kernels: 37.1 us -> 26.1 us  [run_window(): pl.pallas_call(functools.partial(window_kernel, kind, tiles, rotated, gro...]
    unnamed x4 -> x8, local copies, waits for them, and re-layouts: 1.32 us -> 1.33 us
  transfers between devices with their start and end apart: 5 -> 5, of which waited for: 0 -> 0; matrix products, arithmetic and copies ran while one was open for 0% -> 0% of each run, Pallas kernels for 64% -> 56%
where the time goes in v6:
time: 47.3 us; the launch traced here: 47 us
  Pallas kernels  28.4 us (60%)
  starting transfers between devices  14.9 us (32%)
  between operations  1.43 us (3%)
  local copies, waits for them, and re-layouts  1.33 us (3%)
  other arithmetic  0.99 us (2%)
    pallas_call x3, Pallas kernels, run_window(): pl.pallas_call(functools.partial(window_kernel, kind, tiles, rotated, gro...  26.1 us
    ppermute x1, starting transfers between devices, on_device(): edge = lax.ppermute(edge, 'dev', chips)  4.79 us
    ppermute x1, starting transfers between devices, on_device(): new_right = lax.ppermute(trace_low, 'sub', down)  4.17 us
    ppermute x1, starting transfers between devices, on_device(): new_left = lax.ppermute(trace_high, 'sub', up)  3.22 us
    pallas_call x1, Pallas kernels, on_device(): pl.pallas_call(pack_kernel, out_shape=tuple(rims), in_specs=[IN_SMEM] + [...  2.24 us
    ppermute x1, starting transfers between devices, on_device(): middle = lax.ppermute(middle, 'dev', chips)  1.97 us
    unnamed x8, local copies, waits for them, and re-layouts  1.33 us
    concatenate x1, other arithmetic, on_device(): sides = jnp.concatenate([left_data[0], right_data[0]])  0.99 us
  transfers between devices with their start and end apart: 5, of which 0 were waited for; matrix products, arithmetic and copies ran while one was open for 0% of the time, Pallas kernels for 56%

profile of v6, /device:TPU:101, one launch (start us, length us, event | category | flops | bytes accessed | tf_op | source)
XLA Modules:
  0.0 47.0 jit_solution(16022445054793049819)
XLA Ops:
  1.3 1.0 %pad_maximum_fusion.sides.refs_3_ = f32[8,32,256]{2,1,0:T(8,128)S(1)} fusion(f32[4,32,256]{2,1,0:T(8,128)} %bitcast.6, f32[4,32,256]{2,1,0:T(8,128)} %bitcast.7), kind=kLoop, calls=%fused_computation | loop fusion | flops 65536 | bytes 524288 | tf_op jit(solution)/shard_map/concatenate | solution.py:351
  2.3 0.0 copy-start
  2.3 0.0 copy-start.1
  2.3 0.0 copy-start.2
  2.3 2.2 %pack.1 = (f32[104,8,256]{2,1,0:T(8,128)S(1)}, f32[96,8,256]{2,1,0:T(8,128)S(1)}, f32[200,8,256]{2,1,0:T(8,128)S(1)}) custom-call(s32[1]{0:T(128)S(6)} %copy.17.widths, f32[64,32,256]{2,1,0:T(8,128)} %refs_0_.5, f32[64,32,256]{2,1,0:T(8,128)} %refs_1_.5, f32[64,32,256]{2,1,0:T(8,128)} %refs_2_.5, f32[8,32,256]{2,1,0:T(8,128)S(1)} %pad_maximum_fusion.sides.refs_3_), custom_call_target="tpu_custom_call" | custom-call | tf_op jit(solution)/shard_map/pack/pallas_call | solution.py:357
  4.6 0.8 %collective-permute-start.2 = (f32[200,8,256]{2,1,0:T(8,128)S(1)}, f32[200,8,256]{2,1,0:T(8,128)S(1)}, u32[]{:S(2)}, u32[]{:S(2)}) collective-permute-start(f32[200,8,256]{2,1,0:T(8,128)S(1)} %get-tuple-element.13), channel_id=1, source_target_pairs={{0,1},{2,3},{4,5},{6,7},{8,9},{10,11},{12,13},{14,15},{1,0},{3,2},... | collective-permute-start | bytes 4915208 | tf_op jit(solution)/shard_map/ppermute | solution.py:372
  5.3 4.8 %collective-permute-start = (f32[104,8,256]{2,1,0:T(8,128)S(1)}, f32[104,8,256]{2,1,0:T(8,128)S(1)}, u32[]{:S(2)}, u32[]{:S(2)}) collective-permute-start(f32[104,8,256]{2,1,0:T(8,128)S(1)} %get-tuple-element.11), channel_id=1, source_target_pairs={{1,2},{3,4},{5,6},{7,8},{9,10},{11,12},{13,14},{2,1},{4,3},{6,5},{... | collective-permute-start | bytes 2555912 | tf_op jit(solution)/shard_map/ppermute | solution.py:371
  10.1 2.0 %collective-permute-start.1 = (f32[96,8,256]{2,1,0:T(8,128)S(1)}, f32[96,8,256]{2,1,0:T(8,128)S(1)}, u32[]{:S(2)}, u32[]{:S(2)}) collective-permute-start(f32[96,8,256]{2,1,0:T(8,128)S(1)} %get-tuple-element.12), channel_id=1, source_target_pairs={{1,2},{3,4},{5,6},{7,8},{9,10},{11,12},{13,14},{2,1},{4,3},{6,5},{... | collective-permute-start | bytes 2359304 | tf_op jit(solution)/shard_map/ppermute | solution.py:373
  12.1 0.0 collective-permute-done.2.refs_4_
  12.1 0.0 copy-done
  12.1 0.0 copy-done.1
  12.1 0.0 copy-done.2
  12.1 14.3 %inner.1 = (f32[64,32,256]{2,1,0:T(8,128)}, f32[4,32,256]{2,1,0:T(8,128)S(1)}, f32[4,32,256]{2,1,0:T(8,128)S(1)}) custom-call(s32[1]{0:T(128)S(6)} %copy.17.widths, f32[64,32,256]{2,1,0:T(8,128)S(1)} %copy-done, f32[64,32,256]{2,1,0:T(8,128)S(1)} %copy-done.1, f32[64,32,256]{2,1,0:T(8,128)S(1)} %copy-done.2, ...), custom_call_target="tpu_custom_call" | custom-call | flops 57671680 | bytes 10485760 | tf_op jit(solution)/shard_map/inner/pallas_call | solution.py:325
  26.4 0.0 collective-permute-done.refs_4_
  26.4 2.9 %corner.1 = (f32[4,32,256]{2,1,0:T(8,128)S(1)}, f32[4,32,256]{2,1,0:T(8,128)S(1)}) custom-call(s32[1]{0:T(128)S(6)} %copy.17.widths, f32[64,32,256]{2,1,0:T(8,128)S(1)} %copy-done, f32[64,32,256]{2,1,0:T(8,128)S(1)} %copy-done.1, f32[64,32,256]{2,1,0:T(8,128)S(1)} %copy-done.2, ...), custom_call_target="tpu_custom_call", output_to_operand_aliasing={{0}: (6, {}), {1}: (7, {})} | custom-call | flops 10813440 | bytes 1966080 | tf_op jit(solution)/shard_map/corner/pallas_call | solution.py:325
  29.4 3.2 %collective-permute-start.3 = (f32[4,32,256]{2,1,0:T(8,128)S(1)}, f32[4,32,256]{2,1,0:T(8,128)S(1)}, u32[]{:S(2)}, u32[]{:S(2)}) collective-permute-start(f32[4,32,256]{2,1,0:T(8,128)S(1)} %get-tuple-element.18), channel_id=1, source_target_pairs={{0,16},{16,32},{32,48},{48,64},{64,80},{80,96},{96,112},{112,128},... | collective-permute-start | bytes 393224 | tf_op jit(solution)/shard_map/ppermute | solution.py:381
  32.6 4.2 %collective-permute-start.4 = (f32[4,32,256]{2,1,0:T(8,128)S(1)}, f32[4,32,256]{2,1,0:T(8,128)S(1)}, u32[]{:S(2)}, u32[]{:S(2)}) collective-permute-start(f32[4,32,256]{2,1,0:T(8,128)S(1)} %get-tuple-element.17.refs_7_), channel_id=1, source_target_pairs={{16,0},{32,16},{48,32},{64,48},{80,64},{96,80},{112,96},{128,112},... | collective-permute-start | bytes 393224 | tf_op jit(solution)/shard_map/ppermute | solution.py:382
  36.8 0.0 collective-permute-done.1.refs_5_
  36.8 8.9 %outer.1 = f32[64,32,256]{2,1,0:T(8,128)} custom-call(s32[1]{0:T(128)S(6)} %copy.17.widths, f32[64,32,256]{2,1,0:T(8,128)S(1)} %copy-done, f32[64,32,256]{2,1,0:T(8,128)S(1)} %copy-done.1, f32[64,32,256]{2,1,0:T(8,128)S(1)} %copy-done.2, f32[8,32,256]{2,1,0:T(8,128)S(1)} %pad_maximum_fusion.sides.refs_3_, ...), custom_call_target="tpu_custom_call", output_to_operand_aliasing={{}: (7, {})} | custom-call | flops 34603008 | bytes 6291456 | tf_op jit(solution)/shard_map/outer/pallas_call | solution.py:325
  45.7 0.0 collective-permute-done.3
  45.7 0.0 collective-permute-done.4
  45.7 0.7 %copy.18 = f32[1,4,32,256]{3,2,1,0:T(8,128)} copy(f32[1,4,32,256]{3,2,1,0:T(8,128)S(1)} %bitcast.4) | data formatting | bytes 262144
  46.4 0.7 %copy.19 = f32[1,4,32,256]{3,2,1,0:T(8,128)} copy(f32[1,4,32,256]{3,2,1,0:T(8,128)S(1)} %bitcast.5) | data formatting | bytes 262144
Async XLA Ops:
  2.3 9.8 %copy-start = (f32[64,32,256]{2,1,0:T(8,128)S(1)}, f32[64,32,256]{2,1,0:T(8,128)}, u32[]{:S(2)}) copy-start(f32[64,32,256]{2,1,0:T(8,128)} %refs_0_.5) | copy-start | bytes 6291460
  2.3 9.8 %copy-start.1 = (f32[64,32,256]{2,1,0:T(8,128)S(1)}, f32[64,32,256]{2,1,0:T(8,128)}, u32[]{:S(2)}) copy-start(f32[64,32,256]{2,1,0:T(8,128)} %refs_1_.5) | copy-start | bytes 6291460
  2.3 9.8 %copy-start.2 = (f32[64,32,256]{2,1,0:T(8,128)S(1)}, f32[64,32,256]{2,1,0:T(8,128)}, u32[]{:S(2)}) copy-start(f32[64,32,256]{2,1,0:T(8,128)} %refs_2_.5) | copy-start | bytes 6291460
  4.6 7.5 %collective-permute-start.2 = (f32[200,8,256]{2,1,0:T(8,128)S(1)}, f32[200,8,256]{2,1,0:T(8,128)S(1)}, u32[]{:S(2)}, u32[]{:S(2)}) collective-permute-start(f32[200,8,256]{2,1,0:T(8,128)S(1)} %get-tuple-element.13), channel_id=1, source_target_pairs={{0,1},{2,3},{4,5},{6,7},{8,9},{10,11},{12,13},{14,15},{1,0},{3,2},... | collective-permute-start | bytes 4915208 | tf_op jit(solution)/shard_map/ppermute | solution.py:372
  5.3 21.1 %collective-permute-start = (f32[104,8,256]{2,1,0:T(8,128)S(1)}, f32[104,8,256]{2,1,0:T(8,128)S(1)}, u32[]{:S(2)}, u32[]{:S(2)}) collective-permute-start(f32[104,8,256]{2,1,0:T(8,128)S(1)} %get-tuple-element.11), channel_id=1, source_target_pairs={{1,2},{3,4},{5,6},{7,8},{9,10},{11,12},{13,14},{2,1},{4,3},{6,5},{... | collective-permute-start | bytes 2555912 | tf_op jit(solution)/shard_map/ppermute | solution.py:371
  10.1 26.7 %collective-permute-start.1 = (f32[96,8,256]{2,1,0:T(8,128)S(1)}, f32[96,8,256]{2,1,0:T(8,128)S(1)}, u32[]{:S(2)}, u32[]{:S(2)}) collective-permute-start(f32[96,8,256]{2,1,0:T(8,128)S(1)} %get-tuple-element.12), channel_id=1, source_target_pairs={{1,2},{3,4},{5,6},{7,8},{9,10},{11,12},{13,14},{2,1},{4,3},{6,5},{... | collective-permute-start | bytes 2359304 | tf_op jit(solution)/shard_map/ppermute | solution.py:373
  29.4 16.4 %collective-permute-start.3 = (f32[4,32,256]{2,1,0:T(8,128)S(1)}, f32[4,32,256]{2,1,0:T(8,128)S(1)}, u32[]{:S(2)}, u32[]{:S(2)}) collective-permute-start(f32[4,32,256]{2,1,0:T(8,128)S(1)} %get-tuple-element.18), channel_id=1, source_target_pairs={{0,16},{16,32},{32,48},{48,64},{64,80},{80,96},{96,112},{112,128},... | collective-permute-start | bytes 393224 | tf_op jit(solution)/shard_map/ppermute | solution.py:381
  32.6 13.1 %collective-permute-start.4 = (f32[4,32,256]{2,1,0:T(8,128)S(1)}, f32[4,32,256]{2,1,0:T(8,128)S(1)}, u32[]{:S(2)}, u32[]{:S(2)}) collective-permute-start(f32[4,32,256]{2,1,0:T(8,128)S(1)} %get-tuple-element.17.refs_7_), channel_id=1, source_target_pairs={{16,0},{32,16},{48,32},{64,48},{80,64},{96,80},{112,96},{128,112},... | collective-permute-start | bytes 393224 | tf_op jit(solution)/shard_map/ppermute | solution.py:382

commit v7 on v6

--- a/solution.py
+++ b/solution.py
@@ -372,7 +372,7 @@
     on_chip = lax.ppermute(on_chip, "dev", cores)
     middle = lax.ppermute(middle, "dev", chips)
 
-    field, trace_high, trace_low = run_window("inner", 5, 4, 32, WINDOW_BYTES, args, (on_chip,))
+    field, trace_high, trace_low = run_window("inner", 5, 3, 32, WINDOW_BYTES, args, (on_chip,))
     trace_high, trace_low = run_window("corner", 3, 2, 20, WINDOW_BYTES, args, (edge,), (trace_high, trace_low))
 
     subs = lax.axis_size("sub")

time: 47.3 us -> 46.4 us (0.981)
  Pallas kernels: 28.4 us -> 27.4 us
    pallas_call x3, Pallas kernels: 26.1 us -> 25.2 us  [run_window(): pl.pallas_call(functools.partial(window_kernel, kind, tiles, rotated, gro...]
  transfers between devices with their start and end apart: 5 -> 5, of which waited for: 0 -> 0; matrix products, arithmetic and copies ran while one was open for 0% -> 0% of each run, Pallas kernels for 56% -> 55%
where the time goes in v7:
time: 46.4 us; the launch traced here: 46.1 us
  Pallas kernels  27.4 us (59%)
  starting transfers between devices  14.9 us (32%)
  between operations  1.43 us (3%)
  local copies, waits for them, and re-layouts  1.33 us (3%)
  other arithmetic  0.99 us (2%)
    pallas_call x3, Pallas kernels, run_window(): pl.pallas_call(functools.partial(window_kernel, kind, tiles, rotated, gro...  25.2 us
    ppermute x1, starting transfers between devices, on_device(): edge = lax.ppermute(edge, 'dev', chips)  4.79 us
    ppermute x1, starting transfers between devices, on_device(): new_right = lax.ppermute(trace_low, 'sub', down)  4.18 us
    ppermute x1, starting transfers between devices, on_device(): new_left = lax.ppermute(trace_high, 'sub', up)  3.21 us
    pallas_call x1, Pallas kernels, on_device(): pl.pallas_call(pack_kernel, out_shape=tuple(rims), in_specs=[IN_SMEM] + [...  2.24 us
    ppermute x1, starting transfers between devices, on_device(): middle = lax.ppermute(middle, 'dev', chips)  1.97 us
    unnamed x8, local copies, waits for them, and re-layouts  1.33 us
    concatenate x1, other arithmetic, on_device(): sides = jnp.concatenate([left_data[0], right_data[0]])  0.99 us
  transfers between devices with their start and end apart: 5, of which 0 were waited for; matrix products, arithmetic and copies ran while one was open for 0% of the time, Pallas kernels for 55%

profile of v7, /device:TPU:101, one launch (start us, length us, event | category | flops | bytes accessed | tf_op | source)
XLA Modules:
  0.0 46.1 jit_solution(10527908935509906163)
XLA Ops:
  1.3 1.0 %pad_maximum_fusion.sides.refs_3_ = f32[8,32,256]{2,1,0:T(8,128)S(1)} fusion(f32[4,32,256]{2,1,0:T(8,128)} %bitcast.6, f32[4,32,256]{2,1,0:T(8,128)} %bitcast.7), kind=kLoop, calls=%fused_computation | loop fusion | flops 65536 | bytes 524288 | tf_op jit(solution)/shard_map/concatenate | solution.py:351
  2.3 0.0 copy-start
  2.3 0.0 copy-start.1
  2.3 0.0 copy-start.2
  2.3 2.2 %pack.1 = (f32[104,8,256]{2,1,0:T(8,128)S(1)}, f32[96,8,256]{2,1,0:T(8,128)S(1)}, f32[200,8,256]{2,1,0:T(8,128)S(1)}) custom-call(s32[1]{0:T(128)S(6)} %copy.17.widths, f32[64,32,256]{2,1,0:T(8,128)} %refs_0_.5, f32[64,32,256]{2,1,0:T(8,128)} %refs_1_.5, f32[64,32,256]{2,1,0:T(8,128)} %refs_2_.5, f32[8,32,256]{2,1,0:T(8,128)S(1)} %pad_maximum_fusion.sides.refs_3_), custom_call_target="tpu_custom_call" | custom-call | tf_op jit(solution)/shard_map/pack/pallas_call | solution.py:357
  4.6 0.8 %collective-permute-start.2 = (f32[200,8,256]{2,1,0:T(8,128)S(1)}, f32[200,8,256]{2,1,0:T(8,128)S(1)}, u32[]{:S(2)}, u32[]{:S(2)}) collective-permute-start(f32[200,8,256]{2,1,0:T(8,128)S(1)} %get-tuple-element.13), channel_id=1, source_target_pairs={{0,1},{2,3},{4,5},{6,7},{8,9},{10,11},{12,13},{14,15},{1,0},{3,2},... | collective-permute-start | bytes 4915208 | tf_op jit(solution)/shard_map/ppermute | solution.py:372
  5.3 4.8 %collective-permute-start = (f32[104,8,256]{2,1,0:T(8,128)S(1)}, f32[104,8,256]{2,1,0:T(8,128)S(1)}, u32[]{:S(2)}, u32[]{:S(2)}) collective-permute-start(f32[104,8,256]{2,1,0:T(8,128)S(1)} %get-tuple-element.11), channel_id=1, source_target_pairs={{1,2},{3,4},{5,6},{7,8},{9,10},{11,12},{13,14},{2,1},{4,3},{6,5},{... | collective-permute-start | bytes 2555912 | tf_op jit(solution)/shard_map/ppermute | solution.py:371
  10.1 2.0 %collective-permute-start.1 = (f32[96,8,256]{2,1,0:T(8,128)S(1)}, f32[96,8,256]{2,1,0:T(8,128)S(1)}, u32[]{:S(2)}, u32[]{:S(2)}) collective-permute-start(f32[96,8,256]{2,1,0:T(8,128)S(1)} %get-tuple-element.12), channel_id=1, source_target_pairs={{1,2},{3,4},{5,6},{7,8},{9,10},{11,12},{13,14},{2,1},{4,3},{6,5},{... | collective-permute-start | bytes 2359304 | tf_op jit(solution)/shard_map/ppermute | solution.py:373
  12.1 0.0 collective-permute-done.2.refs_4_
  12.1 0.0 copy-done
  12.1 0.0 copy-done.1
  12.1 0.0 copy-done.2
  12.1 13.3 %inner.1 = (f32[64,32,256]{2,1,0:T(8,128)}, f32[4,32,256]{2,1,0:T(8,128)S(1)}, f32[4,32,256]{2,1,0:T(8,128)S(1)}) custom-call(s32[1]{0:T(128)S(6)} %copy.17.widths, f32[64,32,256]{2,1,0:T(8,128)S(1)} %copy-done, f32[64,32,256]{2,1,0:T(8,128)S(1)} %copy-done.1, f32[64,32,256]{2,1,0:T(8,128)S(1)} %copy-done.2, ...), custom_call_target="tpu_custom_call" | custom-call | flops 57671680 | bytes 10485760 | tf_op jit(solution)/shard_map/inner/pallas_call | solution.py:325
  25.5 0.0 collective-permute-done.refs_4_
  25.5 2.9 %corner.1 = (f32[4,32,256]{2,1,0:T(8,128)S(1)}, f32[4,32,256]{2,1,0:T(8,128)S(1)}) custom-call(s32[1]{0:T(128)S(6)} %copy.17.widths, f32[64,32,256]{2,1,0:T(8,128)S(1)} %copy-done, f32[64,32,256]{2,1,0:T(8,128)S(1)} %copy-done.1, f32[64,32,256]{2,1,0:T(8,128)S(1)} %copy-done.2, ...), custom_call_target="tpu_custom_call", output_to_operand_aliasing={{0}: (6, {}), {1}: (7, {})} | custom-call | flops 10813440 | bytes 1966080 | tf_op jit(solution)/shard_map/corner/pallas_call | solution.py:325
  28.4 3.2 %collective-permute-start.3 = (f32[4,32,256]{2,1,0:T(8,128)S(1)}, f32[4,32,256]{2,1,0:T(8,128)S(1)}, u32[]{:S(2)}, u32[]{:S(2)}) collective-permute-start(f32[4,32,256]{2,1,0:T(8,128)S(1)} %get-tuple-element.18), channel_id=1, source_target_pairs={{0,16},{16,32},{32,48},{48,64},{64,80},{80,96},{96,112},{112,128},... | collective-permute-start | bytes 393224 | tf_op jit(solution)/shard_map/ppermute | solution.py:381
  31.6 4.2 %collective-permute-start.4 = (f32[4,32,256]{2,1,0:T(8,128)S(1)}, f32[4,32,256]{2,1,0:T(8,128)S(1)}, u32[]{:S(2)}, u32[]{:S(2)}) collective-permute-start(f32[4,32,256]{2,1,0:T(8,128)S(1)} %get-tuple-element.17.refs_7_), channel_id=1, source_target_pairs={{16,0},{32,16},{48,32},{64,48},{80,64},{96,80},{112,96},{128,112},... | collective-permute-start | bytes 393224 | tf_op jit(solution)/shard_map/ppermute | solution.py:382
  35.8 0.0 collective-permute-done.1.refs_5_
  35.8 8.9 %outer.1 = f32[64,32,256]{2,1,0:T(8,128)} custom-call(s32[1]{0:T(128)S(6)} %copy.17.widths, f32[64,32,256]{2,1,0:T(8,128)S(1)} %copy-done, f32[64,32,256]{2,1,0:T(8,128)S(1)} %copy-done.1, f32[64,32,256]{2,1,0:T(8,128)S(1)} %copy-done.2, f32[8,32,256]{2,1,0:T(8,128)S(1)} %pad_maximum_fusion.sides.refs_3_, ...), custom_call_target="tpu_custom_call", output_to_operand_aliasing={{}: (7, {})} | custom-call | flops 34603008 | bytes 6291456 | tf_op jit(solution)/shard_map/outer/pallas_call | solution.py:325
  44.8 0.0 collective-permute-done.3
  44.8 0.0 collective-permute-done.4
  44.8 0.7 %copy.18 = f32[1,4,32,256]{3,2,1,0:T(8,128)} copy(f32[1,4,32,256]{3,2,1,0:T(8,128)S(1)} %bitcast.4) | data formatting | bytes 262144
  45.4 0.7 %copy.19 = f32[1,4,32,256]{3,2,1,0:T(8,128)} copy(f32[1,4,32,256]{3,2,1,0:T(8,128)S(1)} %bitcast.5) | data formatting | bytes 262144
Async XLA Ops:
  2.3 9.8 %copy-start = (f32[64,32,256]{2,1,0:T(8,128)S(1)}, f32[64,32,256]{2,1,0:T(8,128)}, u32[]{:S(2)}) copy-start(f32[64,32,256]{2,1,0:T(8,128)} %refs_0_.5) | copy-start | bytes 6291460
  2.3 9.8 %copy-start.1 = (f32[64,32,256]{2,1,0:T(8,128)S(1)}, f32[64,32,256]{2,1,0:T(8,128)}, u32[]{:S(2)}) copy-start(f32[64,32,256]{2,1,0:T(8,128)} %refs_1_.5) | copy-start | bytes 6291460
  2.3 9.8 %copy-start.2 = (f32[64,32,256]{2,1,0:T(8,128)S(1)}, f32[64,32,256]{2,1,0:T(8,128)}, u32[]{:S(2)}) copy-start(f32[64,32,256]{2,1,0:T(8,128)} %refs_2_.5) | copy-start | bytes 6291460
  4.6 7.5 %collective-permute-start.2 = (f32[200,8,256]{2,1,0:T(8,128)S(1)}, f32[200,8,256]{2,1,0:T(8,128)S(1)}, u32[]{:S(2)}, u32[]{:S(2)}) collective-permute-start(f32[200,8,256]{2,1,0:T(8,128)S(1)} %get-tuple-element.13), channel_id=1, source_target_pairs={{0,1},{2,3},{4,5},{6,7},{8,9},{10,11},{12,13},{14,15},{1,0},{3,2},... | collective-permute-start | bytes 4915208 | tf_op jit(solution)/shard_map/ppermute | solution.py:372
  5.3 20.2 %collective-permute-start = (f32[104,8,256]{2,1,0:T(8,128)S(1)}, f32[104,8,256]{2,1,0:T(8,128)S(1)}, u32[]{:S(2)}, u32[]{:S(2)}) collective-permute-start(f32[104,8,256]{2,1,0:T(8,128)S(1)} %get-tuple-element.11), channel_id=1, source_target_pairs={{1,2},{3,4},{5,6},{7,8},{9,10},{11,12},{13,14},{2,1},{4,3},{6,5},{... | collective-permute-start | bytes 2555912 | tf_op jit(solution)/shard_map/ppermute | solution.py:371
  10.1 25.7 %collective-permute-start.1 = (f32[96,8,256]{2,1,0:T(8,128)S(1)}, f32[96,8,256]{2,1,0:T(8,128)S(1)}, u32[]{:S(2)}, u32[]{:S(2)}) collective-permute-start(f32[96,8,256]{2,1,0:T(8,128)S(1)} %get-tuple-element.12), channel_id=1, source_target_pairs={{1,2},{3,4},{5,6},{7,8},{9,10},{11,12},{13,14},{2,1},{4,3},{6,5},{... | collective-permute-start | bytes 2359304 | tf_op jit(solution)/shard_map/ppermute | solution.py:373
  28.4 16.3 %collective-permute-start.3 = (f32[4,32,256]{2,1,0:T(8,128)S(1)}, f32[4,32,256]{2,1,0:T(8,128)S(1)}, u32[]{:S(2)}, u32[]{:S(2)}) collective-permute-start(f32[4,32,256]{2,1,0:T(8,128)S(1)} %get-tuple-element.18), channel_id=1, source_target_pairs={{0,16},{16,32},{32,48},{48,64},{64,80},{80,96},{96,112},{112,128},... | collective-permute-start | bytes 393224 | tf_op jit(solution)/shard_map/ppermute | solution.py:381
  31.6 13.1 %collective-permute-start.4 = (f32[4,32,256]{2,1,0:T(8,128)S(1)}, f32[4,32,256]{2,1,0:T(8,128)S(1)}, u32[]{:S(2)}, u32[]{:S(2)}) collective-permute-start(f32[4,32,256]{2,1,0:T(8,128)S(1)} %get-tuple-element.17.refs_7_), channel_id=1, source_target_pairs={{16,0},{32,16},{48,32},{64,48},{80,64},{96,80},{112,96},{128,112},... | collective-permute-start | bytes 393224 | tf_op jit(solution)/shard_map/ppermute | solution.py:382
